TPU v7x, 256 devices: a whole 4x4x8 slice. The times are simulated.
256 devices in a mesh: role: 2 (over core), seq: 32 (over z, y), tp: 4 (over x).
Axes of the slice: x: 4, y: 4, z: 8, core: 2. Of those that a mesh axis runs over, the one named last changes fastest.
Arguments:
- span_hidden: bfloat16 [2, 8192, 5120], P('role', 'seq'), may hold values from -6 to 6
- attn_gain: float32 [5120], replicated, may hold values from 0.25 to 1.75
- kv_weight: bfloat16 [5120, 2, 1024], P(None, None, 'tp'), may hold values from -0.078125 to 0.078125
- q_gain: float32 [128], replicated, may hold values from 0.5 to 16
- key_norm_gain: float32 [128], replicated, may hold values from 0.5 to 16
- q_weight: bfloat16 [5120, 8192], P('seq', 'tp'), may hold values from -0.078125 to 0.078125
- o_weight: bfloat16 [8192, 5120], P('tp', 'seq'), may hold values from -0.0625 to 0.0625
- decode_hidden: bfloat16 [4, 128, 5120], P(None, 'seq'), may hold values from -6 to 6
- cache: bfloat16 [128, 128, 2, 1024], P('seq', None, None, 'tp'), may hold values from -6 to 6
- cache_len: int32 [128], P('seq'), may hold values from 1 to 128
- block_owner: int32 [32, 32], replicated, may hold values from 0 to 31, as said below
- block_slot: int32 [32, 32], replicated, may hold values from 0 to 31, as said below
Outputs:
- kv_sections: bfloat16 [2, 8192, 2, 1024], P('role', 'seq', None, 'tp')
- decode_sections: bfloat16 [2, 4, 128, 5120], P('role', None, 'seq')
Inputs may be any that keep to these rules, and one draw needn't show every extreme that they name: `block_owner`: entry (s, j) names the owner of block j of shard s; every owner receives exactly 32 blocks, no shard sends more than 2 to one owner, and some shard sends exactly 2 to one owner. `block_slot`: the blocks that one owner receives have the slots 0 to 31, each once.
All inputs are finite; a program needn't handle non-finite values.
Results may differ from a plain program's by a relative error of at most 0.014.
Values may be sent and summed in bfloat16 or wider, within the bound.
No kernel may reach another device: no remote copies, remote signals or barrier semaphores. Data moves between devices by JAX's collectives and lax.ppermute only.
A program may use at most 64 MiB of HBM per device.

v0:
```python
import math

import jax
import jax.numpy as jnp
from jax import lax
from jax.sharding import PartitionSpec as P

QUERY_HEADS = 64
KEY_VALUE_HEADS = 8
HEAD_SIZE = 128


EPSILON = 1e-06
THETA_BASE = 1000000.0


def shifted(block, axis, distance):
    devices = range(lax.axis_size(axis))
    route = [(i - distance, i) for i in devices if i - distance in devices]
    return lax.ppermute(block, axis, route)


def row_scaling(values, weights):
    return values * lax.rsqrt(jnp.mean(values * values, axis=-1, keepdims=True) + EPSILON) * weights


def apply_rotary(values, token_position):
    half_dim = values.shape[-1] // 2
    frequency = jnp.exp(
        jnp.arange(half_dim, dtype=jnp.float32) * (-2.0 * math.log(THETA_BASE) / values.shape[-1])
    )
    angles = token_position.astype(jnp.float32)[..., None, None] * frequency
    cosine = jnp.cos(angles)
    sine = jnp.sin(angles)
    first_half = values[..., :half_dim]
    second_half = values[..., half_dim:]
    return jnp.concatenate(
        [first_half * cosine - second_half * sine, second_half * cosine + first_half * sine],
        axis=-1,
    )


def shards(
    span_hidden,
    attn_gain,
    kv_weight,
    q_gain,
    key_norm_gain,
    q_weight,
    o_weight,
    decode_hidden,
    cache,
    cache_len,
    block_owner,
    block_slot,
):
    seq_count = lax.axis_size("seq")
    seq_index = lax.axis_index("seq")
    role_index = lax.axis_index("role")
    prefill_side = role_index == 0
    span_rows = span_hidden.shape[1]
    local_width = kv_weight.shape[2]
    local_heads = local_width // HEAD_SIZE

    def project_span(hidden_rows):
        normed = row_scaling(hidden_rows.astype(jnp.float32), attn_gain).astype(jnp.bfloat16)
        newest_token = jnp.einsum(
            "td,dcw->tcw", normed, kv_weight, preferred_element_type=jnp.float32
        )
        token_position = seq_index * span_rows + jnp.arange(span_rows, dtype=jnp.int32)
        keys_now = apply_rotary(
            row_scaling(
                newest_token[:, 0].reshape(span_rows, local_heads, HEAD_SIZE), key_norm_gain
            ),
            token_position,
        )
        return jnp.stack(
            [keys_now.reshape(span_rows, local_width), newest_token[:, 1]], axis=1
        ).astype(jnp.bfloat16)

    def skip_span(hidden_rows):
        return jnp.zeros((span_rows, 2, local_width), jnp.bfloat16)

    span_kv = lax.cond(prefill_side, project_span, skip_span, span_hidden[0])
    block_count = block_owner.shape[1]
    block_width = span_kv.size // block_count
    capacity = 2 * ((block_count + seq_count - 1) // seq_count)
    buffer_rows = seq_count * capacity
    block_number = jnp.arange(block_count, dtype=jnp.int32)
    same_owner = block_owner[:, :, None] == block_owner[:, None, :]
    earlier = block_number[None, None, :] < block_number[None, :, None]
    rank_table = jnp.sum(jnp.logical_and(same_owner, earlier), axis=2)
    own_owner = lax.dynamic_index_in_dim(block_owner, seq_index, 0, keepdims=False)
    own_rank = lax.dynamic_index_in_dim(rank_table, seq_index, 0, keepdims=False)
    destination = own_owner * capacity + own_rank
    buffer_index = jnp.arange(buffer_rows, dtype=jnp.int32)
    send_table = (destination[None, :] == buffer_index[:, None]).astype(jnp.bfloat16)
    payload = jnp.dot(
        send_table, span_kv.reshape(block_count, block_width), preferred_element_type=jnp.float32
    ).astype(jnp.bfloat16)
    crossed = shifted(payload, "role", 1)
    arrived = lax.all_to_all(crossed, "seq", split_axis=0, concat_axis=0, tiled=True)
    mine = block_owner == seq_index
    target = jnp.where(mine, block_slot, -1)
    source_column = jnp.arange(seq_count, dtype=jnp.int32)[:, None] * capacity + rank_table
    pick_slot = (target[:, :, None] == block_number[None, None, :]).astype(jnp.float32)
    pick_column = (source_column[:, :, None] == buffer_index[None, None, :]).astype(jnp.float32)
    placing = jnp.einsum("sjk,sjc->kc", pick_slot, pick_column).astype(jnp.bfloat16)
    pool = (
        jnp.dot(placing, arrived, preferred_element_type=jnp.float32)
        .astype(jnp.bfloat16)
        .reshape(span_rows, 2, local_width)
    )
    kv_sections = jnp.where(prefill_side, span_kv, pool)[None]
    rows_here = decode_hidden.shape[1]
    step_total = decode_hidden.shape[0]
    context = cache.shape[1]
    query_group_width = QUERY_HEADS // KEY_VALUE_HEADS
    local_query = q_weight.shape[1]
    scale_factor = HEAD_SIZE ** (-0.5)
    column_weight = lax.all_to_all(q_weight, "seq", split_axis=1, concat_axis=0, tiled=True)
    visible = jnp.arange(context, dtype=jnp.int32)[None, :] < cache_len[:, None]
    cached_key_rows = cache[:, :, 0].reshape(rows_here, context, local_heads, HEAD_SIZE)
    cached_value_rows = cache[:, :, 1].reshape(rows_here, context, local_heads, HEAD_SIZE)

    def attend(query_rows, new_keys, new_values):
        grouped_queries = query_rows.reshape(rows_here, local_heads, query_group_width, HEAD_SIZE)
        old_scores = (
            jnp.einsum(
                "rgqd,rcgd->rgqc",
                grouped_queries,
                cached_key_rows,
                preferred_element_type=jnp.float32,
            )
            * scale_factor
        )
        old_scores = jnp.where(visible[:, None, None, :], old_scores, -jnp.inf)
        new_scores = (
            jnp.einsum(
                "rgqd,rngd->rgqn", grouped_queries, new_keys, preferred_element_type=jnp.float32
            )
            * scale_factor
        )
        top = jnp.maximum(
            jnp.max(old_scores, axis=-1, keepdims=True), jnp.max(new_scores, axis=-1, keepdims=True)
        )
        old_exp = jnp.exp(old_scores - top)
        new_exp = jnp.exp(new_scores - top)
        total = jnp.sum(old_exp, axis=-1, keepdims=True) + jnp.sum(new_exp, axis=-1, keepdims=True)
        old_weights = (old_exp / total).astype(jnp.bfloat16)
        new_weights = (new_exp / total).astype(jnp.bfloat16)
        mixed = jnp.einsum(
            "rgqc,rcgd->rgqd", old_weights, cached_value_rows, preferred_element_type=jnp.float32
        )
        mixed = mixed + jnp.einsum(
            "rgqn,rngd->rgqd", new_weights, new_values, preferred_element_type=jnp.float32
        )
        return mixed.reshape(rows_here, local_query).astype(jnp.bfloat16)

    def skip_attention(query_rows, new_keys, new_values):
        return jnp.zeros((rows_here, local_query), jnp.bfloat16)

    gathered_keys = []
    gathered_values = []
    results = []
    for step_index in range(step_total):
        hidden_rows = decode_hidden[step_index]
        normed = row_scaling(hidden_rows.astype(jnp.float32), attn_gain).astype(jnp.bfloat16)
        token_position = cache_len + step_index
        partial_query = jnp.dot(
            lax.all_gather(normed, "seq", axis=0, tiled=True),
            column_weight,
            preferred_element_type=jnp.float32,
        )
        query_raw = lax.all_to_all(partial_query, "seq", split_axis=0, concat_axis=1, tiled=True)
        query_rows = apply_rotary(
            row_scaling(query_raw.reshape(rows_here, local_query // HEAD_SIZE, HEAD_SIZE), q_gain),
            token_position,
        ).astype(jnp.bfloat16)
        newest_token = jnp.einsum(
            "rd,dcw->rcw", normed, kv_weight, preferred_element_type=jnp.float32
        )
        gathered_keys.append(
            apply_rotary(
                row_scaling(
                    newest_token[:, 0].reshape(rows_here, local_heads, HEAD_SIZE), key_norm_gain
                ),
                token_position,
            ).astype(jnp.bfloat16)
        )
        gathered_values.append(
            newest_token[:, 1].reshape(rows_here, local_heads, HEAD_SIZE).astype(jnp.bfloat16)
        )
        attended = lax.cond(
            prefill_side,
            skip_attention,
            attend,
            query_rows,
            jnp.stack(gathered_keys, axis=1),
            jnp.stack(gathered_values, axis=1),
        )
        partial_out = jnp.dot(
            lax.all_gather(attended, "seq", axis=0, tiled=True),
            o_weight,
            preferred_element_type=jnp.float32,
        )
        row_out = lax.all_to_all(
            partial_out.astype(jnp.bfloat16), "seq", split_axis=0, concat_axis=1, tiled=True
        ).astype(partial_out.dtype)
        delta = lax.psum(row_out.astype(jnp.bfloat16), "tp").astype(jnp.float32)
        results.append((hidden_rows.astype(jnp.float32) + delta).astype(jnp.bfloat16))
    decoded = jnp.stack(results)
    decode_sections = jnp.where(prefill_side, jnp.zeros_like(decoded), decoded)[None]
    return (kv_sections, decode_sections)


def solution(mesh):
    placed = (
        P("role", "seq", None),
        P(),
        P(None, None, "tp"),
        P(),
        P(),
        P("seq", "tp"),
        P("tp", "seq"),
        P(None, "seq", None),
        P("seq", None, None, "tp"),
        P("seq"),
        P(),
        P(),
    )
    return jax.shard_map(
        shards,
        mesh=mesh,
        in_specs=placed,
        out_specs=(P("role", "seq", None, "tp"), P("role", None, "seq", None)),
        check_vma=False,
    )
```

profile of v0, /device:TPU:1, one launch (start us, length us, event | category | flops | bytes accessed | tf_op | source)
XLA Modules:
  0.0 666.4 jit_solution(2812950112108696653)
XLA Ops:
  7.2 1.1 fusion.83
  8.4 1.7 fusion.123
  11.6 0.9 conditional.5
  11.6 0.8 broadcast.424.clone
  12.5 0.8 convert_reduce_fusion
  13.3 1.1 convolution_convert_fusion
  14.4 1.3 collective-permute-start
  15.7 1.3 copy.511
  17.0 12.0 %all-to-all-start.1 = ((bf16[160,32,64]{0,2,1:T(8,128)(2,1)}), bf16[160,32,64]{0,2,1:T(8,128)(2,1)S(1)}, u32[]{:S(2)}, u32[]{:S(2)}) async-start(bf16[160,32,64]{0,2,1:T(8,128)(2,1)} %bitcast.21), calls=%async_computation.1 | async-start | bytes 2097152 | tf_op jit(solution)/shard_map/all_to_all | solution.py:121
  29.7 3.5 fusion.67
  33.2 3.3 fusion.65
  36.5 0.8 fusion.63
  37.4 0.8 fusion.61
  41.9 1.5 fusion.131
  43.4 2.2 all_to_all.118
  45.6 2.1 all-to-all-done.1
  47.6 7.5 %all-to-all-start = ((bf16[32,2,4096]{2,1,0:T(2,128)(2,1)}), bf16[32,2,4096]{2,1,0:T(2,128)(2,1)}, u32[]{:S(2)}, u32[]{:S(2)}) async-start(bf16[32,2,4096]{2,1,0:T(2,128)(2,1)} %all_to_all.118), calls=%async_computation | async-start | bytes 1048576 | tf_op jit(solution)/shard_map/all_to_all | solution.py:102
  55.2 1.3 copy.514
  58.2 0.7 iota_compare_fusion.9
  59.0 0.8 compare_select_fusion
  60.3 2.5 reshape.871
  62.9 4.7 all-to-all-done
  67.6 1.2 all_to_all.120
  68.9 21.2 %all-gather.13.cloned.1.call-done = bf16[32,4,5120]{2,1,0:T(4,128)(2,1)} async-done(((bf16[1,4,5120]{2,1,0:T(4,128)(2,1)}), bf16[32,4,5120]{2,1,0:T(4,128)(2,1)}) %all-gather.13.cloned.1.call-update) | async-done | bytes 1310736 | tf_op jit(solution)/shard_map/all_gather | solution.py:171
  90.0 2.0 fusion.75
  92.1 0.7 reshape.883
  92.8 6.3 all-to-all-start.2
  99.2 67.1 %all-gather.15.cloned.1.call-done = bf16[32,4,5120]{2,1,0:T(4,128)(2,1)} async-done(((bf16[1,4,5120]{2,1,0:T(4,128)(2,1)}), bf16[32,4,5120]{2,1,0:T(4,128)(2,1)}) %all-gather.15.cloned.1.call-update) | async-done | bytes 1310736 | tf_op jit(solution)/shard_map/all_gather | solution.py:171
  166.3 2.0 fusion.73
  168.3 74.9 %all-gather.17.cloned.1.call-done = bf16[32,4,5120]{2,1,0:T(4,128)(2,1)} async-done(((bf16[1,4,5120]{2,1,0:T(4,128)(2,1)}), bf16[32,4,5120]{2,1,0:T(4,128)(2,1)}) %all-gather.17.cloned.1.call-update) | async-done | bytes 1310736 | tf_op jit(solution)/shard_map/all_gather | solution.py:171
  243.3 1.9 fusion.71
  245.1 74.9 %all-gather.19.cloned.1.call-done = bf16[32,4,5120]{2,1,0:T(4,128)(2,1)} async-done(((bf16[1,4,5120]{2,1,0:T(4,128)(2,1)}), bf16[32,4,5120]{2,1,0:T(4,128)(2,1)}) %all-gather.19.cloned.1.call-update) | async-done | bytes 1310736 | tf_op jit(solution)/shard_map/all_gather | solution.py:171
  320.1 1.9 fusion.69
  324.2 6.0 all-to-all-start.4
  331.6 7.3 %all-to-all-done.4 = f32[32,1,256]{2,1,0:T(1,128)S(1)} async-done(((f32[32,1,256]{2,1,0:T(1,128)}), f32[32,1,256]{2,1,0:T(1,128)S(1)}, u32[]{:S(2)}, u32[]{:S(2)}) %all-to-all-start.4) | async-done | bytes 32800 | tf_op jit(solution)/shard_map/all_to_all | solution.py:175
  338.9 3.8 all-to-all-start.6
  342.7 0.7 reduce.9
  343.6 7.7 %all-to-all-done.6 = f32[32,1,256]{2,1,0:T(1,128)S(1)} async-done(((f32[32,1,256]{2,1,0:T(1,128)}), f32[32,1,256]{2,1,0:T(1,128)S(1)}, u32[]{:S(2)}, u32[]{:S(2)}) %all-to-all-start.6) | async-done | bytes 32800 | tf_op jit(solution)/shard_map/all_to_all | solution.py:175
  351.3 3.8 all-to-all-start.8
  355.2 0.7 reduce.10
  356.1 7.7 %all-to-all-done.8 = f32[32,1,256]{2,1,0:T(1,128)S(1)} async-done(((f32[32,1,256]{2,1,0:T(1,128)}), f32[32,1,256]{2,1,0:T(1,128)S(1)}, u32[]{:S(2)}, u32[]{:S(2)}) %all-to-all-start.8) | async-done | bytes 32800 | tf_op jit(solution)/shard_map/all_to_all | solution.py:175
  363.8 0.7 reduce.11
  366.2 1.2 conditional.9
  367.3 35.6 %all-gather.7 = bf16[32,4,2048]{2,1,0:T(4,128)(2,1)S(1)} all-gather(bf16[1,4,2048]{2,1,0:T(4,128)(2,1)S(1)} %bitcast.274), channel_id=1, replica_groups=mesh['role'=2,'seq'=32,'tp'=4] {'seq'}, dimensions={0}, use_global_device_ids=true | all-gather | bytes 540672 | tf_op jit(solution)/shard_map/all_gather | solution.py:203
  404.2 4.4 all-to-all-start.9
  408.8 1.2 conditional.8
  410.0 38.5 %all-gather.5 = bf16[32,4,2048]{2,1,0:T(4,128)(2,1)S(1)} all-gather(bf16[1,4,2048]{2,1,0:T(4,128)(2,1)S(1)} %bitcast.276), channel_id=1, replica_groups=mesh['role'=2,'seq'=32,'tp'=4] {'seq'}, dimensions={0}, use_global_device_ids=true | all-gather | bytes 540672 | tf_op jit(solution)/shard_map/all_gather | solution.py:203
  449.9 1.4 conditional.7
  451.3 35.6 %all-gather.3 = bf16[32,4,2048]{2,1,0:T(4,128)(2,1)S(1)} all-gather(bf16[1,4,2048]{2,1,0:T(4,128)(2,1)S(1)} %bitcast.278), channel_id=1, replica_groups=mesh['role'=2,'seq'=32,'tp'=4] {'seq'}, dimensions={0}, use_global_device_ids=true | all-gather | bytes 540672 | tf_op jit(solution)/shard_map/all_gather | solution.py:203
  488.2 0.9 conditional.6
  489.2 7.8 %all-to-all-start.7 = ((bf16[32,4,160]{2,1,0:T(4,128)(2,1)}), bf16[32,4,160]{2,1,0:T(4,128)(2,1)S(1)}, u32[]{:S(2)}, u32[]{:S(2)}) async-start(bf16[32,4,160]{2,1,0:T(4,128)(2,1)} %all_to_all.139), calls=%async_computation.7 | async-start | bytes 131072 | tf_op jit(solution)/shard_map/all_to_all | solution.py:207
  496.9 38.1 %all-gather.1 = bf16[32,4,2048]{2,1,0:T(4,128)(2,1)S(1)} all-gather(bf16[1,4,2048]{2,1,0:T(4,128)(2,1)S(1)} %bitcast.280), channel_id=1, replica_groups=mesh['role'=2,'seq'=32,'tp'=4] {'seq'}, dimensions={0}, use_global_device_ids=true | all-gather | bytes 540672 | tf_op jit(solution)/shard_map/all_gather | solution.py:203
  535.2 6.4 all-to-all-start.5
  542.7 7.7 %all-to-all-done.5 = bf16[32,4,160]{2,1,0:T(4,128)(2,1)S(1)} async-done(((bf16[32,4,160]{2,1,0:T(4,128)(2,1)}), bf16[32,4,160]{2,1,0:T(4,128)(2,1)S(1)}, u32[]{:S(2)}, u32[]{:S(2)}) %all-to-all-start.5) | async-done | bytes 40992 | tf_op jit(solution)/shard_map/all_to_all | solution.py:207
  550.4 3.9 all-to-all-start.3
  555.1 0.8 all_to_all.148
  555.9 0.8 all_to_all.142
  556.7 0.8 all_to_all.136
  557.4 5.6 all-to-all-done.3
  563.1 0.8 all_to_all.130
  563.9 1.0 fusion.78
  564.8 93.3 %all-reduce.3.cloned.1.call-done = (bf16[4,5120]{1,0:T(4,128)(2,1)}, bf16[4,5120]{1,0:T(4,128)(2,1)}, bf16[4,5120]{1,0:T(4,128)(2,1)}, bf16[4,5120]{1,0:T(4,128)(2,1)}) async-done(((bf16[4,5120]{1,0:T(4,128)(2,1)}, bf16[4,5120]{1,0:T(4,128)(2,1)}, bf16[4,5120]{1,0:T(4,128)(2,1)}, bf16[4,5120]{1,0:T(4,128)(2,1)}), (bf16[4,5120]{1,0:T(4,128)(2,1)}, bf16[4,5120]{1,0:T(4,128)(2,1)}, bf16[4,5120]{1,0:T(4,128)(2,1)}, ...) | async-done | bytes 163856 | tf_op jit(solution)/shard_map/psum | solution.py:210
  658.1 0.9 fusion.102
  659.0 0.8 maximum_select_fusion
  (206 shorter events, 24.4 us)
Async XLA Ops:
  7.2 395.9 %copy-start = (bf16[2048,160]{0,1:T(8,128)(2,1)S(1)}, bf16[2048,160]{0,1:T(8,128)(2,1)}, u32[]{:S(2)}) copy-start(bf16[2048,160]{0,1:T(8,128)(2,1)} %param.28) | copy-start | bytes 1966084
  7.2 82.9 %all-gather.13.cloned.1.call-start = ((), (), s32[]{:S(2)}) async-start(), calls=%async_computation.10 | async-start | bytes 1351680 | tf_op jit(solution)/shard_map/all_gather | solution.py:171
  10.1 156.3 %all-gather.15.cloned.1.call-start = ((), (), s32[]{:S(2)}) async-start(), calls=%async_computation.11 | async-start | bytes 1351680 | tf_op jit(solution)/shard_map/all_gather | solution.py:171
  10.8 232.5 %all-gather.17.cloned.1.call-start = ((), (), s32[]{:S(2)}) async-start(), calls=%async_computation.12 | async-start | bytes 1351680 | tf_op jit(solution)/shard_map/all_gather | solution.py:171
  11.6 0.9 copy-start.6
  11.6 4.1 copy-start.3
  11.6 18.1 %copy-start.1 = (bf16[4,4,5120]{2,1,0:T(4,128)(2,1)S(1)}, bf16[4,4,5120]{2,1,0:T(4,128)(2,1)}, u32[]{:S(2)}) copy-start(bf16[4,4,5120]{2,1,0:T(4,128)(2,1)} %param.29) | copy-start | bytes 491524
  12.5 20.7 %copy-start.5 = (f32[5120]{0:T(1024)S(1)}, f32[5120]{0:T(1024)}, u32[]{:S(2)}) copy-start(f32[5120]{0:T(1024)} %param.23) | copy-start | bytes 61444
  14.4 29.0 %collective-permute-start = (bf16[64,4096]{1,0:T(8,128)(2,1)}, bf16[64,4096]{1,0:T(8,128)(2,1)}, u32[]{:S(2)}, u32[]{:S(2)}) collective-permute-start(bf16[64,4096]{1,0:T(8,128)(2,1)} %convolution_convert_fusion), channel_id=1, source_target_pairs={{0,128},{1,129},{2,130},{3,131},{4,132},{5,133},{6,134},{7,135},{8... | collective-permute-start | bytes 1572872 | tf_op jit(solution)/shard_map/ppermute | solution.py:20
  17.0 30.6 %all-to-all-start.1 = ((bf16[160,32,64]{0,2,1:T(8,128)(2,1)}), bf16[160,32,64]{0,2,1:T(8,128)(2,1)S(1)}, u32[]{:S(2)}, u32[]{:S(2)}) async-start(bf16[160,32,64]{0,2,1:T(8,128)(2,1)} %bitcast.21), calls=%async_computation.1 | async-start | bytes 2097152 | tf_op jit(solution)/shard_map/all_to_all | solution.py:121
  29.0 291.0 %all-gather.19.cloned.1.call-start = ((), (), s32[]{:S(2)}) async-start(), calls=%async_computation.13 | async-start | bytes 1351680 | tf_op jit(solution)/shard_map/all_gather | solution.py:171
  29.6 6.8 %slice-start = ((s8[5242880]{0:T(1024)(128)(4,1)}), s8[4194304]{0:T(1024)(128)(4,1)S(1)}, s32[]{:S(2)}) async-start(s8[5242880]{0:T(1024)(128)(4,1)} %bitcast.251), calls=%async_computation.15 | async-start | bytes 8388608
  29.7 6.8 %slice-start.1 = ((s8[5242880]{0:T(1024)(128)(4,1)}), s8[1048576]{0:T(1024)(128)(4,1)S(1)}, s32[]{:S(2)}) async-start(s8[5242880]{0:T(1024)(128)(4,1)} %bitcast.251), calls=%async_computation.16 | async-start | bytes 2097152
  36.5 1.7 copy-start.16
  36.5 2.2 copy-start.13
  36.5 5.4 copy-start.2
  47.6 20.0 %all-to-all-start = ((bf16[32,2,4096]{2,1,0:T(2,128)(2,1)}), bf16[32,2,4096]{2,1,0:T(2,128)(2,1)}, u32[]{:S(2)}, u32[]{:S(2)}) async-start(bf16[32,2,4096]{2,1,0:T(2,128)(2,1)} %all_to_all.118), calls=%async_computation | async-start | bytes 1048576 | tf_op jit(solution)/shard_map/all_to_all | solution.py:102
  62.9 180.4 %copy-start.4 = (bf16[5120,64,1]{0,1,2:T(8,128)(2,1)S(1)}, bf16[5120,64,1]{0,1,2:T(8,128)(2,1)}, u32[]{:S(2)}) copy-start(bf16[5120,64,1]{0,1,2:T(8,128)(2,1)} %reshape.871) | copy-start | bytes 1966084
  92.8 273.0 %copy-start.15 = (f32[128]{0:T(128)S(1)}, f32[128]{0:T(128)}, u32[]{:S(2)}) copy-start(f32[128]{0:T(128)} %param.25) | copy-start | bytes 1540
  92.8 231.3 %all-to-all-start.2 = ((f32[32,1,256]{2,1,0:T(1,128)}), f32[32,1,256]{2,1,0:T(1,128)S(1)}, u32[]{:S(2)}, u32[]{:S(2)}) async-start(f32[32,1,256]{2,1,0:T(1,128)} %reshape.883), calls=%async_computation.2 | async-start | bytes 65536 | tf_op jit(solution)/shard_map/all_to_all | solution.py:175
  99.2 267.0 %copy-start.7 = (bf16[4,4,2,128]{3,2,0,1:T(2,128)(2,1)S(1)}, bf16[4,4,2,128]{3,2,0,1:T(2,128)(2,1)}, u32[]{:S(2)}) copy-start(bf16[4,4,2,128]{3,2,0,1:T(2,128)(2,1)} %maximum_maximum_fusion) | copy-start | bytes 24580
  245.1 163.7 %copy-start.8 = (bf16[4,3,2,128]{3,1,2,0:T(4,128)(2,1)S(1)}, bf16[4,3,2,128]{3,1,2,0:T(4,128)(2,1)}, u32[]{:S(2)}) copy-start(bf16[4,3,2,128]{3,1,2,0:T(4,128)(2,1)} %pad_maximum_fusion.5) | copy-start | bytes 18436
  245.1 163.7 %copy-start.9 = (bf16[4,3,2,128]{3,2,0,1:T(2,128)(2,1)S(1)}, bf16[4,3,2,128]{3,2,0,1:T(2,128)(2,1)}, u32[]{:S(2)}) copy-start(bf16[4,3,2,128]{3,2,0,1:T(2,128)(2,1)} %maximum_maximum_fusion.1) | copy-start | bytes 18436
  324.2 14.7 %all-to-all-start.4 = ((f32[32,1,256]{2,1,0:T(1,128)}), f32[32,1,256]{2,1,0:T(1,128)S(1)}, u32[]{:S(2)}, u32[]{:S(2)}) async-start(f32[32,1,256]{2,1,0:T(1,128)} %reshape.881), calls=%async_computation.4 | async-start | bytes 65536 | tf_op jit(solution)/shard_map/all_to_all | solution.py:175
  338.9 12.5 %all-to-all-start.6 = ((f32[32,1,256]{2,1,0:T(1,128)}), f32[32,1,256]{2,1,0:T(1,128)S(1)}, u32[]{:S(2)}, u32[]{:S(2)}) async-start(f32[32,1,256]{2,1,0:T(1,128)} %reshape.879), calls=%async_computation.6 | async-start | bytes 65536 | tf_op jit(solution)/shard_map/all_to_all | solution.py:175
  351.3 12.4 %all-to-all-start.8 = ((f32[32,1,256]{2,1,0:T(1,128)}), f32[32,1,256]{2,1,0:T(1,128)S(1)}, u32[]{:S(2)}, u32[]{:S(2)}) async-start(f32[32,1,256]{2,1,0:T(1,128)} %reshape.877), calls=%async_computation.8 | async-start | bytes 65536 | tf_op jit(solution)/shard_map/all_to_all | solution.py:175
  356.0 93.9 %copy-start.10 = (bf16[4,2,2,128]{3,2,0,1:T(2,128)(2,1)S(1)}, bf16[4,2,2,128]{3,2,0,1:T(2,128)(2,1)}, u32[]{:S(2)}) copy-start(bf16[4,2,2,128]{3,2,0,1:T(2,128)(2,1)} %maximum_maximum_fusion.2) | copy-start | bytes 12292
  356.0 93.9 %copy-start.11 = (bf16[4,2,2,128]{3,1,2,0:T(2,128)(2,1)S(1)}, bf16[4,2,2,128]{3,1,2,0:T(2,128)(2,1)}, u32[]{:S(2)}) copy-start(bf16[4,2,2,128]{3,1,2,0:T(2,128)(2,1)} %pad_maximum_fusion.7) | copy-start | bytes 12292
  403.1 85.2 %copy-start.12 = (bf16[4,1,2,128]{3,2,0,1:T(2,128)(2,1)S(1)}, bf16[4,1,2,128]{3,2,0,1:T(2,128)(2,1)}, u32[]{:S(2)}) copy-start(bf16[4,1,2,128]{3,2,0,1:T(2,128)(2,1)} %pad_maximum_fusion.8) | copy-start | bytes 6148
  404.2 85.0 %all-to-all-start.9 = ((bf16[32,4,160]{2,1,0:T(4,128)(2,1)}), bf16[32,4,160]{2,1,0:T(4,128)(2,1)S(1)}, u32[]{:S(2)}, u32[]{:S(2)}) async-start(bf16[32,4,160]{2,1,0:T(4,128)(2,1)} %all_to_all.145), calls=%async_computation.9 | async-start | bytes 131072 | tf_op jit(solution)/shard_map/all_to_all | solution.py:207
  489.2 46.0 %all-to-all-start.7 = ((bf16[32,4,160]{2,1,0:T(4,128)(2,1)}), bf16[32,4,160]{2,1,0:T(4,128)(2,1)S(1)}, u32[]{:S(2)}, u32[]{:S(2)}) async-start(bf16[32,4,160]{2,1,0:T(4,128)(2,1)} %all_to_all.139), calls=%async_computation.7 | async-start | bytes 131072 | tf_op jit(solution)/shard_map/all_to_all | solution.py:207
  535.2 15.2 %all-to-all-start.5 = ((bf16[32,4,160]{2,1,0:T(4,128)(2,1)}), bf16[32,4,160]{2,1,0:T(4,128)(2,1)S(1)}, u32[]{:S(2)}, u32[]{:S(2)}) async-start(bf16[32,4,160]{2,1,0:T(4,128)(2,1)} %all_to_all.133), calls=%async_computation.5 | async-start | bytes 131072 | tf_op jit(solution)/shard_map/all_to_all | solution.py:207
  550.4 12.7 %all-to-all-start.3 = ((bf16[32,4,160]{2,1,0:T(4,128)(2,1)}), bf16[32,4,160]{2,1,0:T(4,128)(2,1)S(1)}, u32[]{:S(2)}, u32[]{:S(2)}) async-start(bf16[32,4,160]{2,1,0:T(4,128)(2,1)} %all_to_all.127), calls=%async_computation.3 | async-start | bytes 131072 | tf_op jit(solution)/shard_map/all_to_all | solution.py:207
  554.2 103.9 %all-reduce.3.cloned.1.call-start = ((), (), s32[]{:S(2)}) async-start(), calls=%async_computation.14 | async-start | bytes 327680 | tf_op jit(solution)/shard_map/psum | solution.py:210
Sparse Core Ops, SparseCore 0:
  11.2 78.8 all-gather.12
  92.6 73.6 all-gather.14
  168.9 74.3 all-gather.16
  245.7 74.3 all-gather.18
  564.0 94.0 all-reduce.2
where the time goes:
time: 669 us; the launch traced here: 666 us
  waiting for transfers between devices  376 us (56%)
  blocking collectives  148 us (22%)
  starting transfers between devices  63.4 us (9%)
  local copies, waits for them, and re-layouts  23.8 us (4%)
  matrix products  22.7 us (3%)
  other arithmetic  17.7 us (3%)
  between operations  14.6 us (2%)
    all_gather x4, waiting for transfers between devices, shards(): lax.all_gather(normed, 'seq', axis=0, tiled=True)  238 us
    all_gather x4, blocking collectives, shards(): lax.all_gather(attended, 'seq', axis=0, tiled=True)  148 us
    psum x1, waiting for transfers between devices, shards(): delta = lax.psum(row_out.astype(jnp.bfloat16), 'tp').astype(jnp.float32)  93.3 us
    all_to_all x4, waiting for transfers between devices, shards(): lax.all_to_all(partial_query, 'seq', split_axis=0, concat_axis=1, tiled=T...  22.6 us
    all_to_all x4, starting transfers between devices, shards(): lax.all_to_all(partial_out.astype(jnp.bfloat16), 'seq', split_axis=0, con...  22.4 us
    all_to_all x4, starting transfers between devices, shards(): lax.all_to_all(partial_query, 'seq', split_axis=0, concat_axis=1, tiled=T...  19.9 us
  transfers between devices with their start and end apart: 16, of which 12 were waited for; matrix products, arithmetic and copies ran while one was open for 7% of the time, Pallas kernels for 0%

commit v1 on v0

v1 whole, which is shorter than its diff:
```python
import math

import jax
import jax.numpy as jnp
from jax import lax
from jax.sharding import Mesh, PartitionSpec as P

QUERY_HEADS = 64
KEY_VALUE_HEADS = 8
HEAD_SIZE = 128
EPSILON = 1e-06
THETA_BASE = 1000000.0

Z, Y = 8, 4
SEQ = ("z", "y")
BLOCK_TOKENS = 8
CAPACITY = 2
F32, BF16 = jnp.float32, jnp.bfloat16


def row_scaling(values, weights):
    return values * lax.rsqrt(jnp.mean(values * values, axis=-1, keepdims=True) + EPSILON) * weights


def rotary_tables(token_position):
    half_dim = HEAD_SIZE // 2
    frequency = jnp.exp(
        jnp.arange(half_dim, dtype=F32) * (-2.0 * math.log(THETA_BASE) / HEAD_SIZE)
    )
    angles = token_position.astype(F32)[:, None] * frequency
    return jnp.cos(angles), jnp.sin(angles)


def apply_rotary(values, cosine, sine):
    half_dim = HEAD_SIZE // 2
    first_half = values[..., :half_dim]
    second_half = values[..., half_dim:]
    return jnp.concatenate(
        [first_half * cosine - second_half * sine, second_half * cosine + first_half * sine],
        axis=-1,
    )


def head_norm_rotary(values, gain, cosine, sine):
    rows, width = values.shape
    heads = values.reshape(rows, width // HEAD_SIZE, HEAD_SIZE)
    turned = apply_rotary(row_scaling(heads, gain), cosine[:, None, :], sine[:, None, :])
    return turned.reshape(rows, width)


def shards(
    span_hidden,
    attn_gain,
    kv_weight,
    q_gain,
    key_norm_gain,
    q_weight,
    o_weight,
    decode_hidden,
    cache,
    cache_len,
    block_owner,
    block_slot,
):
    seq_index = lax.axis_index("z") * Y + lax.axis_index("y")
    prefill_side = lax.axis_index("role") == 0
    span_rows = span_hidden.shape[1]
    local_width = kv_weight.shape[2]
    local_heads = local_width // HEAD_SIZE
    steps, requests, width = decode_hidden.shape
    rows = steps * requests
    local_query = q_weight.shape[1]
    seq_count, block_count = block_owner.shape
    buffer_tokens = seq_count * CAPACITY * BLOCK_TOKENS

    def prefill():
        normed = row_scaling(span_hidden[0].astype(F32), attn_gain).astype(BF16)
        projected = jnp.einsum("td,dcw->ctw", normed, kv_weight, preferred_element_type=F32)
        cosine, sine = rotary_tables(seq_index * span_rows + jnp.arange(span_rows, dtype=jnp.int32))
        keys = head_norm_rotary(projected[0], key_norm_gain, cosine, sine)
        span_kv = jnp.concatenate([keys, projected[1]], axis=1).astype(BF16)

        block_number = jnp.arange(block_count, dtype=jnp.int32)
        same_owner = block_owner[:, :, None] == block_owner[:, None, :]
        earlier = block_number[None, None, :] < block_number[None, :, None]
        rank_table = jnp.sum(jnp.logical_and(same_owner, earlier).astype(jnp.int32), axis=2)
        token = jnp.arange(span_rows, dtype=jnp.int32) % BLOCK_TOKENS
        place = jnp.arange(buffer_tokens, dtype=jnp.int32)
        own_owner = lax.dynamic_index_in_dim(block_owner, seq_index, 0, keepdims=False)
        own_rank = lax.dynamic_index_in_dim(rank_table, seq_index, 0, keepdims=False)
        sent_to = jnp.repeat(own_owner * CAPACITY + own_rank, BLOCK_TOKENS) * BLOCK_TOKENS + token
        spread = (place[:, None] == sent_to[None, :]).astype(BF16)
        payload = jnp.dot(spread, span_kv, preferred_element_type=F32).astype(BF16)
        arrived = lax.all_to_all(
            payload.reshape(seq_count, CAPACITY * BLOCK_TOKENS, 2 * local_width),
            SEQ, split_axis=0, concat_axis=0, tiled=True,
        ).reshape(buffer_tokens, 2 * local_width)
        came_as = jnp.arange(seq_count, dtype=jnp.int32)[:, None] * CAPACITY + rank_table
        target = jnp.where(block_owner == seq_index, block_slot, -1)
        source = jnp.sum(
            jnp.where(target[None] == block_number[:, None, None], came_as[None], 0), axis=(1, 2)
        )
        taken_from = jnp.repeat(source, BLOCK_TOKENS) * BLOCK_TOKENS + token
        gather = (taken_from[:, None] == place[None, :]).astype(BF16)
        pool = jnp.dot(gather, arrived, preferred_element_type=F32).astype(BF16)
        return span_kv, pool, jnp.zeros((steps, requests, width), BF16)

    def decode():
        weight = lax.all_to_all(
            jnp.broadcast_to(q_weight[None], (Y,) + q_weight.shape), "y",
            split_axis=0, concat_axis=0, tiled=True,
        ).reshape(Y * q_weight.shape[0], local_query)
        out_weight = lax.all_to_all(jnp.broadcast_to(o_weight[None], (Y,) + o_weight.shape), "y", split_axis=0, concat_axis=0, tiled=True)
        hidden = decode_hidden.reshape(rows, width).astype(F32)
        normed = row_scaling(hidden, attn_gain).astype(BF16)
        chunk = width // Z
        spread = lax.all_to_all(
            normed.reshape(rows, Z, chunk).transpose(1, 0, 2), "z",
            split_axis=0, concat_axis=0, tiled=True,
        ).reshape(Z * rows, chunk)

        position = (
            cache_len[None, :] + jnp.arange(steps, dtype=jnp.int32)[:, None]
        ).reshape(rows)
        cosine, sine = rotary_tables(position)
        fresh = jnp.einsum("rd,dcw->crw", normed, kv_weight, preferred_element_type=F32)
        new_keys = head_norm_rotary(fresh[0], key_norm_gain, cosine, sine).astype(BF16)
        new_values = fresh[1].astype(BF16)

        partial = jnp.dot(spread, weight, preferred_element_type=F32).astype(BF16)
        returned = lax.all_to_all(
            partial.reshape(Z, rows, local_query), "z", split_axis=0, concat_axis=0, tiled=True
        )
        query_raw = jnp.sum(returned.astype(F32), axis=0)
        query = head_norm_rotary(query_raw, q_gain, cosine, sine).astype(BF16)

        context = cache.shape[1]
        group = local_query // local_width
        scale = HEAD_SIZE ** (-0.5)
        row = jnp.arange(rows, dtype=jnp.int32)
        slot = jnp.arange(requests * context, dtype=jnp.int32)
        limit = jnp.repeat(cache_len, context)
        own = (row[:, None] % requests) == (slot[None, :] // context)
        seen = jnp.logical_and(own, (slot % context)[None, :] < limit[None, :])
        own_new = (row[:, None] % requests) == (row[None, :] % requests)
        seen_new = jnp.logical_and(own_new, row[None, :] // requests <= row[:, None] // requests)
        attended = []
        for head in range(local_heads):
            columns = slice(head * HEAD_SIZE, (head + 1) * HEAD_SIZE)
            keys = cache[:, :, 0, columns].reshape(requests * context, HEAD_SIZE)
            values = cache[:, :, 1, columns].reshape(requests * context, HEAD_SIZE)
            queries = query[:, head * group * HEAD_SIZE : (head + 1) * group * HEAD_SIZE]
            queries = queries.reshape(rows, group, HEAD_SIZE)
            old = jnp.einsum("rgd,kd->rgk", queries, keys, preferred_element_type=F32) * scale
            new = jnp.einsum(
                "rgd,kd->rgk", queries, new_keys[:, columns], preferred_element_type=F32
            ) * scale
            old = jnp.where(seen[:, None, :], old, -jnp.inf)
            new = jnp.where(seen_new[:, None, :], new, -jnp.inf)
            top = jnp.maximum(
                jnp.max(old, axis=-1, keepdims=True), jnp.max(new, axis=-1, keepdims=True)
            )
            old_exp = jnp.exp(old - top)
            new_exp = jnp.exp(new - top)
            total = jnp.sum(old_exp, axis=-1, keepdims=True) + jnp.sum(
                new_exp, axis=-1, keepdims=True
            )
            mixed = jnp.einsum(
                "rgk,kd->rgd", (old_exp / total).astype(BF16), values, preferred_element_type=F32
            ) + jnp.einsum(
                "rgk,kd->rgd", (new_exp / total).astype(BF16), new_values[:, columns],
                preferred_element_type=F32,
            )
            attended.append(mixed.reshape(rows, group * HEAD_SIZE))
        attended = jnp.concatenate(attended, axis=1).astype(BF16)
        gathered = lax.all_to_all(
            jnp.broadcast_to(attended[None], (Z, rows, local_query)), "z",
            split_axis=0, concat_axis=0, tiled=True,
        ).reshape(Z * rows, local_query)
        partial_out = jnp.concatenate(
            [
                jnp.dot(gathered, out_weight[part], preferred_element_type=F32).astype(BF16)
                for part in range(Y)
            ],
            axis=1,
        )
        back = lax.all_to_all(
            partial_out.reshape(Z, rows, chunk), "z", split_axis=0, concat_axis=0, tiled=True
        )
        tp_count = lax.axis_size("tp")
        delta = back.astype(F32)
        for shift in range(1, tp_count):
            route = [(i, (i + shift) % tp_count) for i in range(tp_count)]
            delta = delta + lax.ppermute(back, "tp", route).astype(F32)
        delta = delta.transpose(1, 0, 2).reshape(rows, width)
        decoded = (hidden + delta).astype(BF16).reshape(steps, requests, width)
        nothing = jnp.zeros((span_rows, 2 * local_width), BF16)
        return nothing, nothing, decoded

    span_kv, pool, decoded = lax.cond(prefill_side, prefill, decode)
    handed = lax.ppermute(pool, "role", [(0, 1)])
    kv = jnp.where(prefill_side, span_kv, handed)
    kv_sections = kv.reshape(1, span_rows, 2, local_width)
    return kv_sections, decoded[None]


def solution(mesh):
    shape = mesh.devices.shape
    fine = Mesh(mesh.devices.reshape(shape[0], Z, Y, shape[2]), ("role", "z", "y", "tp"))
    placed = (
        P("role", SEQ, None),
        P(),
        P(None, None, "tp"),
        P(),
        P(),
        P(SEQ, "tp"),
        P("tp", SEQ),
        P(None, SEQ, None),
        P(SEQ, None, None, "tp"),
        P(SEQ),
        P(),
        P(),
    )
    return jax.shard_map(
        shards,
        mesh=fine,
        in_specs=placed,
        out_specs=(P("role", SEQ, None, "tp"), P("role", None, SEQ, None)),
        check_vma=False,
    )
```

time: 669 us -> 129 us (0.19)
  waiting for transfers between devices: 376 us -> 49.4 us
  blocking collectives: 148 us -> 25.2 us
  starting transfers between devices: 63.4 us -> 26.7 us
  matrix products: 22.7 us -> 8.62 us
  between operations: 14.6 us -> 0.67 us
  other arithmetic: 17.7 us -> 5.35 us
  local copies, waits for them, and re-layouts: 23.8 us -> 11.6 us
    all_gather x4 -> x0, waiting for transfers between devices: 238 us -> none  [shards(): lax.all_gather(normed, 'seq', axis=0, tiled=True)]
    all_gather x4 -> x0, blocking collectives: 148 us -> none  [shards(): lax.all_gather(attended, 'seq', axis=0, tiled=True)]
    psum x1 -> x0, waiting for transfers between devices: 93.3 us -> none  [shards(): delta = lax.psum(row_out.astype(jnp.bfloat16), 'tp').astype(jnp.float32)]
    all_to_all x10 -> x4, starting transfers between devices: 61.9 us -> 20.6 us  [the longest x1 9.01 us: decode(): lax.all_to_all(normed.reshape(rows, Z, chunk).transpose(1, 0, 2), 'z', sp...]
    all_to_all x0 -> x2, blocking collectives: none -> 25.2 us  [the longest x1 14.5 us: decode(): lax.all_to_all(jnp.broadcast_to(attended[None], (Z, rows, local_query)),...]
    all_to_all x22 -> x0, local copies, waits for them, and re-layouts: 14.1 us -> none  [the longest x12 5.69 us: shards(): lax.all_to_all(partial_out.astype(jnp.bfloat16), 'seq', split_axis=0, con...]
    dot_general x29 -> x14, matrix products: 22.7 us -> 8.62 us  [the longest x1 3.33 us: decode(): jnp.einsum('rd,dcw->crw', normed, kv_weight, preferred_element_type=F32)]
    all_to_all x10 -> x4, waiting for transfers between devices: 42.7 us -> 44 us  [the longest x1 15.8 us: decode(): lax.all_to_all(jnp.broadcast_to(q_weight[None], (Y,) + q_weight.shape), '...]
  transfers between devices with their start and end apart: 16 -> 8, of which waited for: 12 -> 7; matrix products, arithmetic and copies ran while one was open for 7% -> 11% of each run, Pallas kernels for 0% -> 0%
where the time goes in v1:
time: 129 us; the launch traced here: 128 us
  waiting for transfers between devices  49.4 us (38%)
  starting transfers between devices  26.7 us (21%)
  blocking collectives  25.2 us (20%)
  local copies, waits for them, and re-layouts  11.6 us (9%)
  matrix products  8.62 us (7%)
  other arithmetic  5.35 us (4%)
    all_to_all x1, waiting for transfers between devices, decode(): lax.all_to_all(jnp.broadcast_to(q_weight[None], (Y,) + q_weight.shape), '...  15.8 us
    all_to_all x1, blocking collectives, decode(): lax.all_to_all(jnp.broadcast_to(attended[None], (Z, rows, local_query)),...  14.5 us
    all_to_all x1, waiting for transfers between devices, decode(): lax.all_to_all(jnp.broadcast_to(o_weight[None], (Y,) + o_weight.shape), '...  12.6 us
    all_to_all x1, blocking collectives, decode(): lax.all_to_all(partial_out.reshape(Z, rows, chunk), 'z', split_axis=0, co...  10.7 us
    all_to_all x1, starting transfers between devices, decode(): lax.all_to_all(normed.reshape(rows, Z, chunk).transpose(1, 0, 2), 'z', sp...  9.01 us
    all_to_all x1, waiting for transfers between devices, decode(): lax.all_to_all(partial.reshape(Z, rows, local_query), 'z', split_axis=0,...  8.21 us
    all_to_all x1, waiting for transfers between devices, decode(): lax.all_to_all(normed.reshape(rows, Z, chunk).transpose(1, 0, 2), 'z', sp...  7.34 us
    ppermute x3, starting transfers between devices, decode(): delta = delta + lax.ppermute(back, 'tp', route).astype(F32)  4.82 us
  transfers between devices with their start and end apart: 8, of which 7 were waited for; matrix products, arithmetic and copies ran while one was open for 11% of the time, Pallas kernels for 0%

profile of v1, /device:TPU:1, one launch (start us, length us, event | category | flops | bytes accessed | tf_op | source)
XLA Modules:
  0.0 128.4 jit_solution(6709786004132640070)
XLA Ops:
  0.6 123.5 %conditional.1 = (bf16[256,512]{1,0:T(8,128)(2,1)S(1)}, bf16[256,512]{1,0:T(8,128)(2,1)S(1)}, bf16[1,4,4,5120]{3,2,1,0:T(4,128)(2,1)S(1)}) conditional(s32[]{:T(128)} %convert_element_type.126, (bf16[4,4,5120]{2,1,0:T(4,128)(2,1)}, s32[4]{0:T(128)}, f32[5120]{0:T(1024)}, bf16[160,2048]{1,0:T(8,128)(2,1)}, f32[128]{0:T(128)}, ...), branch_computations={%region_0.13_spmd, %region_13.18_spmd} | conditional | flops 1622531968 | bytes 62269352 | solution.py:200
  0.7 1.2 multiply_reduce_fusion
  1.8 1.0 reshape.618
  2.8 0.1 rsqrt.38
  2.9 0.7 mul.243
  3.6 0.1 fusion.13
  3.7 0.7 copy.50
  4.4 9.0 %all-to-all-start = ((bf16[8,16,640]{2,1,0:T(8,128)(2,1)}), bf16[8,16,640]{2,1,0:T(8,128)(2,1)S(1)}, u32[]{:S(2)}, u32[]{:S(2)}) async-start(bf16[8,16,640]{2,1,0:T(8,128)(2,1)} %copy.50), calls=%async_computation | async-start | bytes 327680 | tf_op jit(solution)/shard_map/cond/branch_0_fun/all_to_all | solution.py:117
  13.4 0.9 reshape.619
  14.4 7.3 %all-to-all-done = bf16[8,16,640]{2,1,0:T(8,128)(2,1)S(1)} async-done(((bf16[8,16,640]{2,1,0:T(8,128)(2,1)}), bf16[8,16,640]{2,1,0:T(8,128)(2,1)S(1)}, u32[]{:S(2)}, u32[]{:S(2)}) %all-to-all-start) | async-done | bytes 163872 | tf_op jit(solution)/shard_map/cond/branch_0_fun/all_to_all | solution.py:117
  21.7 1.8 %broadcast_in_dim.49 = bf16[4,160,2048]{2,1,0:T(8,128)(2,1)} broadcast(bf16[160,2048]{1,0:T(8,128)(2,1)S(1)} %copy-done.2), dimensions={1,2} | broadcast | bytes 3276800 | tf_op jit(solution)/shard_map/cond/branch_0_fun/broadcast_in_dim | solution.py:110
  23.5 4.3 %all-to-all-start.1 = ((bf16[4,160,2048]{2,1,0:T(8,128)(2,1)}), bf16[4,160,2048]{2,1,0:T(8,128)(2,1)S(1)}, u32[]{:S(2)}, u32[]{:S(2)}) async-start(bf16[4,160,2048]{2,1,0:T(8,128)(2,1)} %broadcast_in_dim.49), calls=%async_computation.1 | async-start | bytes 5242880 | tf_op jit(solution)/shard_map/cond/branch_0_fun/all_to_all | solution.py:109
  27.9 3.3 %fusion.8 = f32[2,16,256]{2,1,0:T(8,128)S(1)} fusion(bf16[5120,2,256]{2,1,0:T(2,128)(2,1)} %get-tuple-element.172, f32[16,5120]{1,0:T(8,128)S(1)} %reshape.619, f32[5120]{0:T(1024)S(1)} %copy-done.7, f32[16]{0:T(128)S(1)} %rsqrt.38), kind=kOutput, calls=%fused_computation.19 | convolution fusion | flops 84131840 | bytes 5623872 | tf_op jit(solution)/shard_map/cond/branch_0_fun/rd,dcw->crw/dot_general | solution.py:126
  31.3 0.1 convert_element_type.98
  31.4 0.1 multiply_reduce_fusion.2
  31.5 0.1 multiply_cosine_fusion
  31.7 0.1 subtract_convert_fusion.1
  31.8 0.1 pad_maximum_fusion.3
  32.0 15.8 %all-to-all-done.1 = bf16[4,160,2048]{2,1,0:T(8,128)(2,1)S(1)} async-done(((bf16[4,160,2048]{2,1,0:T(8,128)(2,1)}), bf16[4,160,2048]{2,1,0:T(8,128)(2,1)S(1)}, u32[]{:S(2)}, u32[]{:S(2)}) %all-to-all-start.1) | async-done | bytes 2621472 | tf_op jit(solution)/shard_map/cond/branch_0_fun/all_to_all | solution.py:109
  47.8 1.4 %convolution_convert_fusion = bf16[128,2048]{1,0:T(8,128)(2,1)} fusion(bf16[128,640]{1,0:T(8,128)(2,1)S(1)} %bitcast.128, bf16[640,2048]{1,0:T(8,128)(2,1)S(1)} %bitcast.124), kind=kOutput, calls=%fused_computation.2 | convolution fusion | flops 335806464 | bytes 3309568 | tf_op jit(solution)/shard_map/cond/branch_0_fun/dot_general | solution.py:130
  49.2 3.6 %all-to-all-start.2 = ((bf16[8,16,2048]{2,1,0:T(8,128)(2,1)}), bf16[8,16,2048]{2,1,0:T(8,128)(2,1)S(1)}, u32[]{:S(2)}, u32[]{:S(2)}) async-start(bf16[8,16,2048]{2,1,0:T(8,128)(2,1)} %bitcast.4), calls=%async_computation.2 | async-start | bytes 1048576 | tf_op jit(solution)/shard_map/cond/branch_0_fun/all_to_all | solution.py:131
  52.8 0.6 copy.79
  53.4 1.1 copy.54
  54.5 0.7 compare_and_fusion.1
  55.2 0.6 fusion.27
  55.8 0.8 fusion.56
  56.6 8.2 %all-to-all-done.2 = bf16[8,16,2048]{2,1,0:T(8,128)(2,1)S(1)} async-done(((bf16[8,16,2048]{2,1,0:T(8,128)(2,1)}), bf16[8,16,2048]{2,1,0:T(8,128)(2,1)S(1)}, u32[]{:S(2)}, u32[]{:S(2)}) %all-to-all-start.2) | async-done | bytes 524320 | tf_op jit(solution)/shard_map/cond/branch_0_fun/all_to_all | solution.py:131
  64.8 1.8 %broadcast_in_dim.55 = bf16[4,2048,160]{1,2,0:T(8,128)(2,1)} broadcast(bf16[2048,160]{0,1:T(8,128)(2,1)S(1)} %copy-done.3), dimensions={1,2} | broadcast | bytes 3276800 | tf_op jit(solution)/shard_map/cond/branch_0_fun/broadcast_in_dim | solution.py:113
  66.7 3.7 %all-to-all-start.4 = ((bf16[4,2048,160]{1,2,0:T(8,128)(2,1)}), bf16[4,2048,160]{1,2,0:T(8,128)(2,1)S(1)}, u32[]{:S(2)}, u32[]{:S(2)}) async-start(bf16[4,2048,160]{1,2,0:T(8,128)(2,1)} %broadcast_in_dim.55), calls=%async_computation.4 | async-start | bytes 5242880 | tf_op jit(solution)/shard_map/cond/branch_0_fun/all_to_all | solution.py:113
  70.5 0.1 multiply_reduce_fusion.1
  70.6 0.8 multiply_multiply_fusion
  71.4 0.8 subtract_convert_fusion
  72.2 0.1 pad_maximum_fusion.1
  72.3 0.9 fusion.60
  73.2 0.3 fusion.59
  73.5 0.2 fusion.11
  73.7 0.2 fusion.21
  73.9 0.3 fusion.19
  74.2 0.2 fusion.6
  74.5 0.2 fusion.58
  74.7 0.3 fusion.57
  75.0 0.2 fusion.22
  75.1 0.2 fusion.12
  75.3 0.2 fusion.20
  75.6 0.2 fusion.7
  75.9 12.6 %all-to-all-done.4 = bf16[4,2048,160]{1,2,0:T(8,128)(2,1)S(1)} async-done(((bf16[4,2048,160]{1,2,0:T(8,128)(2,1)}), bf16[4,2048,160]{1,2,0:T(8,128)(2,1)S(1)}, u32[]{:S(2)}, u32[]{:S(2)}) %all-to-all-start.4) | async-done | bytes 2621472 | tf_op jit(solution)/shard_map/cond/branch_0_fun/all_to_all | solution.py:113
  88.5 14.5 %all_to_all.28 = bf16[8,16,2048]{2,1,0:T(8,128)(2,1)S(1)} all-to-all(bf16[8,16,2048]{2,1,0:T(8,128)(2,1)S(1)} %broadcast_in_dim.54), channel_id=1, replica_groups=mesh['role'=2,'z'=8,'y'=4,'tp'=4] {'z'}, dimensions={0} | all-to-all | bytes 1048576 | tf_op jit(solution)/shard_map/cond/branch_0_fun/all_to_all | solution.py:176
  103.1 0.3 convolution_convert_fusion.1
  103.4 0.3 convolution_convert_fusion.2
  103.8 0.3 convolution_convert_fusion.3
  104.1 0.3 convolution_convert_fusion.4
  104.5 0.2 copy.51
  104.6 10.7 %all_to_all.29 = bf16[8,16,640]{2,1,0:T(8,128)(2,1)S(1)} all-to-all(bf16[8,16,640]{2,1,0:T(8,128)(2,1)S(1)} %bitcast.129), channel_id=1, replica_groups=mesh['role'=2,'z'=8,'y'=4,'tp'=4] {'z'}, dimensions={0} | all-to-all | bytes 327680 | tf_op jit(solution)/shard_map/cond/branch_0_fun/all_to_all | solution.py:187
  115.3 1.2 collective-permute-start
  116.5 2.5 %collective-permute-start.1 = (bf16[8,16,640]{2,1,0:T(8,128)(2,1)S(1)}, bf16[8,16,640]{2,1,0:T(8,128)(2,1)S(1)}, u32[]{:S(2)}, u32[]{:S(2)}) collective-permute-start(bf16[8,16,640]{2,1,0:T(8,128)(2,1)S(1)} %all_to_all.29), channel_id=1, source_target_pairs={{0,2},{1,3},{2,0},{3,1},{4,6},{5,7},{6,4},{7,5},{8,10},{9,11},{10,... | collective-permute-start | bytes 491528 | tf_op jit(solution)/shard_map/cond/branch_0_fun/ppermute | solution.py:194
  119.0 1.2 collective-permute-start.2
  120.1 0.6 collective-permute-done
  120.7 2.7 %collective-permute-done.1 = bf16[8,16,640]{2,1,0:T(8,128)(2,1)S(1)} collective-permute-done((bf16[8,16,640]{2,1,0:T(8,128)(2,1)S(1)}, bf16[8,16,640]{2,1,0:T(8,128)(2,1)S(1)}, u32[]{:S(2)}, u32[]{:S(2)}) %collective-permute-start.1) | collective-permute-done | bytes 163872 | tf_op jit(solution)/shard_map/cond/branch_0_fun/ppermute | solution.py:194
  123.5 0.1 copy.52
  123.6 0.1 reshape.612
  123.7 0.1 fusion.16
  124.1 1.3 %collective-permute-start.3 = (bf16[256,512]{1,0:T(8,128)(2,1)S(1)}, bf16[256,512]{1,0:T(8,128)(2,1)S(1)}, u32[]{:S(2)}, u32[]{:S(2)}) collective-permute-start(bf16[256,512]{1,0:T(8,128)(2,1)S(1)} %get-tuple-element.55), channel_id=1, source_target_pairs={{0,128},{1,129},{2,130},{3,131},{4,132},{5,133},{6,134},{7,135},{8... | collective-permute-start | bytes 786440 | tf_op jit(solution)/shard_map/ppermute | solution.py:201
  125.4 2.1 %collective-permute-done.3 = bf16[256,512]{1,0:T(8,128)(2,1)S(1)} collective-permute-done((bf16[256,512]{1,0:T(8,128)(2,1)S(1)}, bf16[256,512]{1,0:T(8,128)(2,1)S(1)}, u32[]{:S(2)}, u32[]{:S(2)}) %collective-permute-start.3) | collective-permute-done | bytes 262176 | tf_op jit(solution)/shard_map/ppermute | solution.py:201
  127.6 0.8 reshape.617
  (56 shorter events, 0.7 us)
Async XLA Ops:
  0.6 21.1 %copy-start.2 = (bf16[160,2048]{1,0:T(8,128)(2,1)S(1)}, bf16[160,2048]{1,0:T(8,128)(2,1)}, u32[]{:S(2)}) copy-start(bf16[160,2048]{1,0:T(8,128)(2,1)} %get-tuple-element.65) | copy-start | bytes 1966084 | tf_op jit(solution)/shard_map/cond
  4.4 17.3 %all-to-all-start = ((bf16[8,16,640]{2,1,0:T(8,128)(2,1)}), bf16[8,16,640]{2,1,0:T(8,128)(2,1)S(1)}, u32[]{:S(2)}, u32[]{:S(2)}) async-start(bf16[8,16,640]{2,1,0:T(8,128)(2,1)} %copy.50), calls=%async_computation | async-start | bytes 327680 | tf_op jit(solution)/shard_map/cond/branch_0_fun/all_to_all | solution.py:117
  23.5 4.3 %copy-start.7 = (f32[5120]{0:T(1024)S(1)}, f32[5120]{0:T(1024)}, u32[]{:S(2)}) copy-start(f32[5120]{0:T(1024)} %get-tuple-element.35) | copy-start | bytes 61444 | tf_op jit(solution)/shard_map/cond
  23.5 24.2 %all-to-all-start.1 = ((bf16[4,160,2048]{2,1,0:T(8,128)(2,1)}), bf16[4,160,2048]{2,1,0:T(8,128)(2,1)S(1)}, u32[]{:S(2)}, u32[]{:S(2)}) async-start(bf16[4,160,2048]{2,1,0:T(8,128)(2,1)} %broadcast_in_dim.49), calls=%async_computation.1 | async-start | bytes 5242880 | tf_op jit(solution)/shard_map/cond/branch_0_fun/all_to_all | solution.py:109
  27.9 3.4 %copy-start.15 = (s32[4]{0:T(128)S(1)}, s32[4]{0:T(128)}, u32[]{:S(2)}) copy-start(s32[4]{0:T(128)} %get-tuple-element.64) | copy-start | bytes 52 | tf_op jit(solution)/shard_map/cond
  27.9 3.7 %copy-start.13 = (f32[128]{0:T(128)S(1)}, f32[128]{0:T(128)}, u32[]{:S(2)}) copy-start(f32[128]{0:T(128)} %get-tuple-element.40) | copy-start | bytes 1540 | tf_op jit(solution)/shard_map/cond
  31.6 17.6 %copy-start.8 = (f32[16,64]{1,0:T(8,128)}, f32[16,64]{1,0:T(8,128)S(1)}, u32[]{:S(2)}) copy-start(f32[16,64]{1,0:T(8,128)S(1)} %get-tuple-element.195) | copy-start | bytes 12292 | tf_op jit(solution)/shard_map/cond
  49.1 15.7 %copy-start.3 = (bf16[2048,160]{0,1:T(8,128)(2,1)S(1)}, bf16[2048,160]{0,1:T(8,128)(2,1)}, u32[]{:S(2)}) copy-start(bf16[2048,160]{0,1:T(8,128)(2,1)} %get-tuple-element.68) | copy-start | bytes 1966084 | tf_op jit(solution)/shard_map/cond
  49.2 15.7 %all-to-all-start.2 = ((bf16[8,16,2048]{2,1,0:T(8,128)(2,1)}), bf16[8,16,2048]{2,1,0:T(8,128)(2,1)S(1)}, u32[]{:S(2)}, u32[]{:S(2)}) async-start(bf16[8,16,2048]{2,1,0:T(8,128)(2,1)} %bitcast.4), calls=%async_computation.2 | async-start | bytes 1048576 | tf_op jit(solution)/shard_map/cond/branch_0_fun/all_to_all | solution.py:131
  66.7 21.8 %all-to-all-start.4 = ((bf16[4,2048,160]{1,2,0:T(8,128)(2,1)}), bf16[4,2048,160]{1,2,0:T(8,128)(2,1)S(1)}, u32[]{:S(2)}, u32[]{:S(2)}) async-start(bf16[4,2048,160]{1,2,0:T(8,128)(2,1)} %broadcast_in_dim.55), calls=%async_computation.4 | async-start | bytes 5242880 | tf_op jit(solution)/shard_map/cond/branch_0_fun/all_to_all | solution.py:113
  70.3 3.6 %copy-start.6 = (bf16[4,128,1,128]{3,1,0,2:T(8,128)(2,1)S(1)}, bf16[4,128,1,128]{3,1,0,2:T(8,128)(2,1)}, u32[]{:S(2)}) copy-start(bf16[4,128,1,128]{3,1,0,2:T(8,128)(2,1)} %get-tuple-element.185) | copy-start | bytes 393220 | tf_op jit(solution)/shard_map/cond
  70.3 3.8 %copy-start.12 = (bf16[16,256]{1,0:T(8,128)(2,1)S(1)}, bf16[16,256]{1,0:T(8,128)(2,1)}, u32[]{:S(2)}) copy-start(bf16[16,256]{1,0:T(8,128)(2,1)} %fusion.27) | copy-start | bytes 24580 | tf_op jit(solution)/shard_map/cond
  70.4 4.1 %copy-start.9 = (bf16[2,8,2,128]{3,1,2,0:T(8,128)(2,1)S(1)}, bf16[2,8,2,128]{3,1,2,0:T(8,128)(2,1)}, u32[]{:S(2)}) copy-start(bf16[2,8,2,128]{3,1,2,0:T(8,128)(2,1)} %copy.79) | copy-start | bytes 24580 | tf_op jit(solution)/shard_map/cond
  70.4 4.1 %copy-start.10 = (pred[16,16]{1,0:T(8,128)(4,1)S(1)}, pred[16,16]{1,0:T(8,128)(4,1)}, u32[]{:S(2)}) copy-start(pred[16,16]{1,0:T(8,128)(4,1)} %compare_and_fusion.1) | copy-start | bytes 772 | tf_op jit(solution)/shard_map/cond
  103.7 20.0 %copy-start.1 = (bf16[4,4,5120]{2,1,0:T(4,128)(2,1)S(1)}, bf16[4,4,5120]{2,1,0:T(4,128)(2,1)}, u32[]{:S(2)}) copy-start(bf16[4,4,5120]{2,1,0:T(4,128)(2,1)} %get-tuple-element.63) | copy-start | bytes 491524 | tf_op jit(solution)/shard_map/cond
  115.3 5.4 %collective-permute-start = (bf16[8,16,640]{2,1,0:T(8,128)(2,1)S(1)}, bf16[8,16,640]{2,1,0:T(8,128)(2,1)S(1)}, u32[]{:S(2)}, u32[]{:S(2)}) collective-permute-start(bf16[8,16,640]{2,1,0:T(8,128)(2,1)S(1)} %all_to_all.29), channel_id=1, source_target_pairs={{0,1},{1,2},{2,3},{3,0},{4,5},{5,6},{6,7},{7,4},{8,9},{9,10},{10,1... | collective-permute-start | bytes 491528 | tf_op jit(solution)/shard_map/cond/branch_0_fun/ppermute | solution.py:194
  116.5 6.9 %collective-permute-start.1 = (bf16[8,16,640]{2,1,0:T(8,128)(2,1)S(1)}, bf16[8,16,640]{2,1,0:T(8,128)(2,1)S(1)}, u32[]{:S(2)}, u32[]{:S(2)}) collective-permute-start(bf16[8,16,640]{2,1,0:T(8,128)(2,1)S(1)} %all_to_all.29), channel_id=1, source_target_pairs={{0,2},{1,3},{2,0},{3,1},{4,6},{5,7},{6,4},{7,5},{8,10},{9,11},{10,... | collective-permute-start | bytes 491528 | tf_op jit(solution)/shard_map/cond/branch_0_fun/ppermute | solution.py:194
  119.0 4.5 %collective-permute-start.2 = (bf16[8,16,640]{2,1,0:T(8,128)(2,1)S(1)}, bf16[8,16,640]{2,1,0:T(8,128)(2,1)S(1)}, u32[]{:S(2)}, u32[]{:S(2)}) collective-permute-start(bf16[8,16,640]{2,1,0:T(8,128)(2,1)S(1)} %all_to_all.29), channel_id=1, source_target_pairs={{0,3},{1,0},{2,1},{3,2},{4,7},{5,4},{6,5},{7,6},{8,11},{9,8},{10,9... | collective-permute-start | bytes 491528 | tf_op jit(solution)/shard_map/cond/branch_0_fun/ppermute | solution.py:194
  124.1 4.2 %copy-start.4 = (bf16[1,4,4,5120]{3,2,1,0:T(4,128)(2,1)}, bf16[1,4,4,5120]{3,2,1,0:T(4,128)(2,1)S(1)}, u32[]{:S(2)}) copy-start(bf16[1,4,4,5120]{3,2,1,0:T(4,128)(2,1)S(1)} %get-tuple-element.53) | copy-start | bytes 491524
  124.1 3.4 %collective-permute-start.3 = (bf16[256,512]{1,0:T(8,128)(2,1)S(1)}, bf16[256,512]{1,0:T(8,128)(2,1)S(1)}, u32[]{:S(2)}, u32[]{:S(2)}) collective-permute-start(bf16[256,512]{1,0:T(8,128)(2,1)S(1)} %get-tuple-element.55), channel_id=1, source_target_pairs={{0,128},{1,129},{2,130},{3,131},{4,132},{5,133},{6,134},{7,135},{8... | collective-permute-start | bytes 786440 | tf_op jit(solution)/shard_map/ppermute | solution.py:201

commit v2 on v1

v2 whole, which is shorter than its diff:
```python
import math

import jax
import jax.numpy as jnp
from jax import lax
from jax.experimental import pallas as pl
from jax.experimental.pallas import tpu as pltpu
from jax.sharding import Mesh, PartitionSpec as P

QUERY_HEADS = 64
KEY_VALUE_HEADS = 8
HEAD_SIZE = 128
EPSILON = 1e-06
THETA_BASE = 1000000.0

Z, Y = 8, 4
SEQ = ("z", "y")
BLOCK_TOKENS = 8
CAPACITY = 2
VMEM_LIMIT = 32 * 2**20
F32, BF16 = jnp.float32, jnp.bfloat16


def row_scaling(values, weights):
    return values * lax.rsqrt(jnp.mean(values * values, axis=-1, keepdims=True) + EPSILON) * weights


def rotary_tables(token_position):
    half_dim = HEAD_SIZE // 2
    frequency = jnp.exp(
        jnp.arange(half_dim, dtype=F32) * (-2.0 * math.log(THETA_BASE) / HEAD_SIZE)
    )
    angles = token_position.astype(F32)[:, None] * frequency
    return jnp.cos(angles), jnp.sin(angles)


def apply_rotary(values, cosine, sine):
    half_dim = HEAD_SIZE // 2
    first_half = values[..., :half_dim]
    second_half = values[..., half_dim:]
    return jnp.concatenate(
        [first_half * cosine - second_half * sine, second_half * cosine + first_half * sine],
        axis=-1,
    )


def head_norm_rotary(values, gain, cosine, sine):
    rows, width = values.shape
    heads = values.reshape(rows, width // HEAD_SIZE, HEAD_SIZE)
    turned = apply_rotary(row_scaling(heads, gain), cosine[:, None, :], sine[:, None, :])
    return turned.reshape(rows, width)


def dot(a, b):
    return jnp.dot(a, b, preferred_element_type=F32)


def norm_kernel(y_ref, hidden_ref, gain_ref, spread_ref, normed_ref, *unused):
    hidden = jnp.concatenate(
        [hidden_ref[step].astype(F32) for step in range(hidden_ref.shape[0])], axis=0
    )
    normed = row_scaling(hidden, gain_ref[...])
    normed_ref[...] = normed.astype(BF16)
    chunk = spread_ref.shape[2]
    shift = lax.rem(Y - y_ref[0], Y) * (chunk // Y)
    for z in range(Z):
        block = normed[:, z * chunk : (z + 1) * chunk]
        spread_ref[z] = pltpu.roll(block, shift, axis=1).astype(BF16)


def query_kernel(rows_ref, own_ref, first_ref, second_ref, third_ref, out_ref):
    tile = 512
    for start in range(0, out_ref.shape[1], tile):
        columns = slice(start, start + tile)
        weight = jnp.concatenate(
            [ref[:, columns] for ref in (own_ref, first_ref, second_ref, third_ref)], axis=0
        )
        out_ref[:, columns] = dot(rows_ref[...], weight).astype(BF16)


def attention_kernel(
    length_ref,
    returned_ref,
    gain_ref,
    cosine_ref,
    sine_ref,
    keys_ref,
    values_ref,
    new_keys_ref,
    new_values_ref,
    out_ref,
    *unused,
):
    rows = returned_ref.shape[1]
    requests = rows // 4
    slots, local_width = keys_ref.shape
    context = slots // requests
    group = returned_ref.shape[2] // local_width
    scale = HEAD_SIZE ** (-0.5)
    cosine = jnp.concatenate([cosine_ref[...]] * group, axis=0)
    sine = jnp.concatenate([sine_ref[...]] * group, axis=0)

    def indices(columns):
        row = lax.broadcasted_iota(jnp.int32, (group * rows, columns), 0) % rows
        return row, lax.broadcasted_iota(jnp.int32, (group * rows, columns), 1)

    row, slot = indices(slots)
    request = slot // context
    limit = jnp.full_like(slot, length_ref[0])
    for one in range(1, requests):
        limit = jnp.where(request == one, length_ref[one], limit)
    seen = jnp.logical_and(row % requests == request, slot % context < limit)
    row, new = indices(rows)
    seen_new = jnp.logical_and(
        row % requests == new % requests, new // requests <= row // requests
    )
    for head in range(local_width // HEAD_SIZE):
        columns = slice(head * HEAD_SIZE, (head + 1) * HEAD_SIZE)
        query = []
        for one in range(head * group, (head + 1) * group):
            part = slice(one * HEAD_SIZE, (one + 1) * HEAD_SIZE)
            total = returned_ref[0, :, part].astype(F32)
            for z in range(1, Z):
                total += returned_ref[z, :, part].astype(F32)
            query.append(total)
        query = row_scaling(jnp.concatenate(query, axis=0), gain_ref[...])
        query = query * cosine + pltpu.roll(query, HEAD_SIZE // 2, axis=1) * sine
        query = query.astype(BF16)
        transposed = (((1,), (1,)), ((), ()))
        old = lax.dot_general(
            query, keys_ref[:, columns], transposed, preferred_element_type=F32
        ) * scale
        new = lax.dot_general(
            query, new_keys_ref[:, columns], transposed, preferred_element_type=F32
        ) * scale
        old = jnp.where(seen, old, -jnp.inf)
        new = jnp.where(seen_new, new, -jnp.inf)
        top = jnp.maximum(
            jnp.max(old, axis=-1, keepdims=True), jnp.max(new, axis=-1, keepdims=True)
        )
        old_exp = jnp.exp(old - top)
        new_exp = jnp.exp(new - top)
        total = jnp.sum(old_exp, axis=-1, keepdims=True) + jnp.sum(new_exp, axis=-1, keepdims=True)
        mixed = dot((old_exp / total).astype(BF16), values_ref[:, columns])
        mixed += dot((new_exp / total).astype(BF16), new_values_ref[:, columns])
        mixed = mixed.astype(BF16)
        for one in range(group):
            part = head * group + one
            block = mixed[one * rows : (one + 1) * rows]
            for z in range(Z):
                out_ref[z, :, part * HEAD_SIZE : (part + 1) * HEAD_SIZE] = block


def shards(
    span_hidden,
    attn_gain,
    kv_weight,
    q_gain,
    key_norm_gain,
    q_weight,
    o_weight,
    decode_hidden,
    cache,
    cache_len,
    block_owner,
    block_slot,
):
    y_index = lax.axis_index("y")
    seq_index = lax.axis_index("z") * Y + y_index
    prefill_side = lax.axis_index("role") == 0
    span_rows = span_hidden.shape[1]
    local_width = kv_weight.shape[2]
    steps, requests, width = decode_hidden.shape
    rows = steps * requests
    depth, local_query = q_weight.shape
    out_depth, out_width = o_weight.shape
    seq_count, block_count = block_owner.shape
    buffer_tokens = seq_count * CAPACITY * BLOCK_TOKENS
    chunk = width // Z
    context = cache.shape[1]
    exchanged = (Z, rows, local_query)

    whole = pl.BlockSpec(memory_space=pltpu.VMEM)
    unwritten = pl.BlockSpec(memory_space=pl.ANY)
    section = jax.ShapeDtypeStruct((span_rows, 2, local_width), BF16)
    buffer = jax.ShapeDtypeStruct((seq_count, CAPACITY * BLOCK_TOKENS, 2 * local_width), BF16)

    def rank_table():
        block_number = jnp.arange(block_count, dtype=jnp.int32)
        same_owner = block_owner[:, :, None] == block_owner[:, None, :]
        earlier = block_number[None, None, :] < block_number[None, :, None]
        return jnp.sum(jnp.logical_and(same_owner, earlier).astype(jnp.int32), axis=2)

    token = jnp.arange(span_rows, dtype=jnp.int32) % BLOCK_TOKENS
    place = jnp.arange(buffer_tokens, dtype=jnp.int32)

    def prefill(*_):
        normed = row_scaling(span_hidden[0].astype(F32), attn_gain).astype(BF16)
        projected = jnp.einsum("td,dcw->ctw", normed, kv_weight, preferred_element_type=F32)
        cosine, sine = rotary_tables(seq_index * span_rows + jnp.arange(span_rows, dtype=jnp.int32))
        keys = head_norm_rotary(projected[0], key_norm_gain, cosine, sine)
        span_kv = jnp.concatenate([keys, projected[1]], axis=1).astype(BF16)
        own_owner = lax.dynamic_index_in_dim(block_owner, seq_index, 0, keepdims=False)
        own_rank = lax.dynamic_index_in_dim(rank_table(), seq_index, 0, keepdims=False)
        sent_to = jnp.repeat(own_owner * CAPACITY + own_rank, BLOCK_TOKENS) * BLOCK_TOKENS + token
        spread = (place[:, None] == sent_to[None, :]).astype(BF16)
        payload = dot(spread, span_kv).astype(BF16)
        return (
            jnp.zeros((Z * rows, chunk), BF16),
            jnp.zeros((rows, HEAD_SIZE), F32),
            jnp.zeros((rows, HEAD_SIZE), F32),
            jnp.zeros((rows, local_width), BF16),
            jnp.zeros((rows, local_width), BF16),
            span_kv.reshape(section.shape),
            payload.reshape(buffer.shape),
        )

    def route(payload, *_):
        turned = o_weight.T
        out_weight = jnp.zeros((Y, out_width, out_depth), BF16)
        for shift in range(Y):
            part = turned
            if shift > 0:
                part = lax.ppermute(turned, "y", [(i, (i - shift) % Y) for i in range(Y)])
            out_weight = lax.dynamic_update_index_in_dim(
                out_weight, part, lax.rem(y_index + shift, Y), 0
            )
        arrived = lax.all_to_all(payload, SEQ, split_axis=0, concat_axis=0, tiled=True)
        block_number = jnp.arange(block_count, dtype=jnp.int32)
        came_as = jnp.arange(seq_count, dtype=jnp.int32)[:, None] * CAPACITY + rank_table()
        target = jnp.where(block_owner == seq_index, block_slot, -1)
        source = jnp.sum(
            jnp.where(target[None] == block_number[:, None, None], came_as[None], 0), axis=(1, 2)
        )
        taken_from = jnp.repeat(source, BLOCK_TOKENS) * BLOCK_TOKENS + token
        gather = (taken_from[:, None] == place[None, :]).astype(BF16)
        pool = dot(gather, arrived.reshape(buffer_tokens, 2 * local_width)).astype(BF16)
        return (
            pool.reshape(section.shape),
            out_weight.reshape(Y * out_width, out_depth),
            jnp.zeros(exchanged, BF16),
        )

    arrived_weights = []
    for shift in range(1, Y):
        pairs = [(i, Y + (i - shift) % Y) for i in range(Y)]
        arrived_weights.append(lax.ppermute(q_weight, ("role", "y"), pairs))

    def project(*_):
        spread, normed, span_kv, payload = pl.pallas_call(
            norm_kernel,
            out_shape=(
                jax.ShapeDtypeStruct((Z, rows, chunk), BF16),
                jax.ShapeDtypeStruct((rows, width), BF16),
                section,
                buffer,
            ),
            in_specs=[
                pl.BlockSpec(memory_space=pltpu.SMEM),
                whole,
                whole,
            ],
            out_specs=[whole] * 2 + [unwritten] * 2,
        )(y_index.astype(jnp.int32).reshape(1), decode_hidden, attn_gain.reshape(1, width))
        spread = lax.all_to_all(spread, "z", split_axis=0, concat_axis=0, tiled=True)
        position = (
            cache_len[None, :] + jnp.arange(steps, dtype=jnp.int32)[:, None]
        ).reshape(rows)
        cosine, sine = rotary_tables(position)
        fresh = jnp.einsum("rd,dcw->crw", normed, kv_weight, preferred_element_type=F32)
        new_keys = head_norm_rotary(fresh[0], key_norm_gain, cosine, sine).astype(BF16)
        new_values = fresh[1].astype(BF16)
        cosine = jnp.concatenate([cosine, cosine], axis=1)
        sine = jnp.concatenate([-sine, sine], axis=1)
        spread = spread.reshape(Z * rows, chunk)
        return spread, cosine, sine, new_keys, new_values, span_kv, payload

    spread, cosine, sine, new_keys, new_values, span_kv, payload = lax.cond(
        prefill_side, prefill, project
    )

    def attend(payload, spread, cosine, sine, new_keys, new_values, *weights):
        partial = pl.pallas_call(
            query_kernel,
            in_specs=[whole] * 5,
            out_specs=whole,
            out_shape=jax.ShapeDtypeStruct((Z * rows, local_query), BF16),
            compiler_params=pltpu.CompilerParams(vmem_limit_bytes=VMEM_LIMIT),
        )(spread, q_weight, *weights)
        returned = lax.all_to_all(
            partial.reshape(exchanged), "z", split_axis=0, concat_axis=0, tiled=True
        )
        slots = requests * context
        attended, pool, out_weight = pl.pallas_call(
            attention_kernel,
            out_shape=(
                jax.ShapeDtypeStruct(exchanged, BF16),
                section,
                jax.ShapeDtypeStruct((Y * out_width, out_depth), BF16),
            ),
            in_specs=[pl.BlockSpec(memory_space=pltpu.SMEM)] + [whole] * 8,
            out_specs=[whole] + [unwritten] * 2,
            compiler_params=pltpu.CompilerParams(vmem_limit_bytes=VMEM_LIMIT),
        )(
            cache_len,
            returned,
            q_gain.reshape(1, HEAD_SIZE),
            cosine,
            sine,
            cache[:, :, 0].reshape(slots, local_width),
            cache[:, :, 1].reshape(slots, local_width),
            new_keys,
            new_values,
        )
        return pool, out_weight, attended

    pool, out_weight, attended = lax.cond(
        prefill_side, route, attend,
        payload, spread, cosine, sine, new_keys, new_values, *arrived_weights,
    )
    out_weight = lax.ppermute(out_weight, "role", [(0, 1)])
    pool = lax.ppermute(pool, "role", [(0, 1)])

    def gather(attended):
        return lax.all_to_all(attended, "z", split_axis=0, concat_axis=0, tiled=True)

    attended = lax.cond(prefill_side, lambda attended: attended, gather, attended)

    def finish(attended, out_weight):
        partial = lax.dot_general(
            attended.reshape(Z * rows, local_query),
            out_weight,
            (((1,), (1,)), ((), ())),
            preferred_element_type=F32,
        ).astype(BF16)
        back = lax.all_to_all(
            partial.reshape(Z, rows, chunk), "z", split_axis=0, concat_axis=0, tiled=True
        )
        tp_count = lax.axis_size("tp")
        delta = back.astype(F32)
        for shift in range(1, tp_count):
            pairs = [(i, (i + shift) % tp_count) for i in range(tp_count)]
            delta = delta + lax.ppermute(back, "tp", pairs).astype(F32)
        delta = delta.transpose(1, 0, 2).reshape(steps, requests, width)
        return (decode_hidden.astype(F32) + delta).astype(BF16)[None]

    def idle_finish(attended, out_weight):
        return jnp.zeros((1, steps, requests, width), BF16)

    decoded = lax.cond(prefill_side, idle_finish, finish, attended, out_weight)
    return jnp.where(prefill_side, span_kv, pool)[None], decoded


def solution(mesh):
    shape = mesh.devices.shape
    fine = Mesh(mesh.devices.reshape(shape[0], Z, Y, shape[2]), ("role", "z", "y", "tp"))
    placed = (
        P("role", SEQ, None),
        P(),
        P(None, None, "tp"),
        P(),
        P(),
        P(SEQ, "tp"),
        P("tp", SEQ),
        P(None, SEQ, None),
        P(SEQ, None, None, "tp"),
        P(SEQ),
        P(),
        P(),
    )
    return jax.shard_map(
        shards,
        mesh=fine,
        in_specs=placed,
        out_specs=(P("role", SEQ, None, "tp"), P("role", None, SEQ, None)),
        check_vma=False,
    )
```

time: 129 us -> 90.3 us (0.70)
  waiting for transfers between devices: 49.4 us -> 20.9 us
  local copies, waits for them, and re-layouts: 11.6 us -> 3.49 us
  Pallas kernels: 0 us -> 5.25 us
  matrix products: 8.62 us -> 4.31 us
  other arithmetic: 5.35 us -> 3.9 us
  starting transfers between devices: 26.7 us -> 25.3 us
    all_to_all x4 -> x2, waiting for transfers between devices: 44 us -> 14.5 us  [the longest x1 11 us: attend(): lax.all_to_all(partial.reshape(exchanged), 'z', split_axis=0, concat_axis...]
    all_to_all x4 -> x2, starting transfers between devices: 20.6 us -> 15.1 us  [the longest x1 9.02 us: project(): lax.all_to_all(spread, 'z', split_axis=0, concat_axis=0, tiled=True)]
    pallas_call x0 -> x3, Pallas kernels: none -> 5.25 us  [the longest x1 1.94 us: project(): pl.pallas_call(norm_kernel, out_shape=(jax.ShapeDtypeStruct((Z, rows, chu...]
    dot_general x14 -> x2, matrix products: 8.62 us -> 4.31 us  [the longest x1 3.38 us: project(): jnp.einsum('rd,dcw->crw', normed, kv_weight, preferred_element_type=F32)]
    ppermute x4 -> x8, starting transfers between devices: 6.12 us -> 10.2 us  [the longest x3 3.88 us: shards(): arrived_weights.append(lax.ppermute(q_weight, ('role', 'y'), pairs))]
    broadcast_in_dim x3 -> x0, local copies, waits for them, and re-layouts: 3.71 us -> none  [the longest x1 1.83 us: decode(): jnp.broadcast_to(o_weight[None], (Y,) + o_weight.shape)]
    convert_element_type x3 -> x1, local copies, waits for them, and re-layouts: 2.5 us -> 0.01 us  [project(): new_values = fresh[1].astype(BF16)]
    broadcast_in_dim x1 -> x2, other arithmetic: 0.09 us -> 2.02 us  [the longest x1 1.93 us: shards(): return (jnp.where(prefill_side, span_kv, pool)[None], decoded)]
  transfers between devices with their start and end apart: 8 -> 10, of which waited for: 7 -> 5; matrix products, arithmetic and copies ran while one was open for 11% -> 10% of each run, Pallas kernels for 0% -> 2%
where the time goes in v2:
time: 90.3 us; the launch traced here: 89.5 us
  starting transfers between devices  25.3 us (28%)
  blocking collectives  25.2 us (28%)
  waiting for transfers between devices  20.9 us (23%)
  Pallas kernels  5.25 us (6%)
  matrix products  4.31 us (5%)
  other arithmetic  3.9 us (4%)
  local copies, waits for them, and re-layouts  3.49 us (4%)
    all_to_all x1, blocking collectives, gather(): lax.all_to_all(attended, 'z', split_axis=0, concat_axis=0, tiled=True)  14.5 us
    all_to_all x1, waiting for transfers between devices, attend(): lax.all_to_all(partial.reshape(exchanged), 'z', split_axis=0, concat_axis...  11 us
    all_to_all x1, blocking collectives, finish(): lax.all_to_all(partial.reshape(Z, rows, chunk), 'z', split_axis=0, concat...  10.7 us
    all_to_all x1, starting transfers between devices, project(): lax.all_to_all(spread, 'z', split_axis=0, concat_axis=0, tiled=True)  9.02 us
    ppermute x3, waiting for transfers between devices, finish(): delta = delta + lax.ppermute(back, 'tp', pairs).astype(F32)  6.31 us
    all_to_all x1, starting transfers between devices, attend(): lax.all_to_all(partial.reshape(exchanged), 'z', split_axis=0, concat_axis...  6.11 us
    ppermute x3, starting transfers between devices, shards(): arrived_weights.append(lax.ppermute(q_weight, ('role', 'y'), pairs))  3.88 us
    ppermute x3, starting transfers between devices, finish(): delta = delta + lax.ppermute(back, 'tp', pairs).astype(F32)  3.61 us
  transfers between devices with their start and end apart: 10, of which 5 were waited for; matrix products, arithmetic and copies ran while one was open for 10% of the time, Pallas kernels for 2%

profile of v2, /device:TPU:1, one launch (start us, length us, event | category | flops | bytes accessed | tf_op | source)
XLA Modules:
  0.0 89.5 jit_solution(147956003708014014)
XLA Ops:
  0.6 1.3 %collective-permute-start.6 = (bf16[160,2048]{1,0:T(8,128)(2,1)}, bf16[160,2048]{1,0:T(8,128)(2,1)S(1)}, u32[]{:S(2)}, u32[]{:S(2)}) collective-permute-start(bf16[160,2048]{1,0:T(8,128)(2,1)} %param.25), channel_id=1, source_target_pairs={{0,140},{4,128},{8,132},{12,136},{1,141},{5,129},{9,133},{13,137},... | collective-permute-start | bytes 1966088 | tf_op jit(solution)/shard_map/ppermute | solution.py:247
  1.9 1.3 %collective-permute-start.7 = (bf16[160,2048]{1,0:T(8,128)(2,1)}, bf16[160,2048]{1,0:T(8,128)(2,1)S(1)}, u32[]{:S(2)}, u32[]{:S(2)}) collective-permute-start(bf16[160,2048]{1,0:T(8,128)(2,1)} %param.25), channel_id=1, source_target_pairs={{0,136},{4,140},{8,128},{12,132},{1,137},{5,141},{9,129},{13,133},... | collective-permute-start | bytes 1966088 | tf_op jit(solution)/shard_map/ppermute | solution.py:247
  3.2 1.3 %collective-permute-start.8 = (bf16[160,2048]{1,0:T(8,128)(2,1)}, bf16[160,2048]{1,0:T(8,128)(2,1)S(1)}, u32[]{:S(2)}, u32[]{:S(2)}) collective-permute-start(bf16[160,2048]{1,0:T(8,128)(2,1)} %param.25), channel_id=1, source_target_pairs={{0,132},{4,136},{8,140},{12,128},{1,133},{5,137},{9,141},{13,129},... | collective-permute-start | bytes 1966088 | tf_op jit(solution)/shard_map/ppermute | solution.py:247
  4.5 0.6 and_select_fusion
  5.1 0.6 iota.70
  5.7 0.0 copy-start.1
  5.7 19.2 %conditional.4 = (bf16[128,640]{1,0:T(8,128)(2,1)S(1)}, f32[16,128]{1,0:T(8,128)S(1)}, f32[16,128]{1,0:T(8,128)S(1)}, bf16[16,256]{1,0:T(8,128)(2,1)S(1)}, bf16[...) conditional(s32[]{:T(128)} %convert_element_type.77, (s32[]{:T(128)}, ...), branch_computations={%region_0.2_spmd, %region_2.6_spmd} | conditional | flops 1487554176 | bytes 26235656 | solution.py:278
  5.7 1.9 %branch_0_fun.3 = (bf16[8,16,640]{2,1,0:T(8,128)(2,1)}, bf16[16,5120]{1,0:T(8,128)(2,1)}, bf16[256,2,256]{2,1,0:T(2,128)(2,1)S(1)}, bf16[32,16,512]{2,1,0:T(8,128)(2,1)}) custom-call(s32[1]{0:T(128)} %bitcast.y_ref, bf16[4,4,5120]{2,1,0:T(4,128)(2,1)} %get-tuple-element.83.hidden_ref, f32[1,5120]{1,0:T(1,128)} %bitcast.83), custom_call_target="tpu_custom_call" | custom-call | tf_op jit(solution)/shard_map/cond/branch_0_fun/pallas_call | solution.py:250
  7.7 9.0 %all-to-all-start.1 = ((bf16[8,16,640]{2,1,0:T(8,128)(2,1)}), bf16[8,16,640]{2,1,0:T(8,128)(2,1)S(1)}, u32[]{:S(2)}, u32[]{:S(2)}) async-start(bf16[8,16,640]{2,1,0:T(8,128)(2,1)} %get-tuple-element.85), calls=%async_computation.1 | async-start | bytes 327680 | tf_op jit(solution)/shard_map/cond/branch_0_fun/all_to_all | solution.py:265
  16.7 0.7 add_convert_fusion.1
  17.3 0.1 convert_element_type.58
  17.4 0.0 copy-start.14
  17.4 3.4 %fusion.2 = f32[2,16,256]{2,1,0:T(8,128)S(1)} fusion(bf16[5120,2,256]{2,1,0:T(2,128)(2,1)} %get-tuple-element.284, bf16[16,5120]{1,0:T(8,128)(2,1)} %get-tuple-element.87), kind=kOutput, calls=%fused_computation.2 | convolution fusion | flops 83886080 | bytes 5439488 | tf_op jit(solution)/shard_map/cond/branch_0_fun/rd,dcw->crw/dot_general | solution.py:270
  20.8 0.1 multiply_reduce_fusion
  21.0 0.1 fusion.7
  21.1 0.0 copy-done.14
  21.1 0.1 multiply_multiply_fusion
  21.2 0.1 subtract_convert_fusion
  21.3 0.1 pad_maximum_fusion.2
  21.4 0.1 pad_maximum_fusion
  21.5 3.5 %all-to-all-done.1 = bf16[8,16,640]{2,1,0:T(8,128)(2,1)S(1)} async-done(((bf16[8,16,640]{2,1,0:T(8,128)(2,1)}), bf16[8,16,640]{2,1,0:T(8,128)(2,1)S(1)}, u32[]{:S(2)}, u32[]{:S(2)}) %all-to-all-start.1) | async-done | bytes 163872 | tf_op jit(solution)/shard_map/cond/branch_0_fun/all_to_all | solution.py:265
  25.0 0.0 collective-permute-done.6
  25.0 0.0 collective-permute-done.7
  25.0 0.0 collective-permute-done.8
  25.0 0.0 copy-done.1
  25.0 0.7 copy-done.5
  25.7 21.9 %conditional.5 = (bf16[256,2,256]{2,1,0:T(2,128)(2,1)}, bf16[640,2048]{1,0:T(8,128)(2,1)}, bf16[8,16,2048]{2,1,0:T(8,128)(2,1)S(1)}) conditional(s32[]{:T(128)} %convert_element_type.77, (bf16[128,640]{1,0:T(8,128)(2,1)S(1)}, bf16[160,2048]{1,0:T(8,128)(2,1)S(1)}, bf16[160,2048]{1,0:T(8,128)(2,1)S(1)}, bf16[160,2048]{1,0:T(8,128)(2,1)S(1)}, ...), branch_computations={%region_6.7_spmd, %region_7.10_spmd} | conditional | flops 134712608 | bytes 21811618 | solution.py:317
  25.7 0.0 copy-start.13
  25.7 0.0 copy-start.17
  25.7 1.4 %branch_0_fun.4 = bf16[128,2048]{1,0:T(8,128)(2,1)} custom-call(bf16[128,640]{1,0:T(8,128)(2,1)S(1)} %get-tuple-element.101.rows_ref, bf16[160,2048]{1,0:T(8,128)(2,1)S(1)} %get-tuple-element.102.own_ref, bf16[160,2048]{1,0:T(8,128)(2,1)S(1)} %get-tuple-element.103.first_ref, bf16[160,2048]{1,0:T(8,128)(2,1)S(1)} %get-tuple-element.104.second_ref, ...), custom_call_target="tpu_custom_call" | custom-call | tf_op jit(solution)/shard_map/cond/branch_0_fun/pallas_call | solution.py:283
  27.1 6.1 %all-to-all-start.2 = ((bf16[8,16,2048]{2,1,0:T(8,128)(2,1)}), bf16[8,16,2048]{2,1,0:T(8,128)(2,1)S(1)}, u32[]{:S(2)}, u32[]{:S(2)}) async-start(bf16[8,16,2048]{2,1,0:T(8,128)(2,1)} %bitcast.17), calls=%async_computation.2 | async-start | bytes 1048576 | tf_op jit(solution)/shard_map/cond/branch_0_fun/all_to_all | solution.py:290
  33.2 0.0 copy-done.7
  33.2 0.0 copy-done.8
  33.2 0.0 copy-done.9
  33.2 0.0 copy-done.10
  33.2 1.1 %copy.51 = bf16[4,128,2,256]{3,1,0,2:T(8,128)(2,1)S(1)} copy(bf16[4,128,2,256]{3,2,1,0:T(2,128)(2,1)} %get-tuple-element.300) | data formatting | bytes 1048576 | tf_op jit(solution)/shard_map
  34.4 11.0 %all-to-all-done.2.returned_ref = bf16[8,16,2048]{2,1,0:T(8,128)(2,1)S(1)} async-done(((bf16[8,16,2048]{2,1,0:T(8,128)(2,1)}), bf16[8,16,2048]{2,1,0:T(8,128)(2,1)S(1)}, u32[]{:S(2)}, u32[]{:S(2)}) %all-to-all-start.2) | async-done | bytes 524320 | tf_op jit(solution)/shard_map/cond/branch_0_fun/all_to_all | solution.py:290
  45.4 0.0 copy-done.13
  45.4 0.0 copy-done.17
  45.4 1.9 %branch_0_fun.5 = (bf16[8,16,2048]{2,1,0:T(8,128)(2,1)S(1)}, bf16[256,2,256]{2,1,0:T(2,128)(2,1)}, bf16[640,2048]{1,0:T(8,128)(2,1)}) custom-call(s32[4]{0:T(128)S(1)} %copy-done.13, bf16[8,16,2048]{2,1,0:T(8,128)(2,1)S(1)} %all-to-all-done.2.returned_ref, f32[1,128]{1,0:T(1,128)S(1)} %bitcast.84, f32[16,128]{1,0:T(8,128)} %copy-done.7, ...), custom_call_target="tpu_custom_call" | custom-call | tf_op jit(solution)/shard_map/cond/branch_0_fun/pallas_call | solution.py:294
  47.6 0.0 copy-start.2
  47.6 1.4 %collective-permute-start.10 = (bf16[640,2048]{1,0:T(8,128)(2,1)}, bf16[640,2048]{1,0:T(8,128)(2,1)S(1)}, u32[]{:S(2)}, u32[]{:S(2)}) collective-permute-start(bf16[640,2048]{1,0:T(8,128)(2,1)} %get-tuple-element.147), channel_id=1, source_target_pairs={{0,128},{1,129},{2,130},{3,131},{4,132},{5,133},{6,134},{7,135},{8... | collective-permute-start | bytes 7864328 | tf_op jit(solution)/shard_map/ppermute | solution.py:321
  49.0 1.3 %collective-permute-start.9 = (bf16[256,2,256]{2,1,0:T(2,128)(2,1)}, bf16[256,2,256]{2,1,0:T(2,128)(2,1)}, u32[]{:S(2)}, u32[]{:S(2)}) collective-permute-start(bf16[256,2,256]{2,1,0:T(2,128)(2,1)} %get-tuple-element.145), channel_id=1, source_target_pairs={{0,128},{1,129},{2,130},{3,131},{4,132},{5,133},{6,134},{7,135},{8... | collective-permute-start | bytes 786440 | tf_op jit(solution)/shard_map/ppermute | solution.py:322
  50.3 14.6 %conditional.6 = (bf16[8,16,2048]{2,1,0:T(8,128)(2,1)S(1)}) conditional(s32[]{:T(128)} %convert_element_type.77, bf16[8,16,2048]{2,1,0:T(8,128)(2,1)S(1)} %get-tuple-element.146, bf16[8,16,2048]{2,1,0:T(8,128)(2,1)S(1)} %get-tuple-element.146), branch_computations={%region_10.11_spmd, %region_11.12_spmd} | conditional | bytes 2097160 | solution.py:327
  50.4 14.5 %all_to_all.20 = bf16[8,16,2048]{2,1,0:T(8,128)(2,1)S(1)} all-to-all(bf16[8,16,2048]{2,1,0:T(8,128)(2,1)S(1)} %copy.94), channel_id=1, replica_groups=mesh['role'=2,'z'=8,'y'=4,'tp'=4] {'z'}, dimensions={0} | all-to-all | bytes 1048576 | tf_op jit(solution)/shard_map/cond/branch_0_fun/all_to_all | solution.py:325
  64.9 0.0 collective-permute-done.9
  64.9 1.9 %fusion.36 = bf16[1,256,2,256]{3,2,1,0:T(2,128)(2,1)} fusion(bf16[256,2,256]{2,1,0:T(2,128)(2,1)} %copy-done.5, bf16[256,2,256]{2,1,0:T(2,128)(2,1)} %collective-permute-done.9, pred[]{:T(512)S(6)} %eq.52), kind=kLoop, calls=%fused_computation.79 | loop fusion | flops 131072 | bytes 786433 | tf_op jit(solution)/shard_map/broadcast_in_dim | solution.py:351
  66.8 0.0 collective-permute-done.10
  66.8 0.0 copy-done.2
  66.8 21.9 %conditional.7 = (bf16[1,4,4,5120]{3,2,1,0:T(4,128)(2,1)S(1)}) conditional(s32[]{:T(128)} %convert_element_type.77, (bf16[4,4,5120]{2,1,0:T(4,128)(2,1)S(1)}, bf16[8,16,2048]{2,1,0:T(8,128)(2,1)S(1)}, bf16[640,2048]{1,0:T(8,128)(2,1)S(1)}) %tuple.80, () %tuple.41), branch_computations={%region_12.13_spmd, %region_13.14_spmd} | conditional | flops 336445440 | bytes 8552576 | solution.py:350
  66.9 0.9 %convolution_convert_fusion.2 = bf16[128,640]{1,0:T(8,128)(2,1)S(1)} fusion(bf16[128,2048]{1,0:T(8,128)(2,1)S(1)} %bitcast.71, bf16[640,2048]{1,0:T(8,128)(2,1)S(1)} %get-tuple-element.125), kind=kOutput, calls=%fused_computation.74 | convolution fusion | flops 335626240 | bytes 3309568 | tf_op jit(solution)/shard_map/cond/branch_0_fun/dot_general | solution.py:330
  67.8 10.7 %all_to_all.21 = bf16[8,16,640]{2,1,0:T(8,128)(2,1)S(1)} all-to-all(bf16[8,16,640]{2,1,0:T(8,128)(2,1)S(1)} %bitcast.73), channel_id=1, replica_groups=mesh['role'=2,'z'=8,'y'=4,'tp'=4] {'z'}, dimensions={0} | all-to-all | bytes 327680 | tf_op jit(solution)/shard_map/cond/branch_0_fun/all_to_all | solution.py:336
  78.4 2.5 %collective-permute-start.5 = (bf16[8,16,640]{2,1,0:T(8,128)(2,1)S(1)}, bf16[8,16,640]{2,1,0:T(8,128)(2,1)S(1)}, u32[]{:S(2)}, u32[]{:S(2)}) collective-permute-start(bf16[8,16,640]{2,1,0:T(8,128)(2,1)S(1)} %all_to_all.21), channel_id=1, source_target_pairs={{0,3},{1,0},{2,1},{3,2},{4,7},{5,4},{6,5},{7,6},{8,11},{9,8},{10,9... | collective-permute-start | bytes 491528 | tf_op jit(solution)/shard_map/cond/branch_0_fun/ppermute | solution.py:343
  80.9 0.5 collective-permute-start.4
  81.4 0.6 collective-permute-start.3
  82.1 2.9 %collective-permute-done.5 = bf16[8,16,640]{2,1,0:T(8,128)(2,1)S(1)} collective-permute-done((bf16[8,16,640]{2,1,0:T(8,128)(2,1)S(1)}, bf16[8,16,640]{2,1,0:T(8,128)(2,1)S(1)}, u32[]{:S(2)}, u32[]{:S(2)}) %collective-permute-start.5) | collective-permute-done | bytes 163872 | tf_op jit(solution)/shard_map/cond/branch_0_fun/ppermute | solution.py:343
  85.0 1.8 %collective-permute-done.4 = bf16[8,16,640]{2,1,0:T(8,128)(2,1)S(1)} collective-permute-done((bf16[8,16,640]{2,1,0:T(8,128)(2,1)S(1)}, bf16[8,16,640]{2,1,0:T(8,128)(2,1)S(1)}, u32[]{:S(2)}, u32[]{:S(2)}) %collective-permute-start.4) | collective-permute-done | bytes 163872 | tf_op jit(solution)/shard_map/cond/branch_0_fun/ppermute | solution.py:343
  86.7 1.7 %collective-permute-done.3 = bf16[8,16,640]{2,1,0:T(8,128)(2,1)S(1)} collective-permute-done((bf16[8,16,640]{2,1,0:T(8,128)(2,1)S(1)}, bf16[8,16,640]{2,1,0:T(8,128)(2,1)S(1)}, u32[]{:S(2)}, u32[]{:S(2)}) %collective-permute-start.3) | collective-permute-done | bytes 163872 | tf_op jit(solution)/shard_map/cond/branch_0_fun/ppermute | solution.py:343
  88.4 0.1 add_bitcast_fusion
  88.5 0.1 copy.48
  88.6 0.1 reshape.277
  88.7 0.1 fusion.35
  88.8 0.0 copy-start.6
  88.8 0.7 copy-done.6
  (14 shorter events, 0.1 us)
Async XLA Ops:
  0.6 24.3 %collective-permute-start.6 = (bf16[160,2048]{1,0:T(8,128)(2,1)}, bf16[160,2048]{1,0:T(8,128)(2,1)S(1)}, u32[]{:S(2)}, u32[]{:S(2)}) collective-permute-start(bf16[160,2048]{1,0:T(8,128)(2,1)} %param.25), channel_id=1, source_target_pairs={{0,140},{4,128},{8,132},{12,136},{1,141},{5,129},{9,133},{13,137},... | collective-permute-start | bytes 1966088 | tf_op jit(solution)/shard_map/ppermute | solution.py:247
  1.9 23.0 %collective-permute-start.7 = (bf16[160,2048]{1,0:T(8,128)(2,1)}, bf16[160,2048]{1,0:T(8,128)(2,1)S(1)}, u32[]{:S(2)}, u32[]{:S(2)}) collective-permute-start(bf16[160,2048]{1,0:T(8,128)(2,1)} %param.25), channel_id=1, source_target_pairs={{0,136},{4,140},{8,128},{12,132},{1,137},{5,141},{9,129},{13,133},... | collective-permute-start | bytes 1966088 | tf_op jit(solution)/shard_map/ppermute | solution.py:247
  3.2 21.8 %collective-permute-start.8 = (bf16[160,2048]{1,0:T(8,128)(2,1)}, bf16[160,2048]{1,0:T(8,128)(2,1)S(1)}, u32[]{:S(2)}, u32[]{:S(2)}) collective-permute-start(bf16[160,2048]{1,0:T(8,128)(2,1)} %param.25), channel_id=1, source_target_pairs={{0,132},{4,136},{8,140},{12,128},{1,133},{5,137},{9,141},{13,129},... | collective-permute-start | bytes 1966088 | tf_op jit(solution)/shard_map/ppermute | solution.py:247
  5.7 19.3 %copy-start.1 = (bf16[160,2048]{1,0:T(8,128)(2,1)S(1)}, bf16[160,2048]{1,0:T(8,128)(2,1)}, u32[]{:S(2)}) copy-start(bf16[160,2048]{1,0:T(8,128)(2,1)} %param.25) | copy-start | bytes 1966084
  7.7 17.3 %all-to-all-start.1 = ((bf16[8,16,640]{2,1,0:T(8,128)(2,1)}), bf16[8,16,640]{2,1,0:T(8,128)(2,1)S(1)}, u32[]{:S(2)}, u32[]{:S(2)}) async-start(bf16[8,16,640]{2,1,0:T(8,128)(2,1)} %get-tuple-element.85), calls=%async_computation.1 | async-start | bytes 327680 | tf_op jit(solution)/shard_map/cond/branch_0_fun/all_to_all | solution.py:265
  17.4 3.6 %copy-start.14 = (f32[128]{0:T(128)S(1)}, f32[128]{0:T(128)}, u32[]{:S(2)}) copy-start(f32[128]{0:T(128)} %get-tuple-element.89) | copy-start | bytes 1540 | tf_op jit(solution)/shard_map/cond
  25.0 0.7 copy-start.5
  25.7 7.5 %copy-start.7 = (f32[16,128]{1,0:T(8,128)}, f32[16,128]{1,0:T(8,128)S(1)}, u32[]{:S(2)}) copy-start(f32[16,128]{1,0:T(8,128)S(1)} %get-tuple-element.107.cosine_ref) | copy-start | bytes 24580 | tf_op jit(solution)/shard_map/cond
  25.7 7.5 %copy-start.8 = (f32[16,128]{1,0:T(8,128)}, f32[16,128]{1,0:T(8,128)S(1)}, u32[]{:S(2)}) copy-start(f32[16,128]{1,0:T(8,128)S(1)} %get-tuple-element.108.sine_ref) | copy-start | bytes 24580 | tf_op jit(solution)/shard_map/cond
  25.7 7.5 %copy-start.9 = (bf16[16,256]{1,0:T(8,128)(2,1)}, bf16[16,256]{1,0:T(8,128)(2,1)S(1)}, u32[]{:S(2)}) copy-start(bf16[16,256]{1,0:T(8,128)(2,1)S(1)} %get-tuple-element.110.new_keys_ref) | copy-start | bytes 24580 | tf_op jit(solution)/shard_map/cond
  25.7 7.5 %copy-start.10 = (bf16[16,256]{1,0:T(8,128)(2,1)}, bf16[16,256]{1,0:T(8,128)(2,1)S(1)}, u32[]{:S(2)}) copy-start(bf16[16,256]{1,0:T(8,128)(2,1)S(1)} %get-tuple-element.111.new_values_ref) | copy-start | bytes 24580 | tf_op jit(solution)/shard_map/cond
  25.7 19.8 %copy-start.13 = (s32[4]{0:T(128)S(1)}, s32[4]{0:T(128)}, u32[]{:S(2)}) copy-start(s32[4]{0:T(128)} %get-tuple-element.100.length_ref) | copy-start | bytes 52 | tf_op jit(solution)/shard_map/cond
  25.7 19.8 %copy-start.17 = (f32[128]{0:T(128)S(1)}, f32[128]{0:T(128)}, u32[]{:S(2)}) copy-start(f32[128]{0:T(128)} %get-tuple-element.152) | copy-start | bytes 1540 | tf_op jit(solution)/shard_map/cond
  27.1 18.4 %all-to-all-start.2 = ((bf16[8,16,2048]{2,1,0:T(8,128)(2,1)}), bf16[8,16,2048]{2,1,0:T(8,128)(2,1)S(1)}, u32[]{:S(2)}, u32[]{:S(2)}) async-start(bf16[8,16,2048]{2,1,0:T(8,128)(2,1)} %bitcast.17), calls=%async_computation.2 | async-start | bytes 1048576 | tf_op jit(solution)/shard_map/cond/branch_0_fun/all_to_all | solution.py:290
  47.6 19.3 %copy-start.2 = (bf16[4,4,5120]{2,1,0:T(4,128)(2,1)S(1)}, bf16[4,4,5120]{2,1,0:T(4,128)(2,1)}, u32[]{:S(2)}) copy-start(bf16[4,4,5120]{2,1,0:T(4,128)(2,1)} %param.27) | copy-start | bytes 491524
  47.6 19.3 %collective-permute-start.10 = (bf16[640,2048]{1,0:T(8,128)(2,1)}, bf16[640,2048]{1,0:T(8,128)(2,1)S(1)}, u32[]{:S(2)}, u32[]{:S(2)}) collective-permute-start(bf16[640,2048]{1,0:T(8,128)(2,1)} %get-tuple-element.147), channel_id=1, source_target_pairs={{0,128},{1,129},{2,130},{3,131},{4,132},{5,133},{6,134},{7,135},{8... | collective-permute-start | bytes 7864328 | tf_op jit(solution)/shard_map/ppermute | solution.py:321
  49.0 15.9 %collective-permute-start.9 = (bf16[256,2,256]{2,1,0:T(2,128)(2,1)}, bf16[256,2,256]{2,1,0:T(2,128)(2,1)}, u32[]{:S(2)}, u32[]{:S(2)}) collective-permute-start(bf16[256,2,256]{2,1,0:T(2,128)(2,1)} %get-tuple-element.145), channel_id=1, source_target_pairs={{0,128},{1,129},{2,130},{3,131},{4,132},{5,133},{6,134},{7,135},{8... | collective-permute-start | bytes 786440 | tf_op jit(solution)/shard_map/ppermute | solution.py:322
  78.4 6.5 %collective-permute-start.5 = (bf16[8,16,640]{2,1,0:T(8,128)(2,1)S(1)}, bf16[8,16,640]{2,1,0:T(8,128)(2,1)S(1)}, u32[]{:S(2)}, u32[]{:S(2)}) collective-permute-start(bf16[8,16,640]{2,1,0:T(8,128)(2,1)S(1)} %all_to_all.21), channel_id=1, source_target_pairs={{0,3},{1,0},{2,1},{3,2},{4,7},{5,4},{6,5},{7,6},{8,11},{9,8},{10,9... | collective-permute-start | bytes 491528 | tf_op jit(solution)/shard_map/cond/branch_0_fun/ppermute | solution.py:343
  80.9 5.8 %collective-permute-start.4 = (bf16[8,16,640]{2,1,0:T(8,128)(2,1)S(1)}, bf16[8,16,640]{2,1,0:T(8,128)(2,1)S(1)}, u32[]{:S(2)}, u32[]{:S(2)}) collective-permute-start(bf16[8,16,640]{2,1,0:T(8,128)(2,1)S(1)} %all_to_all.21), channel_id=1, source_target_pairs={{0,2},{1,3},{2,0},{3,1},{4,6},{5,7},{6,4},{7,5},{8,10},{9,11},{10,... | collective-permute-start | bytes 491528 | tf_op jit(solution)/shard_map/cond/branch_0_fun/ppermute | solution.py:343
  81.4 6.9 %collective-permute-start.3 = (bf16[8,16,640]{2,1,0:T(8,128)(2,1)S(1)}, bf16[8,16,640]{2,1,0:T(8,128)(2,1)S(1)}, u32[]{:S(2)}, u32[]{:S(2)}) collective-permute-start(bf16[8,16,640]{2,1,0:T(8,128)(2,1)S(1)} %all_to_all.21), channel_id=1, source_target_pairs={{0,1},{1,2},{2,3},{3,0},{4,5},{5,6},{6,7},{7,4},{8,9},{9,10},{10,1... | collective-permute-start | bytes 491528 | tf_op jit(solution)/shard_map/cond/branch_0_fun/ppermute | solution.py:343
  88.8 0.7 copy-start.6

commit v3 on v2

--- a/solution.py
+++ b/solution.py
@@ -149,6 +149,51 @@
             block = mixed[one * rows : (one + 1) * rows]
             for z in range(Z):
                 out_ref[z, :, part * HEAD_SIZE : (part + 1) * HEAD_SIZE] = block
+
+
+def copy_kernel(source_ref, out_ref):
+    out_ref[0] = source_ref[...]
+
+
+def packed(pool, width):
+    sides = width // pool.shape[1]
+    run = pool.shape[0] // sides
+    return jnp.concatenate([pool[i * run : (i + 1) * run] for i in range(sides)], axis=1)
+
+
+def base_kernel(hidden_ref, back_ref, out_ref):
+    chunk = back_ref.shape[2]
+    for z in range(Z):
+        columns = slice(z * chunk, (z + 1) * chunk)
+        hidden = jnp.concatenate(
+            [hidden_ref[step, :, columns].astype(F32) for step in range(hidden_ref.shape[0])],
+            axis=0,
+        )
+        out_ref[z] = hidden + back_ref[z].astype(F32)
+
+
+def sum_kernel(base_ref, first_ref, second_ref, third_ref, out_ref):
+    steps, requests = out_ref.shape[1:3]
+    chunk = base_ref.shape[2]
+    for z in range(Z):
+        total = base_ref[z] + (
+            first_ref[z].astype(F32) + second_ref[z].astype(F32) + third_ref[z].astype(F32)
+        )
+        total = total.astype(BF16)
+        for step in range(steps):
+            out_ref[0, step, :, z * chunk : (z + 1) * chunk] = total[
+                step * requests : (step + 1) * requests
+            ]
+
+
+def unpack_kernel(handed_ref, out_ref):
+    tokens, sections, width = out_ref.shape[1:]
+    sides = handed_ref.shape[1] // (sections * width)
+    run = tokens // sides
+    for i in range(sides):
+        for section in range(sections):
+            start = (i * sections + section) * width
+            out_ref[0, i * run : (i + 1) * run, section, :] = handed_ref[:, start : start + width]
 
 
 def shards(
@@ -178,6 +223,7 @@
     buffer_tokens = seq_count * CAPACITY * BLOCK_TOKENS
     chunk = width // Z
     context = cache.shape[1]
+    slots = requests * context
     exchanged = (Z, rows, local_query)
 
     whole = pl.BlockSpec(memory_space=pltpu.VMEM)
@@ -191,8 +237,14 @@
         earlier = block_number[None, None, :] < block_number[None, :, None]
         return jnp.sum(jnp.logical_and(same_owner, earlier).astype(jnp.int32), axis=2)
 
-    token = jnp.arange(span_rows, dtype=jnp.int32) % BLOCK_TOKENS
-    place = jnp.arange(buffer_tokens, dtype=jnp.int32)
+    pool_rows = span_rows * 2 * local_width // out_depth
+    handed_over = jax.ShapeDtypeStruct((Y * out_width + pool_rows, out_depth), BF16)
+
+    def one_hot(blocks):
+        token = lax.broadcasted_iota(jnp.int32, (block_count, BLOCK_TOKENS), 1)
+        at = (blocks[:, None] * BLOCK_TOKENS + token).reshape(1, span_rows)
+        place = lax.broadcasted_iota(jnp.int32, (buffer_tokens, span_rows), 0)
+        return (place == at).astype(BF16)
 
     def prefill(*_):
         normed = row_scaling(span_hidden[0].astype(F32), attn_gain).astype(BF16)
@@ -202,28 +254,28 @@
         span_kv = jnp.concatenate([keys, projected[1]], axis=1).astype(BF16)
         own_owner = lax.dynamic_index_in_dim(block_owner, seq_index, 0, keepdims=False)
         own_rank = lax.dynamic_index_in_dim(rank_table(), seq_index, 0, keepdims=False)
-        sent_to = jnp.repeat(own_owner * CAPACITY + own_rank, BLOCK_TOKENS) * BLOCK_TOKENS + token
-        spread = (place[:, None] == sent_to[None, :]).astype(BF16)
-        payload = dot(spread, span_kv).astype(BF16)
+        payload = dot(one_hot(own_owner * CAPACITY + own_rank), span_kv).astype(BF16)
         return (
             jnp.zeros((Z * rows, chunk), BF16),
             jnp.zeros((rows, HEAD_SIZE), F32),
             jnp.zeros((rows, HEAD_SIZE), F32),
             jnp.zeros((rows, local_width), BF16),
             jnp.zeros((rows, local_width), BF16),
+            jnp.zeros((slots, local_width), BF16),
+            jnp.zeros((slots, local_width), BF16),
             span_kv.reshape(section.shape),
             payload.reshape(buffer.shape),
         )
 
     def route(payload, *_):
         turned = o_weight.T
-        out_weight = jnp.zeros((Y, out_width, out_depth), BF16)
+        handed = jnp.zeros(handed_over.shape, BF16)
         for shift in range(Y):
             part = turned
             if shift > 0:
                 part = lax.ppermute(turned, "y", [(i, (i - shift) % Y) for i in range(Y)])
-            out_weight = lax.dynamic_update_index_in_dim(
-                out_weight, part, lax.rem(y_index + shift, Y), 0
+            handed = lax.dynamic_update_slice(
+                handed, part, (lax.rem(y_index + shift, Y) * out_width, 0)
             )
         arrived = lax.all_to_all(payload, SEQ, split_axis=0, concat_axis=0, tiled=True)
         block_number = jnp.arange(block_count, dtype=jnp.int32)
@@ -232,18 +284,18 @@
         source = jnp.sum(
             jnp.where(target[None] == block_number[:, None, None], came_as[None], 0), axis=(1, 2)
         )
-        taken_from = jnp.repeat(source, BLOCK_TOKENS) * BLOCK_TOKENS + token
-        gather = (taken_from[:, None] == place[None, :]).astype(BF16)
-        pool = dot(gather, arrived.reshape(buffer_tokens, 2 * local_width)).astype(BF16)
-        return (
-            pool.reshape(section.shape),
-            out_weight.reshape(Y * out_width, out_depth),
-            jnp.zeros(exchanged, BF16),
-        )
+        pool = lax.dot_general(
+            one_hot(source),
+            arrived.reshape(buffer_tokens, 2 * local_width),
+            (((0,), (0,)), ((), ())),
+            preferred_element_type=F32,
+        ).astype(BF16)
+        handed = lax.dynamic_update_slice(handed, packed(pool, out_depth), (Y * out_width, 0))
+        return handed, jnp.zeros(exchanged, BF16)
 
     arrived_weights = []
     for shift in range(1, Y):
-        pairs = [(i, Y + (i - shift) % Y) for i in range(Y)]
+        pairs = [(i, Y + (i - shift) % Y) for i in range(Y)] + [(Y + i, i) for i in range(Y)]
         arrived_weights.append(lax.ppermute(q_weight, ("role", "y"), pairs))
 
     def project(*_):
@@ -273,13 +325,13 @@
         cosine = jnp.concatenate([cosine, cosine], axis=1)
         sine = jnp.concatenate([-sine, sine], axis=1)
         spread = spread.reshape(Z * rows, chunk)
-        return spread, cosine, sine, new_keys, new_values, span_kv, payload
-
-    spread, cosine, sine, new_keys, new_values, span_kv, payload = lax.cond(
-        prefill_side, prefill, project
-    )
-
-    def attend(payload, spread, cosine, sine, new_keys, new_values, *weights):
+        keys = cache[:, :, 0].reshape(slots, local_width)
+        values = cache[:, :, 1].reshape(slots, local_width)
+        return spread, cosine, sine, new_keys, new_values, keys, values, span_kv, payload
+
+    spread, *beside, span_kv, payload = lax.cond(prefill_side, prefill, project)
+
+    def attend(payload, spread, cosine, sine, new_keys, new_values, keys, values, *weights):
         partial = pl.pallas_call(
             query_kernel,
             in_specs=[whole] * 5,
@@ -290,16 +342,14 @@
         returned = lax.all_to_all(
             partial.reshape(exchanged), "z", split_axis=0, concat_axis=0, tiled=True
         )
-        slots = requests * context
-        attended, pool, out_weight = pl.pallas_call(
+        attended, handed = pl.pallas_call(
             attention_kernel,
             out_shape=(
                 jax.ShapeDtypeStruct(exchanged, BF16),
-                section,
-                jax.ShapeDtypeStruct((Y * out_width, out_depth), BF16),
+                handed_over,
             ),
             in_specs=[pl.BlockSpec(memory_space=pltpu.SMEM)] + [whole] * 8,
-            out_specs=[whole] + [unwritten] * 2,
+            out_specs=[whole, unwritten],
             compiler_params=pltpu.CompilerParams(vmem_limit_bytes=VMEM_LIMIT),
         )(
             cache_len,
@@ -307,48 +357,69 @@
             q_gain.reshape(1, HEAD_SIZE),
             cosine,
             sine,
-            cache[:, :, 0].reshape(slots, local_width),
-            cache[:, :, 1].reshape(slots, local_width),
+            keys,
+            values,
             new_keys,
             new_values,
         )
-        return pool, out_weight, attended
-
-    pool, out_weight, attended = lax.cond(
+        return handed, attended
+
+    handed, attended = lax.cond(
         prefill_side, route, attend,
-        payload, spread, cosine, sine, new_keys, new_values, *arrived_weights,
-    )
-    out_weight = lax.ppermute(out_weight, "role", [(0, 1)])
-    pool = lax.ppermute(pool, "role", [(0, 1)])
+        payload, spread, *beside, *arrived_weights,
+    )
+    handed = lax.ppermute(handed, "role", [(0, 1)])
 
     def gather(attended):
         return lax.all_to_all(attended, "z", split_axis=0, concat_axis=0, tiled=True)
 
     attended = lax.cond(prefill_side, lambda attended: attended, gather, attended)
 
-    def finish(attended, out_weight):
+    def placed(kernel, source, block, index):
+        return pl.pallas_call(
+            kernel,
+            grid=(1,),
+            in_specs=[pl.BlockSpec(block, lambda i: index)],
+            out_specs=pl.BlockSpec((1,) + section.shape, lambda i: (0, 0, 0, 0)),
+            out_shape=jax.ShapeDtypeStruct((1,) + section.shape, BF16),
+        )(source)
+
+    def finish(attended, span_kv, handed):
         partial = lax.dot_general(
             attended.reshape(Z * rows, local_query),
-            out_weight,
+            handed,
             (((1,), (1,)), ((), ())),
             preferred_element_type=F32,
-        ).astype(BF16)
+        )[:, : Y * out_width].astype(BF16)
         back = lax.all_to_all(
             partial.reshape(Z, rows, chunk), "z", split_axis=0, concat_axis=0, tiled=True
         )
         tp_count = lax.axis_size("tp")
-        delta = back.astype(F32)
+        others = []
         for shift in range(1, tp_count):
             pairs = [(i, (i + shift) % tp_count) for i in range(tp_count)]
-            delta = delta + lax.ppermute(back, "tp", pairs).astype(F32)
-        delta = delta.transpose(1, 0, 2).reshape(steps, requests, width)
-        return (decode_hidden.astype(F32) + delta).astype(BF16)[None]
-
-    def idle_finish(attended, out_weight):
-        return jnp.zeros((1, steps, requests, width), BF16)
-
-    decoded = lax.cond(prefill_side, idle_finish, finish, attended, out_weight)
-    return jnp.where(prefill_side, span_kv, pool)[None], decoded
+            others.append(lax.ppermute(back, "tp", pairs))
+        base = pl.pallas_call(
+            base_kernel,
+            in_specs=[whole] * 2,
+            out_specs=whole,
+            out_shape=jax.ShapeDtypeStruct((Z, rows, chunk), F32),
+        )(decode_hidden, back)
+        decoded = pl.pallas_call(
+            sum_kernel,
+            in_specs=[whole] * (1 + len(others)),
+            out_specs=whole,
+            out_shape=jax.ShapeDtypeStruct((1, steps, requests, width), BF16),
+        )(base, *others)
+        pool = placed(
+            unpack_kernel, handed, (pool_rows, out_depth), (Y * out_width // pool_rows, 0)
+        )
+        return pool, decoded
+
+    def idle_finish(attended, span_kv, handed):
+        return placed(copy_kernel, span_kv, section.shape, (0, 0, 0)), jnp.zeros((1, steps, requests, width), BF16)
+
+    return lax.cond(prefill_side, idle_finish, finish, attended, span_kv, handed)
 
 
 def solution(mesh):

time: 90.3 us -> 83.6 us (0.926)
  blocking collectives: 25.2 us -> 42.3 us
  waiting for transfers between devices: 20.9 us -> 4.46 us
  starting transfers between devices: 25.3 us -> 19.3 us
  Pallas kernels: 5.25 us -> 9.96 us
  other arithmetic: 3.9 us -> 0.56 us
  local copies, waits for them, and re-layouts: 3.49 us -> 1.17 us
    all_to_all x0 -> x1, blocking collectives: none -> 16.9 us  [attend(): lax.all_to_all(partial.reshape(exchanged), 'z', split_axis=0, concat_axis...]
    all_to_all x1 -> x0, waiting for transfers between devices: 11 us -> none  [attend(): lax.all_to_all(partial.reshape(exchanged), 'z', split_axis=0, concat_axis...]
    all_to_all x1 -> x0, starting transfers between devices: 6.11 us -> none  [attend(): lax.all_to_all(partial.reshape(exchanged), 'z', split_axis=0, concat_axis...]
    ppermute x5 -> x4, waiting for transfers between devices: 6.31 us -> 0.71 us  [the longest x3 0.7 us: finish(): others.append(lax.ppermute(back, 'tp', pairs))]
    pallas_call x0 -> x3, Pallas kernels: none -> 4.64 us  [the longest x1 1.93 us: finish(): pl.pallas_call(sum_kernel, in_specs=[whole] * (1 + len(others)), out_spec...]
    broadcast_in_dim x2 -> x0, other arithmetic: 2.02 us -> none  [the longest x1 1.93 us: shards(): return (jnp.where(prefill_side, span_kv, pool)[None], decoded)]
    ppermute x3, starting transfers between devices: 3.88 us -> 4.83 us  [shards(): arrived_weights.append(lax.ppermute(q_weight, ('role', 'y'), pairs))]
    ppermute x5 -> x4, starting transfers between devices: 6.32 us -> 6.11 us  [the longest x3 4.82 us: finish(): others.append(lax.ppermute(back, 'tp', pairs))]
  transfers between devices with their start and end apart: 10 -> 8, of which waited for: 5 -> 2; matrix products, arithmetic and copies ran while one was open for 10% -> 5% of each run, Pallas kernels for 2% -> 6%
where the time goes in v3:
time: 83.6 us; the launch traced here: 83.2 us
  blocking collectives  42.3 us (51%)
  starting transfers between devices  19.3 us (23%)
  Pallas kernels  9.96 us (12%)
  waiting for transfers between devices  4.46 us (5%)
  matrix products  4.44 us (5%)
  local copies, waits for them, and re-layouts  1.17 us (1%)
    all_to_all x1, blocking collectives, attend(): lax.all_to_all(partial.reshape(exchanged), 'z', split_axis=0, concat_axis...  16.9 us
    all_to_all x1, blocking collectives, gather(): lax.all_to_all(attended, 'z', split_axis=0, concat_axis=0, tiled=True)  14.5 us
    all_to_all x1, blocking collectives, finish(): lax.all_to_all(partial.reshape(Z, rows, chunk), 'z', split_axis=0, concat...  10.8 us
    all_to_all x1, starting transfers between devices, project(): lax.all_to_all(spread, 'z', split_axis=0, concat_axis=0, tiled=True)  8.32 us
    ppermute x3, starting transfers between devices, shards(): arrived_weights.append(lax.ppermute(q_weight, ('role', 'y'), pairs))  4.83 us
    ppermute x3, starting transfers between devices, finish(): others.append(lax.ppermute(back, 'tp', pairs))  4.82 us
    all_to_all x1, waiting for transfers between devices, project(): lax.all_to_all(spread, 'z', split_axis=0, concat_axis=0, tiled=True)  3.75 us
    dot_general x1, matrix products, project(): jnp.einsum('rd,dcw->crw', normed, kv_weight, preferred_element_type=F32)  3.42 us
  transfers between devices with their start and end apart: 8, of which 2 were waited for; matrix products, arithmetic and copies ran while one was open for 5% of the time, Pallas kernels for 6%

profile of v3, /device:TPU:1, one launch (start us, length us, event | category | flops | bytes accessed | tf_op | source)
XLA Modules:
  0.0 83.2 jit_solution(11473877804757759234)
XLA Ops:
  0.6 3.3 %collective-permute-start.6 = (bf16[160,2048]{1,0:T(8,128)(2,1)}, bf16[160,2048]{1,0:T(8,128)(2,1)S(1)}, u32[]{:S(2)}, u32[]{:S(2)}) collective-permute-start(bf16[160,2048]{1,0:T(8,128)(2,1)} %param.25), channel_id=1, source_target_pairs={{0,140},{4,128},{8,132},{12,136},{128,0},{132,4},{136,8},{140,12},... | collective-permute-start | bytes 1966088 | tf_op jit(solution)/shard_map/ppermute | solution.py:299
  3.9 0.7 collective-permute-start.7
  4.6 0.9 %collective-permute-start.8 = (bf16[160,2048]{1,0:T(8,128)(2,1)}, bf16[160,2048]{1,0:T(8,128)(2,1)}, u32[]{:S(2)}, u32[]{:S(2)}) collective-permute-start(bf16[160,2048]{1,0:T(8,128)(2,1)} %param.25), channel_id=1, source_target_pairs={{0,132},{4,136},{8,140},{12,128},{128,0},{132,4},{136,8},{140,12},... | collective-permute-start | bytes 1966088 | tf_op jit(solution)/shard_map/ppermute | solution.py:299
  5.5 0.0 copy-start.1
  5.5 0.0 copy-start.10
  5.5 0.0 copy-start.15
  5.5 18.5 %conditional.4 = (bf16[128,640]{1,0:T(8,128)(2,1)S(1)}, f32[16,128]{1,0:T(8,128)S(1)}, f32[16,128]{1,0:T(8,128)S(1)}, bf16[16,256]{1,0:T(8,128)(2,1)S(1)}, bf16[...) conditional(s32[]{:T(128)} %convert_element_type.57, ...), branch_computations={%region_0.0_spmd, %region_2.6_spmd} | conditional | flops 1487554176 | bytes 15732424 | solution.py:332
  5.5 1.9 %branch_0_fun.6 = (bf16[8,16,640]{2,1,0:T(8,128)(2,1)}, bf16[16,5120]{1,0:T(8,128)(2,1)}, bf16[256,2,256]{2,1,0:T(2,128)(2,1)}, bf16[32,16,512]{2,1,0:T(8,128)(2,1)}) custom-call(s32[1]{0:T(128)} %bitcast.y_ref, bf16[4,4,5120]{2,1,0:T(4,128)(2,1)} %get-tuple-element.77.hidden_ref, f32[1,5120]{1,0:T(1,128)} %bitcast.69), custom_call_target="tpu_custom_call" | custom-call | tf_op jit(solution)/shard_map/cond/branch_0_fun/pallas_call | solution.py:302
  7.4 0.0 copy-start.11
  7.4 8.3 %all-to-all-start.2 = ((bf16[8,16,640]{2,1,0:T(8,128)(2,1)}), bf16[8,16,640]{2,1,0:T(8,128)(2,1)S(1)}, u32[]{:S(2)}, u32[]{:S(2)}) async-start(bf16[8,16,640]{2,1,0:T(8,128)(2,1)} %get-tuple-element.79), calls=%async_computation.2 | async-start | bytes 327680 | tf_op jit(solution)/shard_map/cond/branch_0_fun/all_to_all | solution.py:317
  15.7 0.0 copy-start.13
  15.7 0.0 copy-start.8
  15.8 0.0 copy-start.5
  15.8 3.4 %fusion.2 = f32[2,16,256]{2,1,0:T(8,128)S(1)} fusion(bf16[5120,2,256]{2,1,0:T(2,128)(2,1)} %get-tuple-element.210, bf16[16,5120]{1,0:T(8,128)(2,1)} %get-tuple-element.81), kind=kOutput, calls=%fused_computation.2 | convolution fusion | flops 83886080 | bytes 5439488 | tf_op jit(solution)/shard_map/cond/branch_0_fun/rd,dcw->crw/dot_general | solution.py:322
  19.2 0.1 multiply_reduce_fusion
  19.3 0.0 copy-done.11
  19.4 0.1 convert_element_type.45
  19.4 0.0 copy-done.13
  19.4 0.1 multiply_multiply_fusion
  19.5 0.1 fusion.7
  19.7 0.1 subtract_convert_fusion
  19.8 0.1 pad_maximum_fusion
  19.8 0.1 pad_maximum_fusion.2
  19.9 0.0 copy-done.8
  19.9 0.2 copy.33
  20.1 0.0 copy-done.5
  20.1 0.1 copy.35
  20.3 3.7 %all-to-all-done.2 = bf16[8,16,640]{2,1,0:T(8,128)(2,1)S(1)} async-done(((bf16[8,16,640]{2,1,0:T(8,128)(2,1)}), bf16[8,16,640]{2,1,0:T(8,128)(2,1)S(1)}, u32[]{:S(2)}, u32[]{:S(2)}) %all-to-all-start.2) | async-done | bytes 163872 | tf_op jit(solution)/shard_map/cond/branch_0_fun/all_to_all | solution.py:317
  24.0 0.0 copy-start
  24.0 0.0 collective-permute-done.6
  24.0 0.0 collective-permute-done.7
  24.0 0.0 collective-permute-done.8
  24.0 0.0 copy-done.1
  24.0 0.0 copy-done.10
  24.0 0.0 copy-done.15
  24.1 0.7 copy-done
  24.7 20.5 %conditional.5 = (bf16[704,2048]{1,0:T(8,128)(2,1)}, bf16[8,16,2048]{2,1,0:T(8,128)(2,1)S(1)}) conditional(s32[]{:T(128)} %convert_element_type.57, (bf16[128,640]{1,0:T(8,128)(2,1)S(1)}, bf16[160,2048]{1,0:T(8,128)(2,1)S(1)}, bf16[160,2048]{1,0:T(8,128)(2,1)S(1)}, bf16[160,2048]{1,0:T(8,128)(2,1)S(1)}, bf16[160,2048]{1,0:T(8,128)(2,1)}, ...), branch_computations={%region_6.7_spmd, %region_7.10_spmd} | conditional | flops 135761232 | bytes 22605258 | solution.py:367
  24.7 0.0 copy-start.12
  24.7 1.7 %branch_0_fun.7 = bf16[128,2048]{1,0:T(8,128)(2,1)S(1)} custom-call(bf16[128,640]{1,0:T(8,128)(2,1)S(1)} %get-tuple-element.94.rows_ref, bf16[160,2048]{1,0:T(8,128)(2,1)S(1)} %get-tuple-element.95.own_ref, bf16[160,2048]{1,0:T(8,128)(2,1)S(1)} %get-tuple-element.96.first_ref, bf16[160,2048]{1,0:T(8,128)(2,1)S(1)} %get-tuple-element.97.second_ref, ...), custom_call_target="tpu_custom_call" | custom-call | tf_op jit(solution)/shard_map/cond/branch_0_fun/pallas_call | solution.py:335
  26.4 16.9 %all_to_all.20.returned_ref = bf16[8,16,2048]{2,1,0:T(8,128)(2,1)S(1)} all-to-all(bf16[8,16,2048]{2,1,0:T(8,128)(2,1)S(1)} %bitcast.52), channel_id=1, replica_groups=mesh['role'=2,'z'=8,'y'=4,'tp'=4] {'z'}, dimensions={0} | all-to-all | bytes 1048576 | tf_op jit(solution)/shard_map/cond/branch_0_fun/all_to_all | solution.py:342
  43.4 0.0 copy-done.12
  43.4 1.7 %branch_0_fun.8 = (bf16[8,16,2048]{2,1,0:T(8,128)(2,1)S(1)}, bf16[704,2048]{1,0:T(8,128)(2,1)}) custom-call(s32[4]{0:T(128)S(1)} %copy-done.12, bf16[8,16,2048]{2,1,0:T(8,128)(2,1)S(1)} %all_to_all.20.returned_ref, f32[1,128]{1,0:T(1,128)S(1)} %bitcast.70, f32[16,128]{1,0:T(8,128)S(1)} %get-tuple-element.100.cosine_ref, ...), custom_call_target="tpu_custom_call" | custom-call | tf_op jit(solution)/shard_map/cond/branch_0_fun/pallas_call | solution.py:345
  45.3 1.3 %collective-permute-start.9 = (bf16[704,2048]{1,0:T(8,128)(2,1)}, bf16[704,2048]{1,0:T(8,128)(2,1)S(1)}, u32[]{:S(2)}, u32[]{:S(2)}) collective-permute-start(bf16[704,2048]{1,0:T(8,128)(2,1)} %get-tuple-element.138), channel_id=1, source_target_pairs={{0,128},{1,129},{2,130},{3,131},{4,132},{5,133},{6,134},{7,135},{8... | collective-permute-start | bytes 8650760 | tf_op jit(solution)/shard_map/ppermute | solution.py:371
  46.6 14.6 %conditional.6 = (bf16[8,16,2048]{2,1,0:T(8,128)(2,1)S(1)}) conditional(s32[]{:T(128)} %convert_element_type.57, bf16[8,16,2048]{2,1,0:T(8,128)(2,1)S(1)} %get-tuple-element.139, bf16[8,16,2048]{2,1,0:T(8,128)(2,1)S(1)} %get-tuple-element.139), branch_computations={%region_10.11_spmd, %region_11.12_spmd} | conditional | bytes 2097160 | solution.py:376
  46.6 14.5 %all_to_all.21 = bf16[8,16,2048]{2,1,0:T(8,128)(2,1)S(1)} all-to-all(bf16[8,16,2048]{2,1,0:T(8,128)(2,1)S(1)} %copy.82), channel_id=1, replica_groups=mesh['role'=2,'z'=8,'y'=4,'tp'=4] {'z'}, dimensions={0} | all-to-all | bytes 1048576 | tf_op jit(solution)/shard_map/cond/branch_0_fun/all_to_all | solution.py:374
  61.2 0.0 collective-permute-done.9
  61.2 22.0 %conditional.7 = (bf16[1,256,2,256]{3,2,1,0:T(2,128)(2,1)}, bf16[1,4,4,5120]{3,2,1,0:T(4,128)(2,1)}) conditional(s32[]{:T(128)} %convert_element_type.57, (bf16[704,2048]{1,0:T(8,128)(2,1)S(1)}, bf16[8,16,2048]{2,1,0:T(8,128)(2,1)S(1)}, bf16[4,4,5120]{2,1,0:T(4,128)(2,1)}) %tuple.41, bf16[256,2,256]{0,2,1:T(8,128)(2,1)} %copy-done), branch_computations={%region_12.13_spmd, %region_13.14_spmd} | conditional | flops 369098752 | bytes 8175836 | solution.py:422
  61.2 1.0 %fusion.33 = bf16[128,704]{1,0:T(8,128)(2,1)S(1)} fusion(bf16[128,2048]{1,0:T(8,128)(2,1)S(1)} %bitcast.55, bf16[704,2048]{1,0:T(8,128)(2,1)S(1)} %get-tuple-element.114.handed_ref), kind=kOutput, calls=%fused_computation.78 | convolution fusion | flops 369098752 | bytes 3588096 | tf_op jit(solution)/shard_map/cond/branch_0_fun/dot_general | solution.py:388
  62.2 0.0 copy-start.2
  62.2 10.8 %all_to_all.22.back_ref = bf16[8,16,640]{2,1,0:T(8,128)(2,1)S(1)} all-to-all(bf16[8,16,640]{2,1,0:T(8,128)(2,1)S(1)} %bitcast.62), channel_id=1, replica_groups=mesh['role'=2,'z'=8,'y'=4,'tp'=4] {'z'}, dimensions={0} | all-to-all | bytes 327680 | tf_op jit(solution)/shard_map/cond/branch_0_fun/all_to_all | solution.py:394
  73.0 0.0 copy-start.3
  73.0 1.2 %collective-permute-start.3 = (bf16[8,16,640]{2,1,0:T(8,128)(2,1)S(1)}, bf16[8,16,640]{2,1,0:T(8,128)(2,1)S(1)}, u32[]{:S(2)}, u32[]{:S(2)}) collective-permute-start(bf16[8,16,640]{2,1,0:T(8,128)(2,1)S(1)} %all_to_all.22.back_ref), channel_id=1, source_target_pairs={{0,1},{1,2},{2,3},{3,0},{4,5},{5,6},{6,7},{7,4},{8,9},{9,10},{10,1... | collective-permute-start | bytes 491528 | tf_op jit(solution)/shard_map/cond/branch_0_fun/ppermute | solution.py:401
  74.3 2.5 %collective-permute-start.4 = (bf16[8,16,640]{2,1,0:T(8,128)(2,1)S(1)}, bf16[8,16,640]{2,1,0:T(8,128)(2,1)}, u32[]{:S(2)}, u32[]{:S(2)}) collective-permute-start(bf16[8,16,640]{2,1,0:T(8,128)(2,1)S(1)} %all_to_all.22.back_ref), channel_id=1, source_target_pairs={{0,2},{1,3},{2,0},{3,1},{4,6},{5,7},{6,4},{7,5},{8,10},{9,11},{10,... | collective-permute-start | bytes 491528 | tf_op jit(solution)/shard_map/cond/branch_0_fun/ppermute | solution.py:401
  76.7 1.2 %collective-permute-start.5 = (bf16[8,16,640]{2,1,0:T(8,128)(2,1)S(1)}, bf16[8,16,640]{2,1,0:T(8,128)(2,1)}, u32[]{:S(2)}, u32[]{:S(2)}) collective-permute-start(bf16[8,16,640]{2,1,0:T(8,128)(2,1)S(1)} %all_to_all.22.back_ref), channel_id=1, source_target_pairs={{0,3},{1,0},{2,1},{3,2},{4,7},{5,4},{6,5},{7,6},{8,11},{9,8},{10,9... | collective-permute-start | bytes 491528 | tf_op jit(solution)/shard_map/cond/branch_0_fun/ppermute | solution.py:401
  77.9 1.0 %branch_0_fun.9 = bf16[1,256,2,256]{3,2,1,0:T(2,128)(2,1)} custom-call(bf16[704,2048]{1,0:T(8,128)(2,1)S(1)} %get-tuple-element.114.handed_ref), custom_call_target="tpu_custom_call" | custom-call | tf_op jit(solution)/shard_map/cond/branch_0_fun/pallas_call | solution.py:379
  78.9 0.0 copy-done.3
  78.9 0.0 copy-done.2
  78.9 1.7 %branch_0_fun.10.base_ref = f32[8,16,640]{2,1,0:T(8,128)} custom-call(bf16[4,4,5120]{2,1,0:T(4,128)(2,1)S(1)} %copy-done.2, bf16[8,16,640]{2,1,0:T(8,128)(2,1)} %copy-done.3), custom_call_target="tpu_custom_call" | custom-call | tf_op jit(solution)/shard_map/cond/branch_0_fun/pallas_call | solution.py:402
  80.6 0.0 collective-permute-done.3.first_ref
  80.6 0.0 copy-start.9
  80.6 0.7 collective-permute-done.4.second_ref
  81.3 0.0 collective-permute-done.5.third_ref
  81.3 0.0 copy-done.9
  81.3 1.9 %branch_0_fun.11 = bf16[1,4,4,5120]{3,2,1,0:T(4,128)(2,1)} custom-call(f32[8,16,640]{2,1,0:T(8,128)} %branch_0_fun.10.base_ref, bf16[8,16,640]{2,1,0:T(8,128)(2,1)} %copy-done.9, bf16[8,16,640]{2,1,0:T(8,128)(2,1)} %collective-permute-done.4.second_ref, bf16[8,16,640]{2,1,0:T(8,128)(2,1)} %collective-permute-done.5.third_ref), custom_call_target="tpu_custom_call" | custom-call | tf_op jit(solution)/shard_map/cond/branch_0_fun/pallas_call | solution.py:408
  (10 shorter events, 0.1 us)
Async XLA Ops:
  0.6 23.4 %collective-permute-start.6 = (bf16[160,2048]{1,0:T(8,128)(2,1)}, bf16[160,2048]{1,0:T(8,128)(2,1)S(1)}, u32[]{:S(2)}, u32[]{:S(2)}) collective-permute-start(bf16[160,2048]{1,0:T(8,128)(2,1)} %param.25), channel_id=1, source_target_pairs={{0,140},{4,128},{8,132},{12,136},{128,0},{132,4},{136,8},{140,12},... | collective-permute-start | bytes 1966088 | tf_op jit(solution)/shard_map/ppermute | solution.py:299
  3.9 20.1 %collective-permute-start.7 = (bf16[160,2048]{1,0:T(8,128)(2,1)}, bf16[160,2048]{1,0:T(8,128)(2,1)S(1)}, u32[]{:S(2)}, u32[]{:S(2)}) collective-permute-start(bf16[160,2048]{1,0:T(8,128)(2,1)} %param.25), channel_id=1, source_target_pairs={{0,136},{4,140},{8,128},{12,132},{128,0},{132,4},{136,8},{140,12},... | collective-permute-start | bytes 1966088 | tf_op jit(solution)/shard_map/ppermute | solution.py:299
  4.6 19.4 %collective-permute-start.8 = (bf16[160,2048]{1,0:T(8,128)(2,1)}, bf16[160,2048]{1,0:T(8,128)(2,1)}, u32[]{:S(2)}, u32[]{:S(2)}) collective-permute-start(bf16[160,2048]{1,0:T(8,128)(2,1)} %param.25), channel_id=1, source_target_pairs={{0,132},{4,136},{8,140},{12,128},{128,0},{132,4},{136,8},{140,12},... | collective-permute-start | bytes 1966088 | tf_op jit(solution)/shard_map/ppermute | solution.py:299
  5.5 18.6 %copy-start.1 = (bf16[160,2048]{1,0:T(8,128)(2,1)S(1)}, bf16[160,2048]{1,0:T(8,128)(2,1)}, u32[]{:S(2)}) copy-start(bf16[160,2048]{1,0:T(8,128)(2,1)} %param.25) | copy-start | bytes 1966084
  5.5 18.6 %copy-start.10 = (s32[32,32]{1,0:T(8,128)S(1)}, s32[32,32]{1,0:T(8,128)}, u32[]{:S(2)}) copy-start(s32[32,32]{1,0:T(8,128)} %param.31) | copy-start | bytes 12292
  5.5 18.6 %copy-start.15 = (f32[128]{0:T(128)S(1)}, f32[128]{0:T(128)}, u32[]{:S(2)}) copy-start(f32[128]{0:T(128)} %param.23) | copy-start | bytes 1540
  7.4 11.9 %copy-start.11 = (s32[4]{0:T(128)S(1)}, s32[4]{0:T(128)}, u32[]{:S(2)}) copy-start(s32[4]{0:T(128)} %get-tuple-element.80) | copy-start | bytes 52 | tf_op jit(solution)/shard_map/cond
  7.4 16.6 %all-to-all-start.2 = ((bf16[8,16,640]{2,1,0:T(8,128)(2,1)}), bf16[8,16,640]{2,1,0:T(8,128)(2,1)S(1)}, u32[]{:S(2)}, u32[]{:S(2)}) async-start(bf16[8,16,640]{2,1,0:T(8,128)(2,1)} %get-tuple-element.79), calls=%async_computation.2 | async-start | bytes 327680 | tf_op jit(solution)/shard_map/cond/branch_0_fun/all_to_all | solution.py:317
  15.7 3.7 %copy-start.13 = (f32[128]{0:T(128)S(1)}, f32[128]{0:T(128)}, u32[]{:S(2)}) copy-start(f32[128]{0:T(128)} %get-tuple-element.83) | copy-start | bytes 1540 | tf_op jit(solution)/shard_map/cond
  15.7 4.2 %copy-start.8 = (bf16[256,2,256]{2,1,0:T(2,128)(2,1)S(1)}, bf16[256,2,256]{2,1,0:T(2,128)(2,1)}, u32[]{:S(2)}) copy-start(bf16[256,2,256]{2,1,0:T(2,128)(2,1)} %get-tuple-element.204) | copy-start | bytes 786436 | tf_op jit(solution)/shard_map/cond
  15.8 4.4 %copy-start.5 = (bf16[4,128,2,256]{3,2,1,0:T(2,128)(2,1)S(1)}, bf16[4,128,2,256]{3,2,1,0:T(2,128)(2,1)}, u32[]{:S(2)}) copy-start(bf16[4,128,2,256]{3,2,1,0:T(2,128)(2,1)} %get-tuple-element.212) | copy-start | bytes 1572868 | tf_op jit(solution)/shard_map/cond
  24.0 0.7 copy-start
  24.7 18.6 %copy-start.12 = (s32[4]{0:T(128)S(1)}, s32[4]{0:T(128)}, u32[]{:S(2)}) copy-start(s32[4]{0:T(128)} %get-tuple-element.93.length_ref) | copy-start | bytes 52 | tf_op jit(solution)/shard_map/cond
  45.3 15.9 %collective-permute-start.9 = (bf16[704,2048]{1,0:T(8,128)(2,1)}, bf16[704,2048]{1,0:T(8,128)(2,1)S(1)}, u32[]{:S(2)}, u32[]{:S(2)}) collective-permute-start(bf16[704,2048]{1,0:T(8,128)(2,1)} %get-tuple-element.138), channel_id=1, source_target_pairs={{0,128},{1,129},{2,130},{3,131},{4,132},{5,133},{6,134},{7,135},{8... | collective-permute-start | bytes 8650760 | tf_op jit(solution)/shard_map/ppermute | solution.py:371
  62.2 16.7 %copy-start.2 = (bf16[4,4,5120]{2,1,0:T(4,128)(2,1)S(1)}, bf16[4,4,5120]{2,1,0:T(4,128)(2,1)}, u32[]{:S(2)}) copy-start(bf16[4,4,5120]{2,1,0:T(4,128)(2,1)} %get-tuple-element.115.hidden_ref) | copy-start | bytes 491524 | tf_op jit(solution)/shard_map/cond
  73.0 5.8 %copy-start.3 = (bf16[8,16,640]{2,1,0:T(8,128)(2,1)}, bf16[8,16,640]{2,1,0:T(8,128)(2,1)S(1)}, u32[]{:S(2)}) copy-start(bf16[8,16,640]{2,1,0:T(8,128)(2,1)S(1)} %all_to_all.22.back_ref) | copy-start | bytes 491524 | tf_op jit(solution)/shard_map/cond
  73.0 7.5 %collective-permute-start.3 = (bf16[8,16,640]{2,1,0:T(8,128)(2,1)S(1)}, bf16[8,16,640]{2,1,0:T(8,128)(2,1)S(1)}, u32[]{:S(2)}, u32[]{:S(2)}) collective-permute-start(bf16[8,16,640]{2,1,0:T(8,128)(2,1)S(1)} %all_to_all.22.back_ref), channel_id=1, source_target_pairs={{0,1},{1,2},{2,3},{3,0},{4,5},{5,6},{6,7},{7,4},{8,9},{9,10},{10,1... | collective-permute-start | bytes 491528 | tf_op jit(solution)/shard_map/cond/branch_0_fun/ppermute | solution.py:401
  74.3 7.0 %collective-permute-start.4 = (bf16[8,16,640]{2,1,0:T(8,128)(2,1)S(1)}, bf16[8,16,640]{2,1,0:T(8,128)(2,1)}, u32[]{:S(2)}, u32[]{:S(2)}) collective-permute-start(bf16[8,16,640]{2,1,0:T(8,128)(2,1)S(1)} %all_to_all.22.back_ref), channel_id=1, source_target_pairs={{0,2},{1,3},{2,0},{3,1},{4,6},{5,7},{6,4},{7,5},{8,10},{9,11},{10,... | collective-permute-start | bytes 491528 | tf_op jit(solution)/shard_map/cond/branch_0_fun/ppermute | solution.py:401
  76.7 4.6 %collective-permute-start.5 = (bf16[8,16,640]{2,1,0:T(8,128)(2,1)S(1)}, bf16[8,16,640]{2,1,0:T(8,128)(2,1)}, u32[]{:S(2)}, u32[]{:S(2)}) collective-permute-start(bf16[8,16,640]{2,1,0:T(8,128)(2,1)S(1)} %all_to_all.22.back_ref), channel_id=1, source_target_pairs={{0,3},{1,0},{2,1},{3,2},{4,7},{5,4},{6,5},{7,6},{8,11},{9,8},{10,9... | collective-permute-start | bytes 491528 | tf_op jit(solution)/shard_map/cond/branch_0_fun/ppermute | solution.py:401
  80.6 0.7 copy-start.9

commit v4 on v3

--- a/solution.py
+++ b/solution.py
@@ -17,7 +17,7 @@
 SEQ = ("z", "y")
 BLOCK_TOKENS = 8
 CAPACITY = 2
-VMEM_LIMIT = 32 * 2**20
+VMEM_LIMIT = 8 * 2**20
 F32, BF16 = jnp.float32, jnp.bfloat16
 
 
@@ -161,32 +161,8 @@
     return jnp.concatenate([pool[i * run : (i + 1) * run] for i in range(sides)], axis=1)
 
 
-def base_kernel(hidden_ref, back_ref, out_ref):
-    chunk = back_ref.shape[2]
-    for z in range(Z):
-        columns = slice(z * chunk, (z + 1) * chunk)
-        hidden = jnp.concatenate(
-            [hidden_ref[step, :, columns].astype(F32) for step in range(hidden_ref.shape[0])],
-            axis=0,
-        )
-        out_ref[z] = hidden + back_ref[z].astype(F32)
-
-
-def sum_kernel(base_ref, first_ref, second_ref, third_ref, out_ref):
-    steps, requests = out_ref.shape[1:3]
-    chunk = base_ref.shape[2]
-    for z in range(Z):
-        total = base_ref[z] + (
-            first_ref[z].astype(F32) + second_ref[z].astype(F32) + third_ref[z].astype(F32)
-        )
-        total = total.astype(BF16)
-        for step in range(steps):
-            out_ref[0, step, :, z * chunk : (z + 1) * chunk] = total[
-                step * requests : (step + 1) * requests
-            ]
-
-
-def unpack_kernel(handed_ref, out_ref):
+def unpack_kernel(handed_ref, hidden_ref, out_ref, wide_ref):
+    wide_ref[...] = hidden_ref[...].astype(F32)
     tokens, sections, width = out_ref.shape[1:]
     sides = handed_ref.shape[1] // (sections * width)
     run = tokens // sides
@@ -293,10 +269,10 @@
         handed = lax.dynamic_update_slice(handed, packed(pool, out_depth), (Y * out_width, 0))
         return handed, jnp.zeros(exchanged, BF16)
 
-    arrived_weights = []
-    for shift in range(1, Y):
+    arrived_weights = [None] * (Y - 1)
+    for shift in (2, 3, 1):
         pairs = [(i, Y + (i - shift) % Y) for i in range(Y)] + [(Y + i, i) for i in range(Y)]
-        arrived_weights.append(lax.ppermute(q_weight, ("role", "y"), pairs))
+        arrived_weights[shift - 1] = lax.ppermute(q_weight, ("role", "y"), pairs)
 
     def project(*_):
         spread, normed, span_kv, payload = pl.pallas_call(
@@ -313,6 +289,7 @@
                 whole,
             ],
             out_specs=[whole] * 2 + [unwritten] * 2,
+            compiler_params=pltpu.CompilerParams(vmem_limit_bytes=VMEM_LIMIT),
         )(y_index.astype(jnp.int32).reshape(1), decode_hidden, attn_gain.reshape(1, width))
         spread = lax.all_to_all(spread, "z", split_axis=0, concat_axis=0, tiled=True)
         position = (
@@ -375,14 +352,8 @@
 
     attended = lax.cond(prefill_side, lambda attended: attended, gather, attended)
 
-    def placed(kernel, source, block, index):
-        return pl.pallas_call(
-            kernel,
-            grid=(1,),
-            in_specs=[pl.BlockSpec(block, lambda i: index)],
-            out_specs=pl.BlockSpec((1,) + section.shape, lambda i: (0, 0, 0, 0)),
-            out_shape=jax.ShapeDtypeStruct((1,) + section.shape, BF16),
-        )(source)
+    limited = pltpu.CompilerParams(vmem_limit_bytes=VMEM_LIMIT)
+    placed = jax.ShapeDtypeStruct((1,) + section.shape, BF16)
 
     def finish(attended, span_kv, handed):
         partial = lax.dot_general(
@@ -395,29 +366,32 @@
             partial.reshape(Z, rows, chunk), "z", split_axis=0, concat_axis=0, tiled=True
         )
         tp_count = lax.axis_size("tp")
-        others = []
+        delta = back.astype(F32)
         for shift in range(1, tp_count):
             pairs = [(i, (i + shift) % tp_count) for i in range(tp_count)]
-            others.append(lax.ppermute(back, "tp", pairs))
-        base = pl.pallas_call(
-            base_kernel,
-            in_specs=[whole] * 2,
-            out_specs=whole,
-            out_shape=jax.ShapeDtypeStruct((Z, rows, chunk), F32),
-        )(decode_hidden, back)
-        decoded = pl.pallas_call(
-            sum_kernel,
-            in_specs=[whole] * (1 + len(others)),
-            out_specs=whole,
-            out_shape=jax.ShapeDtypeStruct((1, steps, requests, width), BF16),
-        )(base, *others)
-        pool = placed(
-            unpack_kernel, handed, (pool_rows, out_depth), (Y * out_width // pool_rows, 0)
-        )
-        return pool, decoded
+            delta = delta + lax.ppermute(back, "tp", pairs).astype(F32)
+        delta = delta.transpose(1, 0, 2).reshape(steps, requests, width)
+        pool, hidden = pl.pallas_call(
+            unpack_kernel,
+            grid=(1,),
+            in_specs=[
+                pl.BlockSpec((pool_rows, out_depth), lambda i: (Y * out_width // pool_rows, 0)),
+                pl.BlockSpec((steps, requests, width), lambda i: (0, 0, 0)),
+            ],
+            out_specs=[
+                pl.BlockSpec(placed.shape, lambda i: (0, 0, 0, 0)),
+                pl.BlockSpec((steps, requests, width), lambda i: (0, 0, 0)),
+            ],
+            out_shape=(placed, jax.ShapeDtypeStruct((steps, requests, width), F32)),
+            compiler_params=limited,
+        )(handed, decode_hidden)
+        return pool, (hidden + delta).astype(BF16)[None]
 
     def idle_finish(attended, span_kv, handed):
-        return placed(copy_kernel, span_kv, section.shape, (0, 0, 0)), jnp.zeros((1, steps, requests, width), BF16)
+        span = pl.pallas_call(
+            copy_kernel, in_specs=[whole], out_specs=whole, out_shape=placed, compiler_params=limited
+        )(span_kv)
+        return span, jnp.zeros((1, steps, requests, width), BF16)
 
     return lax.cond(prefill_side, idle_finish, finish, attended, span_kv, handed)
 

time: 83.6 us -> 82.4 us (0.986)
  Pallas kernels: 9.96 us -> 6.34 us
  waiting for transfers between devices: 4.46 us -> 6.17 us
    pallas_call x3 -> x1, Pallas kernels: 4.64 us -> 1.02 us  [finish(): pl.pallas_call(unpack_kernel, grid=(1,), in_specs=[pl.BlockSpec((pool_row...]
    ppermute x6, waiting for transfers between devices: 0.71 us -> 2.3 us  [the longest x3 2.29 us: finish(): delta = delta + lax.ppermute(back, 'tp', pairs).astype(F32)]
  transfers between devices with their start and end apart: 8 -> 8, of which waited for: 2 -> 2; matrix products, arithmetic and copies ran while one was open for 5% -> 5% of each run, Pallas kernels for 6% -> 4%
where the time goes in v4:
time: 82.4 us; the launch traced here: 82.1 us
  blocking collectives  42.2 us (51%)
  starting transfers between devices  19.2 us (23%)
  Pallas kernels  6.34 us (8%)
  waiting for transfers between devices  6.17 us (7%)
  matrix products  4.35 us (5%)
  local copies, waits for them, and re-layouts  1.39 us (2%)
  other arithmetic  1.39 us (2%)
    all_to_all x1, blocking collectives, attend(): lax.all_to_all(partial.reshape(exchanged), 'z', split_axis=0, concat_axis...  16.9 us
    all_to_all x1, blocking collectives, gather(): lax.all_to_all(attended, 'z', split_axis=0, concat_axis=0, tiled=True)  14.5 us
    all_to_all x1, blocking collectives, finish(): lax.all_to_all(partial.reshape(Z, rows, chunk), 'z', split_axis=0, concat...  10.7 us
    all_to_all x1, starting transfers between devices, project(): lax.all_to_all(spread, 'z', split_axis=0, concat_axis=0, tiled=True)  8.32 us
    ppermute x3, starting transfers between devices, shards(): arrived_weights[shift - 1] = lax.ppermute(q_weight, ('role', 'y'), pairs)  4.83 us
    ppermute x3, starting transfers between devices, finish(): delta = delta + lax.ppermute(back, 'tp', pairs).astype(F32)  4.81 us
    all_to_all x1, waiting for transfers between devices, project(): lax.all_to_all(spread, 'z', split_axis=0, concat_axis=0, tiled=True)  3.87 us
    dot_general x1, matrix products, project(): jnp.einsum('rd,dcw->crw', normed, kv_weight, preferred_element_type=F32)  3.33 us
  transfers between devices with their start and end apart: 8, of which 2 were waited for; matrix products, arithmetic and copies ran while one was open for 5% of the time, Pallas kernels for 4%

profile of v4, /device:TPU:1, one launch (start us, length us, event | category | flops | bytes accessed | tf_op | source)
XLA Modules:
  0.0 82.1 jit_solution(4238381360454306050)
XLA Ops:
  0.6 3.3 %collective-permute-start.6 = (bf16[160,2048]{1,0:T(8,128)(2,1)}, bf16[160,2048]{1,0:T(8,128)(2,1)S(1)}, u32[]{:S(2)}, u32[]{:S(2)}) collective-permute-start(bf16[160,2048]{1,0:T(8,128)(2,1)} %param.25), channel_id=1, source_target_pairs={{0,140},{4,128},{8,132},{12,136},{128,0},{132,4},{136,8},{140,12},... | collective-permute-start | bytes 1966088 | tf_op jit(solution)/shard_map/ppermute | solution.py:275
  3.9 0.7 collective-permute-start.7
  4.6 0.9 %collective-permute-start.8 = (bf16[160,2048]{1,0:T(8,128)(2,1)}, bf16[160,2048]{1,0:T(8,128)(2,1)}, u32[]{:S(2)}, u32[]{:S(2)}) collective-permute-start(bf16[160,2048]{1,0:T(8,128)(2,1)} %param.25), channel_id=1, source_target_pairs={{0,132},{4,136},{8,140},{12,128},{128,0},{132,4},{136,8},{140,12},... | collective-permute-start | bytes 1966088 | tf_op jit(solution)/shard_map/ppermute | solution.py:275
  5.5 0.0 copy-start.2
  5.5 0.0 copy-start.7
  5.5 0.0 copy-start.12
  5.5 18.5 %conditional.4 = (bf16[128,640]{1,0:T(8,128)(2,1)S(1)}, f32[16,128]{1,0:T(8,128)S(1)}, f32[16,128]{1,0:T(8,128)S(1)}, bf16[16,256]{1,0:T(8,128)(2,1)S(1)}, bf16[...) conditional(s32[]{:T(128)} %convert_element_type.72, ...), branch_computations={%region_0.0_spmd, %region_2.6_spmd} | conditional | flops 1487554176 | bytes 15732424 | solution.py:309
  5.5 1.9 %branch_0_fun.4 = (bf16[8,16,640]{2,1,0:T(8,128)(2,1)}, bf16[16,5120]{1,0:T(8,128)(2,1)S(1)}, bf16[256,2,256]{2,1,0:T(2,128)(2,1)S(1)}, bf16[32,16,512]{2,1,0:T(8,128)(2,1)}) custom-call(s32[1]{0:T(128)} %bitcast.y_ref, bf16[4,4,5120]{2,1,0:T(4,128)(2,1)} %get-tuple-element.77.hidden_ref, f32[1,5120]{1,0:T(1,128)} %bitcast.73), custom_call_target="tpu_custom_call" | custom-call | tf_op jit(solution)/shard_map/cond/branch_0_fun/pallas_call | solution.py:278
  7.4 0.0 copy-start.8
  7.4 8.3 %all-to-all-start.2 = ((bf16[8,16,640]{2,1,0:T(8,128)(2,1)}), bf16[8,16,640]{2,1,0:T(8,128)(2,1)S(1)}, u32[]{:S(2)}, u32[]{:S(2)}) async-start(bf16[8,16,640]{2,1,0:T(8,128)(2,1)} %get-tuple-element.79), calls=%async_computation.2 | async-start | bytes 327680 | tf_op jit(solution)/shard_map/cond/branch_0_fun/all_to_all | solution.py:294
  15.7 0.0 copy-start.10
  15.7 0.0 copy-start.4
  15.8 3.3 %fusion.2 = f32[2,16,256]{2,1,0:T(8,128)S(1)} fusion(bf16[5120,2,256]{2,1,0:T(2,128)(2,1)} %get-tuple-element.233, bf16[16,5120]{1,0:T(8,128)(2,1)S(1)} %get-tuple-element.81), kind=kOutput, calls=%fused_computation.2 | convolution fusion | flops 83886080 | bytes 5439488 | tf_op jit(solution)/shard_map/cond/branch_0_fun/rd,dcw->crw/dot_general | solution.py:299
  19.1 0.1 multiply_reduce_fusion
  19.2 0.0 copy-done.8
  19.2 0.1 convert_element_type.55
  19.3 0.0 copy-done.10
  19.3 0.1 multiply_multiply_fusion
  19.4 0.1 fusion.7
  19.5 0.1 subtract_convert_fusion
  19.6 0.1 pad_maximum_fusion
  19.7 0.1 pad_maximum_fusion.2
  19.8 0.2 copy.39
  20.0 0.0 copy-done.4
  20.0 0.1 copy.42
  20.1 3.9 %all-to-all-done.2 = bf16[8,16,640]{2,1,0:T(8,128)(2,1)S(1)} async-done(((bf16[8,16,640]{2,1,0:T(8,128)(2,1)}), bf16[8,16,640]{2,1,0:T(8,128)(2,1)S(1)}, u32[]{:S(2)}, u32[]{:S(2)}) %all-to-all-start.2) | async-done | bytes 163872 | tf_op jit(solution)/shard_map/cond/branch_0_fun/all_to_all | solution.py:294
  24.0 0.0 copy-start
  24.0 0.0 collective-permute-done.6
  24.0 0.0 collective-permute-done.7
  24.0 0.0 collective-permute-done.8
  24.0 0.0 copy-done.2
  24.0 0.0 copy-done.7
  24.0 0.0 copy-done.12
  24.1 0.7 copy-done
  24.7 20.5 %conditional.5 = (bf16[704,2048]{1,0:T(8,128)(2,1)}, bf16[8,16,2048]{2,1,0:T(8,128)(2,1)S(1)}) conditional(s32[]{:T(128)} %convert_element_type.72, (bf16[128,640]{1,0:T(8,128)(2,1)S(1)}, bf16[160,2048]{1,0:T(8,128)(2,1)S(1)}, bf16[160,2048]{1,0:T(8,128)(2,1)S(1)}, bf16[160,2048]{1,0:T(8,128)(2,1)S(1)}, bf16[160,2048]{1,0:T(8,128)(2,1)}, ...), branch_computations={%region_6.7_spmd, %region_7.10_spmd} | conditional | flops 135761232 | bytes 22605258 | solution.py:344
  24.7 0.0 copy-start.9
  24.7 1.7 %branch_0_fun.5 = bf16[128,2048]{1,0:T(8,128)(2,1)S(1)} custom-call(bf16[128,640]{1,0:T(8,128)(2,1)S(1)} %get-tuple-element.94.rows_ref, bf16[160,2048]{1,0:T(8,128)(2,1)S(1)} %get-tuple-element.95.own_ref, bf16[160,2048]{1,0:T(8,128)(2,1)S(1)} %get-tuple-element.96.first_ref, bf16[160,2048]{1,0:T(8,128)(2,1)S(1)} %get-tuple-element.97.second_ref, ...), custom_call_target="tpu_custom_call" | custom-call | tf_op jit(solution)/shard_map/cond/branch_0_fun/pallas_call | solution.py:312
  26.4 16.9 %all_to_all.20.returned_ref = bf16[8,16,2048]{2,1,0:T(8,128)(2,1)S(1)} all-to-all(bf16[8,16,2048]{2,1,0:T(8,128)(2,1)S(1)} %bitcast.56), channel_id=1, replica_groups=mesh['role'=2,'z'=8,'y'=4,'tp'=4] {'z'}, dimensions={0} | all-to-all | bytes 1048576 | tf_op jit(solution)/shard_map/cond/branch_0_fun/all_to_all | solution.py:319
  43.4 0.0 copy-done.9
  43.4 1.7 %branch_0_fun.6 = (bf16[8,16,2048]{2,1,0:T(8,128)(2,1)S(1)}, bf16[704,2048]{1,0:T(8,128)(2,1)}) custom-call(s32[4]{0:T(128)S(1)} %copy-done.9, bf16[8,16,2048]{2,1,0:T(8,128)(2,1)S(1)} %all_to_all.20.returned_ref, f32[1,128]{1,0:T(1,128)S(1)} %bitcast.74, f32[16,128]{1,0:T(8,128)S(1)} %get-tuple-element.100.cosine_ref, ...), custom_call_target="tpu_custom_call" | custom-call | tf_op jit(solution)/shard_map/cond/branch_0_fun/pallas_call | solution.py:322
  45.3 1.3 %collective-permute-start.9 = (bf16[704,2048]{1,0:T(8,128)(2,1)}, bf16[704,2048]{1,0:T(8,128)(2,1)S(1)}, u32[]{:S(2)}, u32[]{:S(2)}) collective-permute-start(bf16[704,2048]{1,0:T(8,128)(2,1)} %get-tuple-element.140), channel_id=1, source_target_pairs={{0,128},{1,129},{2,130},{3,131},{4,132},{5,133},{6,134},{7,135},{8... | collective-permute-start | bytes 8650760 | tf_op jit(solution)/shard_map/ppermute | solution.py:348
  46.6 14.6 %conditional.6 = (bf16[8,16,2048]{2,1,0:T(8,128)(2,1)S(1)}) conditional(s32[]{:T(128)} %convert_element_type.72, bf16[8,16,2048]{2,1,0:T(8,128)(2,1)S(1)} %get-tuple-element.141, bf16[8,16,2048]{2,1,0:T(8,128)(2,1)S(1)} %get-tuple-element.141), branch_computations={%region_10.11_spmd, %region_11.12_spmd} | conditional | bytes 2097160 | solution.py:353
  46.6 14.5 %all_to_all.21 = bf16[8,16,2048]{2,1,0:T(8,128)(2,1)S(1)} all-to-all(bf16[8,16,2048]{2,1,0:T(8,128)(2,1)S(1)} %copy.89), channel_id=1, replica_groups=mesh['role'=2,'z'=8,'y'=4,'tp'=4] {'z'}, dimensions={0} | all-to-all | bytes 1048576 | tf_op jit(solution)/shard_map/cond/branch_0_fun/all_to_all | solution.py:351
  61.2 0.0 collective-permute-done.9
  61.2 20.9 %conditional.7 = (bf16[1,256,2,256]{3,2,1,0:T(2,128)(2,1)}, bf16[1,4,4,5120]{3,2,1,0:T(4,128)(2,1)}) conditional(s32[]{:T(128)} %convert_element_type.72, (bf16[704,2048]{1,0:T(8,128)(2,1)S(1)}, bf16[4,4,5120]{2,1,0:T(4,128)(2,1)}, bf16[8,16,2048]{2,1,0:T(8,128)(2,1)S(1)}) %tuple.41, bf16[256,2,256]{0,2,1:T(8,128)(2,1)} %copy-done), branch_computations={%region_12.13_spmd, %region_13.14_spmd} | conditional | flops 369836032 | bytes 9978020 | solution.py:396
  61.2 0.0 copy-start.1
  61.2 1.0 %fusion.34 = bf16[128,704]{1,0:T(8,128)(2,1)S(1)} fusion(bf16[128,2048]{1,0:T(8,128)(2,1)S(1)} %bitcast.59, bf16[704,2048]{1,0:T(8,128)(2,1)S(1)} %get-tuple-element.114.handed_ref), kind=kOutput, calls=%fused_computation.81 | convolution fusion | flops 369098752 | bytes 3588096 | tf_op jit(solution)/shard_map/cond/branch_0_fun/dot_general | solution.py:359
  62.2 10.7 %all_to_all.22 = bf16[8,16,640]{2,1,0:T(8,128)(2,1)S(1)} all-to-all(bf16[8,16,640]{2,1,0:T(8,128)(2,1)S(1)} %bitcast.66), channel_id=1, replica_groups=mesh['role'=2,'z'=8,'y'=4,'tp'=4] {'z'}, dimensions={0} | all-to-all | bytes 327680 | tf_op jit(solution)/shard_map/cond/branch_0_fun/all_to_all | solution.py:365
  72.9 1.2 %collective-permute-start.3 = (bf16[8,16,640]{2,1,0:T(8,128)(2,1)S(1)}, bf16[8,16,640]{2,1,0:T(8,128)(2,1)S(1)}, u32[]{:S(2)}, u32[]{:S(2)}) collective-permute-start(bf16[8,16,640]{2,1,0:T(8,128)(2,1)S(1)} %all_to_all.22), channel_id=1, source_target_pairs={{0,1},{1,2},{2,3},{3,0},{4,5},{5,6},{6,7},{7,4},{8,9},{9,10},{10,1... | collective-permute-start | bytes 491528 | tf_op jit(solution)/shard_map/cond/branch_0_fun/ppermute | solution.py:372
  74.1 2.5 %collective-permute-start.4 = (bf16[8,16,640]{2,1,0:T(8,128)(2,1)S(1)}, bf16[8,16,640]{2,1,0:T(8,128)(2,1)S(1)}, u32[]{:S(2)}, u32[]{:S(2)}) collective-permute-start(bf16[8,16,640]{2,1,0:T(8,128)(2,1)S(1)} %all_to_all.22), channel_id=1, source_target_pairs={{0,2},{1,3},{2,0},{3,1},{4,6},{5,7},{6,4},{7,5},{8,10},{9,11},{10,... | collective-permute-start | bytes 491528 | tf_op jit(solution)/shard_map/cond/branch_0_fun/ppermute | solution.py:372
  76.6 1.2 %collective-permute-start.5 = (bf16[8,16,640]{2,1,0:T(8,128)(2,1)S(1)}, bf16[8,16,640]{2,1,0:T(8,128)(2,1)S(1)}, u32[]{:S(2)}, u32[]{:S(2)}) collective-permute-start(bf16[8,16,640]{2,1,0:T(8,128)(2,1)S(1)} %all_to_all.22), channel_id=1, source_target_pairs={{0,3},{1,0},{2,1},{3,2},{4,7},{5,4},{6,5},{7,6},{8,11},{9,8},{10,9... | collective-permute-start | bytes 491528 | tf_op jit(solution)/shard_map/cond/branch_0_fun/ppermute | solution.py:372
  77.7 0.0 copy-done.1
  77.7 1.0 %branch_0_fun.7 = (bf16[1,256,2,256]{3,2,1,0:T(2,128)(2,1)}, f32[4,4,5120]{2,1,0:T(4,128)S(1)}) custom-call(bf16[704,2048]{1,0:T(8,128)(2,1)S(1)} %get-tuple-element.114.handed_ref, bf16[4,4,5120]{2,1,0:T(4,128)(2,1)S(1)} %copy-done.1), custom_call_target="tpu_custom_call" | custom-call | tf_op jit(solution)/shard_map/cond/branch_0_fun/pallas_call | solution.py:374
  78.7 0.0 collective-permute-done.3
  78.7 2.3 %collective-permute-done.4 = bf16[8,16,640]{2,1,0:T(8,128)(2,1)S(1)} collective-permute-done((bf16[8,16,640]{2,1,0:T(8,128)(2,1)S(1)}, bf16[8,16,640]{2,1,0:T(8,128)(2,1)S(1)}, u32[]{:S(2)}, u32[]{:S(2)}) %collective-permute-start.4) | collective-permute-done | bytes 163872 | tf_op jit(solution)/shard_map/cond/branch_0_fun/ppermute | solution.py:372
  81.0 0.0 collective-permute-done.5
  81.0 0.1 add_bitcast_fusion
  81.1 0.1 copy.40
  81.2 0.1 reshape.307
  81.4 0.8 fusion.31
  (10 shorter events, 0.1 us)
Async XLA Ops:
  0.6 23.4 %collective-permute-start.6 = (bf16[160,2048]{1,0:T(8,128)(2,1)}, bf16[160,2048]{1,0:T(8,128)(2,1)S(1)}, u32[]{:S(2)}, u32[]{:S(2)}) collective-permute-start(bf16[160,2048]{1,0:T(8,128)(2,1)} %param.25), channel_id=1, source_target_pairs={{0,140},{4,128},{8,132},{12,136},{128,0},{132,4},{136,8},{140,12},... | collective-permute-start | bytes 1966088 | tf_op jit(solution)/shard_map/ppermute | solution.py:275
  3.9 20.1 %collective-permute-start.7 = (bf16[160,2048]{1,0:T(8,128)(2,1)}, bf16[160,2048]{1,0:T(8,128)(2,1)S(1)}, u32[]{:S(2)}, u32[]{:S(2)}) collective-permute-start(bf16[160,2048]{1,0:T(8,128)(2,1)} %param.25), channel_id=1, source_target_pairs={{0,136},{4,140},{8,128},{12,132},{128,0},{132,4},{136,8},{140,12},... | collective-permute-start | bytes 1966088 | tf_op jit(solution)/shard_map/ppermute | solution.py:275
  4.6 19.4 %collective-permute-start.8 = (bf16[160,2048]{1,0:T(8,128)(2,1)}, bf16[160,2048]{1,0:T(8,128)(2,1)}, u32[]{:S(2)}, u32[]{:S(2)}) collective-permute-start(bf16[160,2048]{1,0:T(8,128)(2,1)} %param.25), channel_id=1, source_target_pairs={{0,132},{4,136},{8,140},{12,128},{128,0},{132,4},{136,8},{140,12},... | collective-permute-start | bytes 1966088 | tf_op jit(solution)/shard_map/ppermute | solution.py:275
  5.5 18.6 %copy-start.2 = (bf16[160,2048]{1,0:T(8,128)(2,1)S(1)}, bf16[160,2048]{1,0:T(8,128)(2,1)}, u32[]{:S(2)}) copy-start(bf16[160,2048]{1,0:T(8,128)(2,1)} %param.25) | copy-start | bytes 1966084
  5.5 18.6 %copy-start.7 = (s32[32,32]{1,0:T(8,128)S(1)}, s32[32,32]{1,0:T(8,128)}, u32[]{:S(2)}) copy-start(s32[32,32]{1,0:T(8,128)} %param.31) | copy-start | bytes 12292
  5.5 18.6 %copy-start.12 = (f32[128]{0:T(128)S(1)}, f32[128]{0:T(128)}, u32[]{:S(2)}) copy-start(f32[128]{0:T(128)} %param.23) | copy-start | bytes 1540
  7.4 11.8 %copy-start.8 = (s32[4]{0:T(128)S(1)}, s32[4]{0:T(128)}, u32[]{:S(2)}) copy-start(s32[4]{0:T(128)} %get-tuple-element.80) | copy-start | bytes 52 | tf_op jit(solution)/shard_map/cond
  7.4 16.6 %all-to-all-start.2 = ((bf16[8,16,640]{2,1,0:T(8,128)(2,1)}), bf16[8,16,640]{2,1,0:T(8,128)(2,1)S(1)}, u32[]{:S(2)}, u32[]{:S(2)}) async-start(bf16[8,16,640]{2,1,0:T(8,128)(2,1)} %get-tuple-element.79), calls=%async_computation.2 | async-start | bytes 327680 | tf_op jit(solution)/shard_map/cond/branch_0_fun/all_to_all | solution.py:294
  15.7 3.6 %copy-start.10 = (f32[128]{0:T(128)S(1)}, f32[128]{0:T(128)}, u32[]{:S(2)}) copy-start(f32[128]{0:T(128)} %get-tuple-element.83) | copy-start | bytes 1540 | tf_op jit(solution)/shard_map/cond
  15.7 4.3 %copy-start.4 = (bf16[4,128,2,256]{3,2,1,0:T(2,128)(2,1)S(1)}, bf16[4,128,2,256]{3,2,1,0:T(2,128)(2,1)}, u32[]{:S(2)}) copy-start(bf16[4,128,2,256]{3,2,1,0:T(2,128)(2,1)} %get-tuple-element.235) | copy-start | bytes 1572868 | tf_op jit(solution)/shard_map/cond
  24.0 0.7 copy-start
  24.7 18.6 %copy-start.9 = (s32[4]{0:T(128)S(1)}, s32[4]{0:T(128)}, u32[]{:S(2)}) copy-start(s32[4]{0:T(128)} %get-tuple-element.93.length_ref) | copy-start | bytes 52 | tf_op jit(solution)/shard_map/cond
  45.3 15.9 %collective-permute-start.9 = (bf16[704,2048]{1,0:T(8,128)(2,1)}, bf16[704,2048]{1,0:T(8,128)(2,1)S(1)}, u32[]{:S(2)}, u32[]{:S(2)}) collective-permute-start(bf16[704,2048]{1,0:T(8,128)(2,1)} %get-tuple-element.140), channel_id=1, source_target_pairs={{0,128},{1,129},{2,130},{3,131},{4,132},{5,133},{6,134},{7,135},{8... | collective-permute-start | bytes 8650760 | tf_op jit(solution)/shard_map/ppermute | solution.py:348
  61.2 16.5 %copy-start.1 = (bf16[4,4,5120]{2,1,0:T(4,128)(2,1)S(1)}, bf16[4,4,5120]{2,1,0:T(4,128)(2,1)}, u32[]{:S(2)}) copy-start(bf16[4,4,5120]{2,1,0:T(4,128)(2,1)} %get-tuple-element.115.hidden_ref) | copy-start | bytes 491524 | tf_op jit(solution)/shard_map/cond
  72.9 5.8 %collective-permute-start.3 = (bf16[8,16,640]{2,1,0:T(8,128)(2,1)S(1)}, bf16[8,16,640]{2,1,0:T(8,128)(2,1)S(1)}, u32[]{:S(2)}, u32[]{:S(2)}) collective-permute-start(bf16[8,16,640]{2,1,0:T(8,128)(2,1)S(1)} %all_to_all.22), channel_id=1, source_target_pairs={{0,1},{1,2},{2,3},{3,0},{4,5},{5,6},{6,7},{7,4},{8,9},{9,10},{10,1... | collective-permute-start | bytes 491528 | tf_op jit(solution)/shard_map/cond/branch_0_fun/ppermute | solution.py:372
  74.1 6.9 %collective-permute-start.4 = (bf16[8,16,640]{2,1,0:T(8,128)(2,1)S(1)}, bf16[8,16,640]{2,1,0:T(8,128)(2,1)S(1)}, u32[]{:S(2)}, u32[]{:S(2)}) collective-permute-start(bf16[8,16,640]{2,1,0:T(8,128)(2,1)S(1)} %all_to_all.22), channel_id=1, source_target_pairs={{0,2},{1,3},{2,0},{3,1},{4,6},{5,7},{6,4},{7,5},{8,10},{9,11},{10,... | collective-permute-start | bytes 491528 | tf_op jit(solution)/shard_map/cond/branch_0_fun/ppermute | solution.py:372
  76.6 4.5 %collective-permute-start.5 = (bf16[8,16,640]{2,1,0:T(8,128)(2,1)S(1)}, bf16[8,16,640]{2,1,0:T(8,128)(2,1)S(1)}, u32[]{:S(2)}, u32[]{:S(2)}) collective-permute-start(bf16[8,16,640]{2,1,0:T(8,128)(2,1)S(1)} %all_to_all.22), channel_id=1, source_target_pairs={{0,3},{1,0},{2,1},{3,2},{4,7},{5,4},{6,5},{7,6},{8,11},{9,8},{10,9... | collective-permute-start | bytes 491528 | tf_op jit(solution)/shard_map/cond/branch_0_fun/ppermute | solution.py:372

commit v5 on v4

--- a/solution.py
+++ b/solution.py
@@ -167,9 +167,12 @@
     sides = handed_ref.shape[1] // (sections * width)
     run = tokens // sides
     for i in range(sides):
+        parts = []
         for section in range(sections):
             start = (i * sections + section) * width
-            out_ref[0, i * run : (i + 1) * run, section, :] = handed_ref[:, start : start + width]
+            parts.append(handed_ref[:, start : start + width].astype(F32)[:, None, :])
+        run_kv = jnp.concatenate(parts, axis=1).astype(out_ref.dtype)
+        out_ref[0, i * run : (i + 1) * run] = run_kv
 
 
 def shards(
@@ -367,7 +370,7 @@
         )
         tp_count = lax.axis_size("tp")
         delta = back.astype(F32)
-        for shift in range(1, tp_count):
+        for shift in sorted(range(1, tp_count), key=lambda shift: -min(shift, tp_count - shift)):
             pairs = [(i, (i + shift) % tp_count) for i in range(tp_count)]
             delta = delta + lax.ppermute(back, "tp", pairs).astype(F32)
         delta = delta.transpose(1, 0, 2).reshape(steps, requests, width)

time: 82.4 us -> 82.5 us (level)
  no operation moved by 1% of the time
where the time goes in v5:
time: 82.5 us; the launch traced here: 82.1 us
  blocking collectives  42.2 us (51%)
  starting transfers between devices  19.9 us (24%)
  Pallas kernels  6.44 us (8%)
  waiting for transfers between devices  5.47 us (7%)
  matrix products  4.35 us (5%)
  local copies, waits for them, and re-layouts  1.39 us (2%)
  other arithmetic  1.39 us (2%)
    all_to_all x1, blocking collectives, attend(): lax.all_to_all(partial.reshape(exchanged), 'z', split_axis=0, concat_axis...  16.9 us
    all_to_all x1, blocking collectives, gather(): lax.all_to_all(attended, 'z', split_axis=0, concat_axis=0, tiled=True)  14.5 us
    all_to_all x1, blocking collectives, finish(): lax.all_to_all(partial.reshape(Z, rows, chunk), 'z', split_axis=0, concat...  10.7 us
    all_to_all x1, starting transfers between devices, project(): lax.all_to_all(spread, 'z', split_axis=0, concat_axis=0, tiled=True)  8.32 us
    ppermute x3, starting transfers between devices, finish(): delta = delta + lax.ppermute(back, 'tp', pairs).astype(F32)  5.42 us
    ppermute x3, starting transfers between devices, shards(): arrived_weights[shift - 1] = lax.ppermute(q_weight, ('role', 'y'), pairs)  4.83 us
    all_to_all x1, waiting for transfers between devices, project(): lax.all_to_all(spread, 'z', split_axis=0, concat_axis=0, tiled=True)  3.87 us
    dot_general x1, matrix products, project(): jnp.einsum('rd,dcw->crw', normed, kv_weight, preferred_element_type=F32)  3.33 us
  transfers between devices with their start and end apart: 8, of which 2 were waited for; matrix products, arithmetic and copies ran while one was open for 5% of the time, Pallas kernels for 4%

profile of v5, /device:TPU:1, one launch (start us, length us, event | category | flops | bytes accessed | tf_op | source)
XLA Modules:
  0.0 82.1 jit_solution(15626347186834904640)
XLA Ops:
  0.6 3.3 %collective-permute-start.6 = (bf16[160,2048]{1,0:T(8,128)(2,1)}, bf16[160,2048]{1,0:T(8,128)(2,1)S(1)}, u32[]{:S(2)}, u32[]{:S(2)}) collective-permute-start(bf16[160,2048]{1,0:T(8,128)(2,1)} %param.25), channel_id=1, source_target_pairs={{0,140},{4,128},{8,132},{12,136},{128,0},{132,4},{136,8},{140,12},... | collective-permute-start | bytes 1966088 | tf_op jit(solution)/shard_map/ppermute | solution.py:278
  3.9 0.7 collective-permute-start.7
  4.6 0.9 %collective-permute-start.8 = (bf16[160,2048]{1,0:T(8,128)(2,1)}, bf16[160,2048]{1,0:T(8,128)(2,1)}, u32[]{:S(2)}, u32[]{:S(2)}) collective-permute-start(bf16[160,2048]{1,0:T(8,128)(2,1)} %param.25), channel_id=1, source_target_pairs={{0,132},{4,136},{8,140},{12,128},{128,0},{132,4},{136,8},{140,12},... | collective-permute-start | bytes 1966088 | tf_op jit(solution)/shard_map/ppermute | solution.py:278
  5.5 0.0 copy-start.2
  5.5 0.0 copy-start.7
  5.5 0.0 copy-start.12
  5.5 18.5 %conditional.4 = (bf16[128,640]{1,0:T(8,128)(2,1)S(1)}, f32[16,128]{1,0:T(8,128)S(1)}, f32[16,128]{1,0:T(8,128)S(1)}, bf16[16,256]{1,0:T(8,128)(2,1)S(1)}, bf16[...) conditional(s32[]{:T(128)} %convert_element_type.72, ...), branch_computations={%region_0.0_spmd, %region_2.6_spmd} | conditional | flops 1487554176 | bytes 15732424 | solution.py:312
  5.5 1.9 %branch_0_fun.4 = (bf16[8,16,640]{2,1,0:T(8,128)(2,1)}, bf16[16,5120]{1,0:T(8,128)(2,1)S(1)}, bf16[256,2,256]{2,1,0:T(2,128)(2,1)S(1)}, bf16[32,16,512]{2,1,0:T(8,128)(2,1)}) custom-call(s32[1]{0:T(128)} %bitcast.y_ref, bf16[4,4,5120]{2,1,0:T(4,128)(2,1)} %get-tuple-element.77.hidden_ref, f32[1,5120]{1,0:T(1,128)} %bitcast.73), custom_call_target="tpu_custom_call" | custom-call | tf_op jit(solution)/shard_map/cond/branch_0_fun/pallas_call | solution.py:281
  7.4 0.0 copy-start.8
  7.4 8.3 %all-to-all-start.2 = ((bf16[8,16,640]{2,1,0:T(8,128)(2,1)}), bf16[8,16,640]{2,1,0:T(8,128)(2,1)S(1)}, u32[]{:S(2)}, u32[]{:S(2)}) async-start(bf16[8,16,640]{2,1,0:T(8,128)(2,1)} %get-tuple-element.79), calls=%async_computation.2 | async-start | bytes 327680 | tf_op jit(solution)/shard_map/cond/branch_0_fun/all_to_all | solution.py:297
  15.7 0.0 copy-start.10
  15.7 0.0 copy-start.4
  15.8 3.3 %fusion.2 = f32[2,16,256]{2,1,0:T(8,128)S(1)} fusion(bf16[5120,2,256]{2,1,0:T(2,128)(2,1)} %get-tuple-element.233, bf16[16,5120]{1,0:T(8,128)(2,1)S(1)} %get-tuple-element.81), kind=kOutput, calls=%fused_computation.2 | convolution fusion | flops 83886080 | bytes 5439488 | tf_op jit(solution)/shard_map/cond/branch_0_fun/rd,dcw->crw/dot_general | solution.py:302
  19.1 0.1 multiply_reduce_fusion
  19.2 0.0 copy-done.8
  19.2 0.1 convert_element_type.55
  19.3 0.0 copy-done.10
  19.3 0.1 multiply_multiply_fusion
  19.4 0.1 fusion.7
  19.5 0.1 subtract_convert_fusion
  19.6 0.1 pad_maximum_fusion
  19.7 0.1 pad_maximum_fusion.2
  19.8 0.2 copy.39
  20.0 0.0 copy-done.4
  20.0 0.1 copy.42
  20.1 3.9 %all-to-all-done.2 = bf16[8,16,640]{2,1,0:T(8,128)(2,1)S(1)} async-done(((bf16[8,16,640]{2,1,0:T(8,128)(2,1)}), bf16[8,16,640]{2,1,0:T(8,128)(2,1)S(1)}, u32[]{:S(2)}, u32[]{:S(2)}) %all-to-all-start.2) | async-done | bytes 163872 | tf_op jit(solution)/shard_map/cond/branch_0_fun/all_to_all | solution.py:297
  24.0 0.0 copy-start
  24.0 0.0 collective-permute-done.6
  24.0 0.0 collective-permute-done.7
  24.0 0.0 collective-permute-done.8
  24.0 0.0 copy-done.2
  24.0 0.0 copy-done.7
  24.0 0.0 copy-done.12
  24.1 0.7 copy-done
  24.7 20.5 %conditional.5 = (bf16[704,2048]{1,0:T(8,128)(2,1)}, bf16[8,16,2048]{2,1,0:T(8,128)(2,1)S(1)}) conditional(s32[]{:T(128)} %convert_element_type.72, (bf16[128,640]{1,0:T(8,128)(2,1)S(1)}, bf16[160,2048]{1,0:T(8,128)(2,1)S(1)}, bf16[160,2048]{1,0:T(8,128)(2,1)S(1)}, bf16[160,2048]{1,0:T(8,128)(2,1)S(1)}, bf16[160,2048]{1,0:T(8,128)(2,1)}, ...), branch_computations={%region_6.7_spmd, %region_7.10_spmd} | conditional | flops 135761232 | bytes 22605258 | solution.py:347
  24.7 0.0 copy-start.9
  24.7 1.7 %branch_0_fun.5 = bf16[128,2048]{1,0:T(8,128)(2,1)S(1)} custom-call(bf16[128,640]{1,0:T(8,128)(2,1)S(1)} %get-tuple-element.94.rows_ref, bf16[160,2048]{1,0:T(8,128)(2,1)S(1)} %get-tuple-element.95.own_ref, bf16[160,2048]{1,0:T(8,128)(2,1)S(1)} %get-tuple-element.96.first_ref, bf16[160,2048]{1,0:T(8,128)(2,1)S(1)} %get-tuple-element.97.second_ref, ...), custom_call_target="tpu_custom_call" | custom-call | tf_op jit(solution)/shard_map/cond/branch_0_fun/pallas_call | solution.py:315
  26.4 16.9 %all_to_all.20.returned_ref = bf16[8,16,2048]{2,1,0:T(8,128)(2,1)S(1)} all-to-all(bf16[8,16,2048]{2,1,0:T(8,128)(2,1)S(1)} %bitcast.56), channel_id=1, replica_groups=mesh['role'=2,'z'=8,'y'=4,'tp'=4] {'z'}, dimensions={0} | all-to-all | bytes 1048576 | tf_op jit(solution)/shard_map/cond/branch_0_fun/all_to_all | solution.py:322
  43.4 0.0 copy-done.9
  43.4 1.7 %branch_0_fun.6 = (bf16[8,16,2048]{2,1,0:T(8,128)(2,1)S(1)}, bf16[704,2048]{1,0:T(8,128)(2,1)}) custom-call(s32[4]{0:T(128)S(1)} %copy-done.9, bf16[8,16,2048]{2,1,0:T(8,128)(2,1)S(1)} %all_to_all.20.returned_ref, f32[1,128]{1,0:T(1,128)S(1)} %bitcast.74, f32[16,128]{1,0:T(8,128)S(1)} %get-tuple-element.100.cosine_ref, ...), custom_call_target="tpu_custom_call" | custom-call | tf_op jit(solution)/shard_map/cond/branch_0_fun/pallas_call | solution.py:325
  45.3 1.3 %collective-permute-start.9 = (bf16[704,2048]{1,0:T(8,128)(2,1)}, bf16[704,2048]{1,0:T(8,128)(2,1)S(1)}, u32[]{:S(2)}, u32[]{:S(2)}) collective-permute-start(bf16[704,2048]{1,0:T(8,128)(2,1)} %get-tuple-element.140), channel_id=1, source_target_pairs={{0,128},{1,129},{2,130},{3,131},{4,132},{5,133},{6,134},{7,135},{8... | collective-permute-start | bytes 8650760 | tf_op jit(solution)/shard_map/ppermute | solution.py:351
  46.6 14.6 %conditional.6 = (bf16[8,16,2048]{2,1,0:T(8,128)(2,1)S(1)}) conditional(s32[]{:T(128)} %convert_element_type.72, bf16[8,16,2048]{2,1,0:T(8,128)(2,1)S(1)} %get-tuple-element.141, bf16[8,16,2048]{2,1,0:T(8,128)(2,1)S(1)} %get-tuple-element.141), branch_computations={%region_10.11_spmd, %region_11.12_spmd} | conditional | bytes 2097160 | solution.py:356
  46.6 14.5 %all_to_all.21 = bf16[8,16,2048]{2,1,0:T(8,128)(2,1)S(1)} all-to-all(bf16[8,16,2048]{2,1,0:T(8,128)(2,1)S(1)} %copy.89), channel_id=1, replica_groups=mesh['role'=2,'z'=8,'y'=4,'tp'=4] {'z'}, dimensions={0} | all-to-all | bytes 1048576 | tf_op jit(solution)/shard_map/cond/branch_0_fun/all_to_all | solution.py:354
  61.2 0.0 collective-permute-done.9
  61.2 20.9 %conditional.7 = (bf16[1,256,2,256]{3,2,1,0:T(2,128)(2,1)}, bf16[1,4,4,5120]{3,2,1,0:T(4,128)(2,1)}) conditional(s32[]{:T(128)} %convert_element_type.72, (bf16[704,2048]{1,0:T(8,128)(2,1)S(1)}, bf16[4,4,5120]{2,1,0:T(4,128)(2,1)}, bf16[8,16,2048]{2,1,0:T(8,128)(2,1)S(1)}) %tuple.41, bf16[256,2,256]{0,2,1:T(8,128)(2,1)} %copy-done), branch_computations={%region_12.13_spmd, %region_13.14_spmd} | conditional | flops 369836032 | bytes 9978020 | solution.py:399
  61.2 0.0 copy-start.1
  61.2 1.0 %fusion.34 = bf16[128,704]{1,0:T(8,128)(2,1)S(1)} fusion(bf16[128,2048]{1,0:T(8,128)(2,1)S(1)} %bitcast.59, bf16[704,2048]{1,0:T(8,128)(2,1)S(1)} %get-tuple-element.114.handed_ref), kind=kOutput, calls=%fused_computation.81 | convolution fusion | flops 369098752 | bytes 3588096 | tf_op jit(solution)/shard_map/cond/branch_0_fun/dot_general | solution.py:362
  62.2 10.7 %all_to_all.22 = bf16[8,16,640]{2,1,0:T(8,128)(2,1)S(1)} all-to-all(bf16[8,16,640]{2,1,0:T(8,128)(2,1)S(1)} %bitcast.66), channel_id=1, replica_groups=mesh['role'=2,'z'=8,'y'=4,'tp'=4] {'z'}, dimensions={0} | all-to-all | bytes 327680 | tf_op jit(solution)/shard_map/cond/branch_0_fun/all_to_all | solution.py:368
  72.9 2.7 %collective-permute-start.3 = (bf16[8,16,640]{2,1,0:T(8,128)(2,1)S(1)}, bf16[8,16,640]{2,1,0:T(8,128)(2,1)S(1)}, u32[]{:S(2)}, u32[]{:S(2)}) collective-permute-start(bf16[8,16,640]{2,1,0:T(8,128)(2,1)S(1)} %all_to_all.22), channel_id=1, source_target_pairs={{0,2},{1,3},{2,0},{3,1},{4,6},{5,7},{6,4},{7,5},{8,10},{9,11},{10,... | collective-permute-start | bytes 491528 | tf_op jit(solution)/shard_map/cond/branch_0_fun/ppermute | solution.py:375
  75.7 0.3 collective-permute-start.4
  76.0 2.4 %collective-permute-start.5 = (bf16[8,16,640]{2,1,0:T(8,128)(2,1)S(1)}, bf16[8,16,640]{2,1,0:T(8,128)(2,1)S(1)}, u32[]{:S(2)}, u32[]{:S(2)}) collective-permute-start(bf16[8,16,640]{2,1,0:T(8,128)(2,1)S(1)} %all_to_all.22), channel_id=1, source_target_pairs={{0,3},{1,0},{2,1},{3,2},{4,7},{5,4},{6,5},{7,6},{8,11},{9,8},{10,9... | collective-permute-start | bytes 491528 | tf_op jit(solution)/shard_map/cond/branch_0_fun/ppermute | solution.py:375
  78.3 0.0 copy-done.1
  78.3 1.1 %branch_0_fun.7 = (bf16[1,256,2,256]{3,2,1,0:T(2,128)(2,1)}, f32[4,4,5120]{2,1,0:T(4,128)S(1)}) custom-call(bf16[704,2048]{1,0:T(8,128)(2,1)S(1)} %get-tuple-element.114.handed_ref, bf16[4,4,5120]{2,1,0:T(4,128)(2,1)S(1)} %copy-done.1), custom_call_target="tpu_custom_call" | custom-call | tf_op jit(solution)/shard_map/cond/branch_0_fun/pallas_call | solution.py:377
  79.5 0.0 collective-permute-done.3
  79.5 1.6 %collective-permute-done.4 = bf16[8,16,640]{2,1,0:T(8,128)(2,1)S(1)} collective-permute-done((bf16[8,16,640]{2,1,0:T(8,128)(2,1)S(1)}, bf16[8,16,640]{2,1,0:T(8,128)(2,1)S(1)}, u32[]{:S(2)}, u32[]{:S(2)}) %collective-permute-start.4) | collective-permute-done | bytes 163872 | tf_op jit(solution)/shard_map/cond/branch_0_fun/ppermute | solution.py:375
  81.0 0.0 collective-permute-done.5
  81.0 0.1 add_bitcast_fusion
  81.1 0.1 copy.40
  81.2 0.1 reshape.307
  81.4 0.8 fusion.31
  (10 shorter events, 0.1 us)
Async XLA Ops:
  0.6 23.4 %collective-permute-start.6 = (bf16[160,2048]{1,0:T(8,128)(2,1)}, bf16[160,2048]{1,0:T(8,128)(2,1)S(1)}, u32[]{:S(2)}, u32[]{:S(2)}) collective-permute-start(bf16[160,2048]{1,0:T(8,128)(2,1)} %param.25), channel_id=1, source_target_pairs={{0,140},{4,128},{8,132},{12,136},{128,0},{132,4},{136,8},{140,12},... | collective-permute-start | bytes 1966088 | tf_op jit(solution)/shard_map/ppermute | solution.py:278
  3.9 20.1 %collective-permute-start.7 = (bf16[160,2048]{1,0:T(8,128)(2,1)}, bf16[160,2048]{1,0:T(8,128)(2,1)S(1)}, u32[]{:S(2)}, u32[]{:S(2)}) collective-permute-start(bf16[160,2048]{1,0:T(8,128)(2,1)} %param.25), channel_id=1, source_target_pairs={{0,136},{4,140},{8,128},{12,132},{128,0},{132,4},{136,8},{140,12},... | collective-permute-start | bytes 1966088 | tf_op jit(solution)/shard_map/ppermute | solution.py:278
  4.6 19.4 %collective-permute-start.8 = (bf16[160,2048]{1,0:T(8,128)(2,1)}, bf16[160,2048]{1,0:T(8,128)(2,1)}, u32[]{:S(2)}, u32[]{:S(2)}) collective-permute-start(bf16[160,2048]{1,0:T(8,128)(2,1)} %param.25), channel_id=1, source_target_pairs={{0,132},{4,136},{8,140},{12,128},{128,0},{132,4},{136,8},{140,12},... | collective-permute-start | bytes 1966088 | tf_op jit(solution)/shard_map/ppermute | solution.py:278
  5.5 18.6 %copy-start.2 = (bf16[160,2048]{1,0:T(8,128)(2,1)S(1)}, bf16[160,2048]{1,0:T(8,128)(2,1)}, u32[]{:S(2)}) copy-start(bf16[160,2048]{1,0:T(8,128)(2,1)} %param.25) | copy-start | bytes 1966084
  5.5 18.6 %copy-start.7 = (s32[32,32]{1,0:T(8,128)S(1)}, s32[32,32]{1,0:T(8,128)}, u32[]{:S(2)}) copy-start(s32[32,32]{1,0:T(8,128)} %param.31) | copy-start | bytes 12292
  5.5 18.6 %copy-start.12 = (f32[128]{0:T(128)S(1)}, f32[128]{0:T(128)}, u32[]{:S(2)}) copy-start(f32[128]{0:T(128)} %param.23) | copy-start | bytes 1540
  7.4 11.8 %copy-start.8 = (s32[4]{0:T(128)S(1)}, s32[4]{0:T(128)}, u32[]{:S(2)}) copy-start(s32[4]{0:T(128)} %get-tuple-element.80) | copy-start | bytes 52 | tf_op jit(solution)/shard_map/cond
  7.4 16.6 %all-to-all-start.2 = ((bf16[8,16,640]{2,1,0:T(8,128)(2,1)}), bf16[8,16,640]{2,1,0:T(8,128)(2,1)S(1)}, u32[]{:S(2)}, u32[]{:S(2)}) async-start(bf16[8,16,640]{2,1,0:T(8,128)(2,1)} %get-tuple-element.79), calls=%async_computation.2 | async-start | bytes 327680 | tf_op jit(solution)/shard_map/cond/branch_0_fun/all_to_all | solution.py:297
  15.7 3.6 %copy-start.10 = (f32[128]{0:T(128)S(1)}, f32[128]{0:T(128)}, u32[]{:S(2)}) copy-start(f32[128]{0:T(128)} %get-tuple-element.83) | copy-start | bytes 1540 | tf_op jit(solution)/shard_map/cond
  15.7 4.3 %copy-start.4 = (bf16[4,128,2,256]{3,2,1,0:T(2,128)(2,1)S(1)}, bf16[4,128,2,256]{3,2,1,0:T(2,128)(2,1)}, u32[]{:S(2)}) copy-start(bf16[4,128,2,256]{3,2,1,0:T(2,128)(2,1)} %get-tuple-element.235) | copy-start | bytes 1572868 | tf_op jit(solution)/shard_map/cond
  24.0 0.7 copy-start
  24.7 18.6 %copy-start.9 = (s32[4]{0:T(128)S(1)}, s32[4]{0:T(128)}, u32[]{:S(2)}) copy-start(s32[4]{0:T(128)} %get-tuple-element.93.length_ref) | copy-start | bytes 52 | tf_op jit(solution)/shard_map/cond
  45.3 15.9 %collective-permute-start.9 = (bf16[704,2048]{1,0:T(8,128)(2,1)}, bf16[704,2048]{1,0:T(8,128)(2,1)S(1)}, u32[]{:S(2)}, u32[]{:S(2)}) collective-permute-start(bf16[704,2048]{1,0:T(8,128)(2,1)} %get-tuple-element.140), channel_id=1, source_target_pairs={{0,128},{1,129},{2,130},{3,131},{4,132},{5,133},{6,134},{7,135},{8... | collective-permute-start | bytes 8650760 | tf_op jit(solution)/shard_map/ppermute | solution.py:351
  61.2 17.1 %copy-start.1 = (bf16[4,4,5120]{2,1,0:T(4,128)(2,1)S(1)}, bf16[4,4,5120]{2,1,0:T(4,128)(2,1)}, u32[]{:S(2)}) copy-start(bf16[4,4,5120]{2,1,0:T(4,128)(2,1)} %get-tuple-element.115.hidden_ref) | copy-start | bytes 491524 | tf_op jit(solution)/shard_map/cond
  72.9 6.5 %collective-permute-start.3 = (bf16[8,16,640]{2,1,0:T(8,128)(2,1)S(1)}, bf16[8,16,640]{2,1,0:T(8,128)(2,1)S(1)}, u32[]{:S(2)}, u32[]{:S(2)}) collective-permute-start(bf16[8,16,640]{2,1,0:T(8,128)(2,1)S(1)} %all_to_all.22), channel_id=1, source_target_pairs={{0,2},{1,3},{2,0},{3,1},{4,6},{5,7},{6,4},{7,5},{8,10},{9,11},{10,... | collective-permute-start | bytes 491528 | tf_op jit(solution)/shard_map/cond/branch_0_fun/ppermute | solution.py:375
  75.7 5.4 %collective-permute-start.4 = (bf16[8,16,640]{2,1,0:T(8,128)(2,1)S(1)}, bf16[8,16,640]{2,1,0:T(8,128)(2,1)S(1)}, u32[]{:S(2)}, u32[]{:S(2)}) collective-permute-start(bf16[8,16,640]{2,1,0:T(8,128)(2,1)S(1)} %all_to_all.22), channel_id=1, source_target_pairs={{0,1},{1,2},{2,3},{3,0},{4,5},{5,6},{6,7},{7,4},{8,9},{9,10},{10,1... | collective-permute-start | bytes 491528 | tf_op jit(solution)/shard_map/cond/branch_0_fun/ppermute | solution.py:375
  76.0 5.1 %collective-permute-start.5 = (bf16[8,16,640]{2,1,0:T(8,128)(2,1)S(1)}, bf16[8,16,640]{2,1,0:T(8,128)(2,1)S(1)}, u32[]{:S(2)}, u32[]{:S(2)}) collective-permute-start(bf16[8,16,640]{2,1,0:T(8,128)(2,1)S(1)} %all_to_all.22), channel_id=1, source_target_pairs={{0,3},{1,0},{2,1},{3,2},{4,7},{5,4},{6,5},{7,6},{8,11},{9,8},{10,9... | collective-permute-start | bytes 491528 | tf_op jit(solution)/shard_map/cond/branch_0_fun/ppermute | solution.py:375

commit v6 on v5

--- a/solution.py
+++ b/solution.py
@@ -68,14 +68,23 @@
         spread_ref[z] = pltpu.roll(block, shift, axis=1).astype(BF16)
 
 
-def query_kernel(rows_ref, own_ref, first_ref, second_ref, third_ref, out_ref):
+def query_kernel(
+    rows_ref, own_ref, first_ref, second_ref, third_ref, out_ref, last_ref, total_ref, semaphore
+):
+    copy = pltpu.make_async_copy(third_ref, last_ref, semaphore)
+    copy.start()
     tile = 512
-    for start in range(0, out_ref.shape[1], tile):
-        columns = slice(start, start + tile)
+    depth = 3 * own_ref.shape[0]
+    tiles = [slice(start, start + tile) for start in range(0, out_ref.shape[1], tile)]
+    for columns in tiles:
         weight = jnp.concatenate(
-            [ref[:, columns] for ref in (own_ref, first_ref, second_ref, third_ref)], axis=0
-        )
-        out_ref[:, columns] = dot(rows_ref[...], weight).astype(BF16)
+            [ref[:, columns] for ref in (own_ref, first_ref, second_ref)], axis=0
+        )
+        total_ref[:, columns] = dot(rows_ref[:, :depth], weight)
+    copy.wait()
+    for columns in tiles:
+        last = dot(rows_ref[:, depth:], last_ref[:, columns])
+        out_ref[:, columns] = (total_ref[:, columns] + last).astype(BF16)
 
 
 def attention_kernel(
@@ -206,7 +215,7 @@
     exchanged = (Z, rows, local_query)
 
     whole = pl.BlockSpec(memory_space=pltpu.VMEM)
-    unwritten = pl.BlockSpec(memory_space=pl.ANY)
+    unwritten = anywhere = pl.BlockSpec(memory_space=pl.ANY)
     section = jax.ShapeDtypeStruct((span_rows, 2, local_width), BF16)
     buffer = jax.ShapeDtypeStruct((seq_count, CAPACITY * BLOCK_TOKENS, 2 * local_width), BF16)
 
@@ -314,9 +323,14 @@
     def attend(payload, spread, cosine, sine, new_keys, new_values, keys, values, *weights):
         partial = pl.pallas_call(
             query_kernel,
-            in_specs=[whole] * 5,
+            in_specs=[whole] * 4 + [anywhere],
             out_specs=whole,
             out_shape=jax.ShapeDtypeStruct((Z * rows, local_query), BF16),
+            scratch_shapes=[
+                pltpu.VMEM((depth, local_query), BF16),
+                pltpu.VMEM((Z * rows, local_query), F32),
+                pltpu.SemaphoreType.DMA,
+            ],
             compiler_params=pltpu.CompilerParams(vmem_limit_bytes=VMEM_LIMIT),
         )(spread, q_weight, *weights)
         returned = lax.all_to_all(

time: 82.5 us -> 82.2 us (level)
  no operation moved by 1% of the time
where the time goes in v6:
time: 82.2 us; the launch traced here: 81.9 us
  blocking collectives  42.1 us (51%)
  starting transfers between devices  19.9 us (24%)
  Pallas kernels  6.23 us (8%)
  waiting for transfers between devices  5.47 us (7%)
  matrix products  4.35 us (5%)
  local copies, waits for them, and re-layouts  1.39 us (2%)
  other arithmetic  1.39 us (2%)
    all_to_all x1, blocking collectives, attend(): lax.all_to_all(partial.reshape(exchanged), 'z', split_axis=0, concat_axis...  16.9 us
    all_to_all x1, blocking collectives, gather(): lax.all_to_all(attended, 'z', split_axis=0, concat_axis=0, tiled=True)  14.5 us
    all_to_all x1, blocking collectives, finish(): lax.all_to_all(partial.reshape(Z, rows, chunk), 'z', split_axis=0, concat...  10.7 us
    all_to_all x1, starting transfers between devices, project(): lax.all_to_all(spread, 'z', split_axis=0, concat_axis=0, tiled=True)  8.32 us
    ppermute x3, starting transfers between devices, finish(): delta = delta + lax.ppermute(back, 'tp', pairs).astype(F32)  5.42 us
    ppermute x3, starting transfers between devices, shards(): arrived_weights[shift - 1] = lax.ppermute(q_weight, ('role', 'y'), pairs)  4.83 us
    all_to_all x1, waiting for transfers between devices, project(): lax.all_to_all(spread, 'z', split_axis=0, concat_axis=0, tiled=True)  3.87 us
    dot_general x1, matrix products, project(): jnp.einsum('rd,dcw->crw', normed, kv_weight, preferred_element_type=F32)  3.33 us
  transfers between devices with their start and end apart: 8, of which 2 were waited for; matrix products, arithmetic and copies ran while one was open for 5% of the time, Pallas kernels for 4%

profile of v6, /device:TPU:1, one launch (start us, length us, event | category | flops | bytes accessed | tf_op | source)
XLA Modules:
  0.0 81.9 jit_solution(12270531486346242764)
XLA Ops:
  0.6 3.3 %collective-permute-start.6 = (bf16[160,2048]{1,0:T(8,128)(2,1)}, bf16[160,2048]{1,0:T(8,128)(2,1)S(1)}, u32[]{:S(2)}, u32[]{:S(2)}) collective-permute-start(bf16[160,2048]{1,0:T(8,128)(2,1)} %param.25), channel_id=1, source_target_pairs={{0,140},{4,128},{8,132},{12,136},{128,0},{132,4},{136,8},{140,12},... | collective-permute-start | bytes 1966088 | tf_op jit(solution)/shard_map/ppermute | solution.py:287
  3.9 0.7 collective-permute-start.7
  4.6 0.9 %collective-permute-start.8 = (bf16[160,2048]{1,0:T(8,128)(2,1)}, bf16[160,2048]{1,0:T(8,128)(2,1)}, u32[]{:S(2)}, u32[]{:S(2)}) collective-permute-start(bf16[160,2048]{1,0:T(8,128)(2,1)} %param.25), channel_id=1, source_target_pairs={{0,132},{4,136},{8,140},{12,128},{128,0},{132,4},{136,8},{140,12},... | collective-permute-start | bytes 1966088 | tf_op jit(solution)/shard_map/ppermute | solution.py:287
  5.5 0.0 copy-start.2
  5.5 0.0 copy-start.7
  5.5 0.0 copy-start.12
  5.5 18.5 %conditional.4 = (bf16[128,640]{1,0:T(8,128)(2,1)S(1)}, f32[16,128]{1,0:T(8,128)S(1)}, f32[16,128]{1,0:T(8,128)S(1)}, bf16[16,256]{1,0:T(8,128)(2,1)S(1)}, bf16[...) conditional(s32[]{:T(128)} %convert_element_type.72, ...), branch_computations={%region_0.0_spmd, %region_2.6_spmd} | conditional | flops 1487554176 | bytes 15732424 | solution.py:321
  5.5 1.9 %branch_0_fun.4 = (bf16[8,16,640]{2,1,0:T(8,128)(2,1)}, bf16[16,5120]{1,0:T(8,128)(2,1)S(1)}, bf16[256,2,256]{2,1,0:T(2,128)(2,1)S(1)}, bf16[32,16,512]{2,1,0:T(8,128)(2,1)}) custom-call(s32[1]{0:T(128)} %bitcast.y_ref, bf16[4,4,5120]{2,1,0:T(4,128)(2,1)} %get-tuple-element.77.hidden_ref, f32[1,5120]{1,0:T(1,128)} %bitcast.73), custom_call_target="tpu_custom_call" | custom-call | tf_op jit(solution)/shard_map/cond/branch_0_fun/pallas_call | solution.py:290
  7.4 0.0 copy-start.8
  7.4 8.3 %all-to-all-start.2 = ((bf16[8,16,640]{2,1,0:T(8,128)(2,1)}), bf16[8,16,640]{2,1,0:T(8,128)(2,1)S(1)}, u32[]{:S(2)}, u32[]{:S(2)}) async-start(bf16[8,16,640]{2,1,0:T(8,128)(2,1)} %get-tuple-element.79), calls=%async_computation.2 | async-start | bytes 327680 | tf_op jit(solution)/shard_map/cond/branch_0_fun/all_to_all | solution.py:306
  15.7 0.0 copy-start.10
  15.7 0.0 copy-start.4
  15.8 3.3 %fusion.2 = f32[2,16,256]{2,1,0:T(8,128)S(1)} fusion(bf16[5120,2,256]{2,1,0:T(2,128)(2,1)} %get-tuple-element.233, bf16[16,5120]{1,0:T(8,128)(2,1)S(1)} %get-tuple-element.81), kind=kOutput, calls=%fused_computation.2 | convolution fusion | flops 83886080 | bytes 5439488 | tf_op jit(solution)/shard_map/cond/branch_0_fun/rd,dcw->crw/dot_general | solution.py:311
  19.1 0.1 multiply_reduce_fusion
  19.2 0.0 copy-done.8
  19.2 0.1 convert_element_type.55
  19.3 0.0 copy-done.10
  19.3 0.1 multiply_multiply_fusion
  19.4 0.1 fusion.7
  19.5 0.1 subtract_convert_fusion
  19.6 0.1 pad_maximum_fusion
  19.7 0.1 pad_maximum_fusion.2
  19.8 0.2 copy.39
  20.0 0.0 copy-done.4
  20.0 0.1 copy.42
  20.1 3.9 %all-to-all-done.2 = bf16[8,16,640]{2,1,0:T(8,128)(2,1)S(1)} async-done(((bf16[8,16,640]{2,1,0:T(8,128)(2,1)}), bf16[8,16,640]{2,1,0:T(8,128)(2,1)S(1)}, u32[]{:S(2)}, u32[]{:S(2)}) %all-to-all-start.2) | async-done | bytes 163872 | tf_op jit(solution)/shard_map/cond/branch_0_fun/all_to_all | solution.py:306
  24.0 0.0 copy-start
  24.0 0.0 collective-permute-done.6
  24.0 0.0 collective-permute-done.7
  24.0 0.0 collective-permute-done.8
  24.0 0.0 copy-done.2
  24.0 0.0 copy-done.7
  24.0 0.0 copy-done.12
  24.1 0.7 copy-done
  24.7 20.3 %conditional.5 = (bf16[704,2048]{1,0:T(8,128)(2,1)}, bf16[8,16,2048]{2,1,0:T(8,128)(2,1)S(1)}) conditional(s32[]{:T(128)} %convert_element_type.72, (bf16[128,640]{1,0:T(8,128)(2,1)S(1)}, bf16[160,2048]{1,0:T(8,128)(2,1)S(1)}, bf16[160,2048]{1,0:T(8,128)(2,1)S(1)}, bf16[160,2048]{1,0:T(8,128)(2,1)S(1)}, bf16[160,2048]{1,0:T(8,128)(2,1)}, ...), branch_computations={%region_6.7_spmd, %region_7.10_spmd} | conditional | flops 135761232 | bytes 22605258 | solution.py:361
  24.7 0.0 copy-start.9
  24.7 1.5 %branch_0_fun.5 = bf16[128,2048]{1,0:T(8,128)(2,1)S(1)} custom-call(bf16[128,640]{1,0:T(8,128)(2,1)S(1)} %get-tuple-element.94.rows_ref, bf16[160,2048]{1,0:T(8,128)(2,1)S(1)} %get-tuple-element.95.own_ref, bf16[160,2048]{1,0:T(8,128)(2,1)S(1)} %get-tuple-element.96.first_ref, bf16[160,2048]{1,0:T(8,128)(2,1)S(1)} %get-tuple-element.97.second_ref, ...), custom_call_target="tpu_custom_call" | custom-call | tf_op jit(solution)/shard_map/cond/branch_0_fun/pallas_call | solution.py:324
  26.2 16.9 %all_to_all.20.returned_ref = bf16[8,16,2048]{2,1,0:T(8,128)(2,1)S(1)} all-to-all(bf16[8,16,2048]{2,1,0:T(8,128)(2,1)S(1)} %bitcast.56), channel_id=1, replica_groups=mesh['role'=2,'z'=8,'y'=4,'tp'=4] {'z'}, dimensions={0} | all-to-all | bytes 1048576 | tf_op jit(solution)/shard_map/cond/branch_0_fun/all_to_all | solution.py:336
  43.1 0.0 copy-done.9
  43.1 1.7 %branch_0_fun.6 = (bf16[8,16,2048]{2,1,0:T(8,128)(2,1)S(1)}, bf16[704,2048]{1,0:T(8,128)(2,1)}) custom-call(s32[4]{0:T(128)S(1)} %copy-done.9, bf16[8,16,2048]{2,1,0:T(8,128)(2,1)S(1)} %all_to_all.20.returned_ref, f32[1,128]{1,0:T(1,128)S(1)} %bitcast.74, f32[16,128]{1,0:T(8,128)S(1)} %get-tuple-element.100.cosine_ref, ...), custom_call_target="tpu_custom_call" | custom-call | tf_op jit(solution)/shard_map/cond/branch_0_fun/pallas_call | solution.py:339
  45.0 1.3 %collective-permute-start.9 = (bf16[704,2048]{1,0:T(8,128)(2,1)}, bf16[704,2048]{1,0:T(8,128)(2,1)S(1)}, u32[]{:S(2)}, u32[]{:S(2)}) collective-permute-start(bf16[704,2048]{1,0:T(8,128)(2,1)} %get-tuple-element.140), channel_id=1, source_target_pairs={{0,128},{1,129},{2,130},{3,131},{4,132},{5,133},{6,134},{7,135},{8... | collective-permute-start | bytes 8650760 | tf_op jit(solution)/shard_map/ppermute | solution.py:365
  46.3 14.6 %conditional.6 = (bf16[8,16,2048]{2,1,0:T(8,128)(2,1)S(1)}) conditional(s32[]{:T(128)} %convert_element_type.72, bf16[8,16,2048]{2,1,0:T(8,128)(2,1)S(1)} %get-tuple-element.141, bf16[8,16,2048]{2,1,0:T(8,128)(2,1)S(1)} %get-tuple-element.141), branch_computations={%region_10.11_spmd, %region_11.12_spmd} | conditional | bytes 2097160 | solution.py:370
  46.4 14.5 %all_to_all.21 = bf16[8,16,2048]{2,1,0:T(8,128)(2,1)S(1)} all-to-all(bf16[8,16,2048]{2,1,0:T(8,128)(2,1)S(1)} %copy.89), channel_id=1, replica_groups=mesh['role'=2,'z'=8,'y'=4,'tp'=4] {'z'}, dimensions={0} | all-to-all | bytes 1048576 | tf_op jit(solution)/shard_map/cond/branch_0_fun/all_to_all | solution.py:368
  61.0 0.0 collective-permute-done.9
  61.0 20.9 %conditional.7 = (bf16[1,256,2,256]{3,2,1,0:T(2,128)(2,1)}, bf16[1,4,4,5120]{3,2,1,0:T(4,128)(2,1)}) conditional(s32[]{:T(128)} %convert_element_type.72, (bf16[704,2048]{1,0:T(8,128)(2,1)S(1)}, bf16[4,4,5120]{2,1,0:T(4,128)(2,1)}, bf16[8,16,2048]{2,1,0:T(8,128)(2,1)S(1)}) %tuple.41, bf16[256,2,256]{0,2,1:T(8,128)(2,1)} %copy-done), branch_computations={%region_12.13_spmd, %region_13.14_spmd} | conditional | flops 369836032 | bytes 9978020 | solution.py:413
  61.0 0.0 copy-start.1
  61.0 1.0 %fusion.34 = bf16[128,704]{1,0:T(8,128)(2,1)S(1)} fusion(bf16[128,2048]{1,0:T(8,128)(2,1)S(1)} %bitcast.59, bf16[704,2048]{1,0:T(8,128)(2,1)S(1)} %get-tuple-element.114.handed_ref), kind=kOutput, calls=%fused_computation.81 | convolution fusion | flops 369098752 | bytes 3588096 | tf_op jit(solution)/shard_map/cond/branch_0_fun/dot_general | solution.py:376
  62.0 10.7 %all_to_all.22 = bf16[8,16,640]{2,1,0:T(8,128)(2,1)S(1)} all-to-all(bf16[8,16,640]{2,1,0:T(8,128)(2,1)S(1)} %bitcast.66), channel_id=1, replica_groups=mesh['role'=2,'z'=8,'y'=4,'tp'=4] {'z'}, dimensions={0} | all-to-all | bytes 327680 | tf_op jit(solution)/shard_map/cond/branch_0_fun/all_to_all | solution.py:382
  72.7 2.7 %collective-permute-start.3 = (bf16[8,16,640]{2,1,0:T(8,128)(2,1)S(1)}, bf16[8,16,640]{2,1,0:T(8,128)(2,1)S(1)}, u32[]{:S(2)}, u32[]{:S(2)}) collective-permute-start(bf16[8,16,640]{2,1,0:T(8,128)(2,1)S(1)} %all_to_all.22), channel_id=1, source_target_pairs={{0,2},{1,3},{2,0},{3,1},{4,6},{5,7},{6,4},{7,5},{8,10},{9,11},{10,... | collective-permute-start | bytes 491528 | tf_op jit(solution)/shard_map/cond/branch_0_fun/ppermute | solution.py:389
  75.4 0.3 collective-permute-start.4
  75.7 2.4 %collective-permute-start.5 = (bf16[8,16,640]{2,1,0:T(8,128)(2,1)S(1)}, bf16[8,16,640]{2,1,0:T(8,128)(2,1)S(1)}, u32[]{:S(2)}, u32[]{:S(2)}) collective-permute-start(bf16[8,16,640]{2,1,0:T(8,128)(2,1)S(1)} %all_to_all.22), channel_id=1, source_target_pairs={{0,3},{1,0},{2,1},{3,2},{4,7},{5,4},{6,5},{7,6},{8,11},{9,8},{10,9... | collective-permute-start | bytes 491528 | tf_op jit(solution)/shard_map/cond/branch_0_fun/ppermute | solution.py:389
  78.1 0.0 copy-done.1
  78.1 1.1 %branch_0_fun.7 = (bf16[1,256,2,256]{3,2,1,0:T(2,128)(2,1)}, f32[4,4,5120]{2,1,0:T(4,128)S(1)}) custom-call(bf16[704,2048]{1,0:T(8,128)(2,1)S(1)} %get-tuple-element.114.handed_ref, bf16[4,4,5120]{2,1,0:T(4,128)(2,1)S(1)} %copy-done.1), custom_call_target="tpu_custom_call" | custom-call | tf_op jit(solution)/shard_map/cond/branch_0_fun/pallas_call | solution.py:391
  79.2 0.0 collective-permute-done.3
  79.2 1.6 %collective-permute-done.4 = bf16[8,16,640]{2,1,0:T(8,128)(2,1)S(1)} collective-permute-done((bf16[8,16,640]{2,1,0:T(8,128)(2,1)S(1)}, bf16[8,16,640]{2,1,0:T(8,128)(2,1)S(1)}, u32[]{:S(2)}, u32[]{:S(2)}) %collective-permute-start.4) | collective-permute-done | bytes 163872 | tf_op jit(solution)/shard_map/cond/branch_0_fun/ppermute | solution.py:389
  80.8 0.0 collective-permute-done.5
  80.8 0.1 add_bitcast_fusion
  80.9 0.1 copy.40
  81.0 0.1 reshape.307
  81.1 0.8 fusion.31
  (10 shorter events, 0.1 us)
Async XLA Ops:
  0.6 23.4 %collective-permute-start.6 = (bf16[160,2048]{1,0:T(8,128)(2,1)}, bf16[160,2048]{1,0:T(8,128)(2,1)S(1)}, u32[]{:S(2)}, u32[]{:S(2)}) collective-permute-start(bf16[160,2048]{1,0:T(8,128)(2,1)} %param.25), channel_id=1, source_target_pairs={{0,140},{4,128},{8,132},{12,136},{128,0},{132,4},{136,8},{140,12},... | collective-permute-start | bytes 1966088 | tf_op jit(solution)/shard_map/ppermute | solution.py:287
  3.9 20.1 %collective-permute-start.7 = (bf16[160,2048]{1,0:T(8,128)(2,1)}, bf16[160,2048]{1,0:T(8,128)(2,1)S(1)}, u32[]{:S(2)}, u32[]{:S(2)}) collective-permute-start(bf16[160,2048]{1,0:T(8,128)(2,1)} %param.25), channel_id=1, source_target_pairs={{0,136},{4,140},{8,128},{12,132},{128,0},{132,4},{136,8},{140,12},... | collective-permute-start | bytes 1966088 | tf_op jit(solution)/shard_map/ppermute | solution.py:287
  4.6 19.4 %collective-permute-start.8 = (bf16[160,2048]{1,0:T(8,128)(2,1)}, bf16[160,2048]{1,0:T(8,128)(2,1)}, u32[]{:S(2)}, u32[]{:S(2)}) collective-permute-start(bf16[160,2048]{1,0:T(8,128)(2,1)} %param.25), channel_id=1, source_target_pairs={{0,132},{4,136},{8,140},{12,128},{128,0},{132,4},{136,8},{140,12},... | collective-permute-start | bytes 1966088 | tf_op jit(solution)/shard_map/ppermute | solution.py:287
  5.5 18.6 %copy-start.2 = (bf16[160,2048]{1,0:T(8,128)(2,1)S(1)}, bf16[160,2048]{1,0:T(8,128)(2,1)}, u32[]{:S(2)}) copy-start(bf16[160,2048]{1,0:T(8,128)(2,1)} %param.25) | copy-start | bytes 1966084
  5.5 18.6 %copy-start.7 = (s32[32,32]{1,0:T(8,128)S(1)}, s32[32,32]{1,0:T(8,128)}, u32[]{:S(2)}) copy-start(s32[32,32]{1,0:T(8,128)} %param.31) | copy-start | bytes 12292
  5.5 18.6 %copy-start.12 = (f32[128]{0:T(128)S(1)}, f32[128]{0:T(128)}, u32[]{:S(2)}) copy-start(f32[128]{0:T(128)} %param.23) | copy-start | bytes 1540
  7.4 11.8 %copy-start.8 = (s32[4]{0:T(128)S(1)}, s32[4]{0:T(128)}, u32[]{:S(2)}) copy-start(s32[4]{0:T(128)} %get-tuple-element.80) | copy-start | bytes 52 | tf_op jit(solution)/shard_map/cond
  7.4 16.6 %all-to-all-start.2 = ((bf16[8,16,640]{2,1,0:T(8,128)(2,1)}), bf16[8,16,640]{2,1,0:T(8,128)(2,1)S(1)}, u32[]{:S(2)}, u32[]{:S(2)}) async-start(bf16[8,16,640]{2,1,0:T(8,128)(2,1)} %get-tuple-element.79), calls=%async_computation.2 | async-start | bytes 327680 | tf_op jit(solution)/shard_map/cond/branch_0_fun/all_to_all | solution.py:306
  15.7 3.6 %copy-start.10 = (f32[128]{0:T(128)S(1)}, f32[128]{0:T(128)}, u32[]{:S(2)}) copy-start(f32[128]{0:T(128)} %get-tuple-element.83) | copy-start | bytes 1540 | tf_op jit(solution)/shard_map/cond
  15.7 4.3 %copy-start.4 = (bf16[4,128,2,256]{3,2,1,0:T(2,128)(2,1)S(1)}, bf16[4,128,2,256]{3,2,1,0:T(2,128)(2,1)}, u32[]{:S(2)}) copy-start(bf16[4,128,2,256]{3,2,1,0:T(2,128)(2,1)} %get-tuple-element.235) | copy-start | bytes 1572868 | tf_op jit(solution)/shard_map/cond
  24.0 0.7 copy-start
  24.7 18.4 %copy-start.9 = (s32[4]{0:T(128)S(1)}, s32[4]{0:T(128)}, u32[]{:S(2)}) copy-start(s32[4]{0:T(128)} %get-tuple-element.93.length_ref) | copy-start | bytes 52 | tf_op jit(solution)/shard_map/cond
  45.0 15.9 %collective-permute-start.9 = (bf16[704,2048]{1,0:T(8,128)(2,1)}, bf16[704,2048]{1,0:T(8,128)(2,1)S(1)}, u32[]{:S(2)}, u32[]{:S(2)}) collective-permute-start(bf16[704,2048]{1,0:T(8,128)(2,1)} %get-tuple-element.140), channel_id=1, source_target_pairs={{0,128},{1,129},{2,130},{3,131},{4,132},{5,133},{6,134},{7,135},{8... | collective-permute-start | bytes 8650760 | tf_op jit(solution)/shard_map/ppermute | solution.py:365
  61.0 17.1 %copy-start.1 = (bf16[4,4,5120]{2,1,0:T(4,128)(2,1)S(1)}, bf16[4,4,5120]{2,1,0:T(4,128)(2,1)}, u32[]{:S(2)}) copy-start(bf16[4,4,5120]{2,1,0:T(4,128)(2,1)} %get-tuple-element.115.hidden_ref) | copy-start | bytes 491524 | tf_op jit(solution)/shard_map/cond
  72.7 6.5 %collective-permute-start.3 = (bf16[8,16,640]{2,1,0:T(8,128)(2,1)S(1)}, bf16[8,16,640]{2,1,0:T(8,128)(2,1)S(1)}, u32[]{:S(2)}, u32[]{:S(2)}) collective-permute-start(bf16[8,16,640]{2,1,0:T(8,128)(2,1)S(1)} %all_to_all.22), channel_id=1, source_target_pairs={{0,2},{1,3},{2,0},{3,1},{4,6},{5,7},{6,4},{7,5},{8,10},{9,11},{10,... | collective-permute-start | bytes 491528 | tf_op jit(solution)/shard_map/cond/branch_0_fun/ppermute | solution.py:389
  75.4 5.4 %collective-permute-start.4 = (bf16[8,16,640]{2,1,0:T(8,128)(2,1)S(1)}, bf16[8,16,640]{2,1,0:T(8,128)(2,1)S(1)}, u32[]{:S(2)}, u32[]{:S(2)}) collective-permute-start(bf16[8,16,640]{2,1,0:T(8,128)(2,1)S(1)} %all_to_all.22), channel_id=1, source_target_pairs={{0,1},{1,2},{2,3},{3,0},{4,5},{5,6},{6,7},{7,4},{8,9},{9,10},{10,1... | collective-permute-start | bytes 491528 | tf_op jit(solution)/shard_map/cond/branch_0_fun/ppermute | solution.py:389
  75.7 5.1 %collective-permute-start.5 = (bf16[8,16,640]{2,1,0:T(8,128)(2,1)S(1)}, bf16[8,16,640]{2,1,0:T(8,128)(2,1)S(1)}, u32[]{:S(2)}, u32[]{:S(2)}) collective-permute-start(bf16[8,16,640]{2,1,0:T(8,128)(2,1)S(1)} %all_to_all.22), channel_id=1, source_target_pairs={{0,3},{1,0},{2,1},{3,2},{4,7},{5,4},{6,5},{7,6},{8,11},{9,8},{10,9... | collective-permute-start | bytes 491528 | tf_op jit(solution)/shard_map/cond/branch_0_fun/ppermute | solution.py:389

commit v7 on v6

--- a/solution.py
+++ b/solution.py
@@ -68,21 +68,33 @@
         spread_ref[z] = pltpu.roll(block, shift, axis=1).astype(BF16)
 
 
-def query_kernel(
-    rows_ref, own_ref, first_ref, second_ref, third_ref, out_ref, last_ref, total_ref, semaphore
-):
-    copy = pltpu.make_async_copy(third_ref, last_ref, semaphore)
-    copy.start()
-    tile = 512
+TILE = 512
+
+
+def query_kernel(rows_ref, own_ref, first_ref, second_ref, total_ref):
     depth = 3 * own_ref.shape[0]
-    tiles = [slice(start, start + tile) for start in range(0, out_ref.shape[1], tile)]
-    for columns in tiles:
+    for start in range(0, total_ref.shape[1], TILE):
+        columns = slice(start, start + TILE)
         weight = jnp.concatenate(
             [ref[:, columns] for ref in (own_ref, first_ref, second_ref)], axis=0
         )
         total_ref[:, columns] = dot(rows_ref[:, :depth], weight)
-    copy.wait()
-    for columns in tiles:
+
+
+def last_query_kernel(rows_ref, total_ref, third_ref, out_ref, last_ref, semaphores):
+    depth = 3 * last_ref.shape[0]
+    copies = []
+    for i in range(out_ref.shape[1] // TILE):
+        columns = slice(i * TILE, (i + 1) * TILE)
+        copies.append(
+            pltpu.make_async_copy(
+                third_ref.at[:, columns], last_ref.at[:, columns], semaphores.at[i]
+            )
+        )
+        copies[i].start()
+    for i, copy in enumerate(copies):
+        columns = slice(i * TILE, (i + 1) * TILE)
+        copy.wait()
         last = dot(rows_ref[:, depth:], last_ref[:, columns])
         out_ref[:, columns] = (total_ref[:, columns] + last).astype(BF16)
 
@@ -320,19 +332,26 @@
 
     spread, *beside, span_kv, payload = lax.cond(prefill_side, prefill, project)
 
-    def attend(payload, spread, cosine, sine, new_keys, new_values, keys, values, *weights):
+    total = pl.pallas_call(
+        query_kernel,
+        in_specs=[whole] * 4,
+        out_specs=whole,
+        out_shape=jax.ShapeDtypeStruct((Z * rows, local_query), F32),
+        compiler_params=pltpu.CompilerParams(vmem_limit_bytes=VMEM_LIMIT),
+    )(spread, q_weight, *arrived_weights[:2])
+
+    def attend(payload, spread, cosine, sine, new_keys, new_values, keys, values, total, last):
         partial = pl.pallas_call(
-            query_kernel,
-            in_specs=[whole] * 4 + [anywhere],
+            last_query_kernel,
+            in_specs=[whole] * 2 + [anywhere],
             out_specs=whole,
             out_shape=jax.ShapeDtypeStruct((Z * rows, local_query), BF16),
             scratch_shapes=[
                 pltpu.VMEM((depth, local_query), BF16),
-                pltpu.VMEM((Z * rows, local_query), F32),
-                pltpu.SemaphoreType.DMA,
+                pltpu.SemaphoreType.DMA((local_query // TILE,)),
             ],
             compiler_params=pltpu.CompilerParams(vmem_limit_bytes=VMEM_LIMIT),
-        )(spread, q_weight, *weights)
+        )(spread, total, last)
         returned = lax.all_to_all(
             partial.reshape(exchanged), "z", split_axis=0, concat_axis=0, tiled=True
         )
@@ -360,7 +379,7 @@
 
     handed, attended = lax.cond(
         prefill_side, route, attend,
-        payload, spread, *beside, *arrived_weights,
+        payload, spread, *beside, total, arrived_weights[2],
     )
     handed = lax.ppermute(handed, "role", [(0, 1)])
 

time: 82.2 us -> 83.4 us (1.015)
  Pallas kernels: 6.23 us -> 7.09 us
    pallas_call x1 -> x2, Pallas kernels: 1.46 us -> 2.32 us  [the longest x1 1.87 us: attend(): pl.pallas_call(last_query_kernel, in_specs=[whole] * 2 + [anywhere], out_...]
where the time goes in v7:
time: 83.4 us; the launch traced here: 83 us
  blocking collectives  42.7 us (51%)
  starting transfers between devices  19.9 us (24%)
  Pallas kernels  7.09 us (9%)
  waiting for transfers between devices  5.47 us (7%)
  matrix products  4.34 us (5%)
  other arithmetic  1.39 us (2%)
  local copies, waits for them, and re-layouts  0.98 us (1%)
    all_to_all x1, blocking collectives, attend(): lax.all_to_all(partial.reshape(exchanged), 'z', split_axis=0, concat_axis...  16.8 us
    all_to_all x1, blocking collectives, gather(): lax.all_to_all(attended, 'z', split_axis=0, concat_axis=0, tiled=True)  15.3 us
    all_to_all x1, blocking collectives, finish(): lax.all_to_all(partial.reshape(Z, rows, chunk), 'z', split_axis=0, concat...  10.7 us
    all_to_all x1, starting transfers between devices, project(): lax.all_to_all(spread, 'z', split_axis=0, concat_axis=0, tiled=True)  8.32 us
    ppermute x3, starting transfers between devices, finish(): delta = delta + lax.ppermute(back, 'tp', pairs).astype(F32)  5.43 us
    ppermute x3, starting transfers between devices, shards(): arrived_weights[shift - 1] = lax.ppermute(q_weight, ('role', 'y'), pairs)  4.83 us
    all_to_all x1, waiting for transfers between devices, project(): lax.all_to_all(spread, 'z', split_axis=0, concat_axis=0, tiled=True)  3.87 us
    dot_general x1, matrix products, project(): jnp.einsum('rd,dcw->crw', normed, kv_weight, preferred_element_type=F32)  3.33 us
  transfers between devices with their start and end apart: 8, of which 2 were waited for; matrix products, arithmetic and copies ran while one was open for 5% of the time, Pallas kernels for 4%

profile of v7, /device:TPU:1, one launch (start us, length us, event | category | flops | bytes accessed | tf_op | source)
XLA Modules:
  0.0 83.0 jit_solution(13385763354273646842)
XLA Ops:
  0.6 3.3 %collective-permute-start.6 = (bf16[160,2048]{1,0:T(8,128)(2,1)}, bf16[160,2048]{1,0:T(8,128)(2,1)S(1)}, u32[]{:S(2)}, u32[]{:S(2)}) collective-permute-start(bf16[160,2048]{1,0:T(8,128)(2,1)} %own_ref.1), channel_id=1, source_target_pairs={{0,140},{4,128},{8,132},{12,136},{128,0},{132,4},{136,8},{140,12},... | collective-permute-start | bytes 1966088 | tf_op jit(solution)/shard_map/ppermute | solution.py:299
  3.9 0.7 collective-permute-start.7
  4.6 0.9 %collective-permute-start.8 = (bf16[160,2048]{1,0:T(8,128)(2,1)}, bf16[160,2048]{1,0:T(8,128)(2,1)}, u32[]{:S(2)}, u32[]{:S(2)}) collective-permute-start(bf16[160,2048]{1,0:T(8,128)(2,1)} %own_ref.1), channel_id=1, source_target_pairs={{0,132},{4,136},{8,140},{12,128},{128,0},{132,4},{136,8},{140,12},... | collective-permute-start | bytes 1966088 | tf_op jit(solution)/shard_map/ppermute | solution.py:299
  5.5 0.0 copy-start
  5.5 18.5 %conditional.4 = (bf16[128,640]{1,0:T(8,128)(2,1)S(1)}, f32[16,128]{1,0:T(8,128)S(1)}, f32[16,128]{1,0:T(8,128)S(1)}, bf16[16,256]{1,0:T(8,128)(2,1)S(1)}, bf16[...) conditional(s32[]{:T(128)} %convert_element_type.72, ...), branch_computations={%region_0.0_spmd, %region_2.6_spmd} | conditional | flops 1487554176 | bytes 15732424 | solution.py:333
  5.5 1.9 %branch_0_fun.4 = (bf16[8,16,640]{2,1,0:T(8,128)(2,1)}, bf16[16,5120]{1,0:T(8,128)(2,1)S(1)}, bf16[256,2,256]{2,1,0:T(2,128)(2,1)S(1)}, bf16[32,16,512]{2,1,0:T(8,128)(2,1)}) custom-call(s32[1]{0:T(128)} %bitcast.y_ref, bf16[4,4,5120]{2,1,0:T(4,128)(2,1)} %get-tuple-element.73.hidden_ref, f32[1,5120]{1,0:T(1,128)} %bitcast.69), custom_call_target="tpu_custom_call" | custom-call | tf_op jit(solution)/shard_map/cond/branch_0_fun/pallas_call | solution.py:302
  7.4 0.0 copy-start.8
  7.4 8.3 %all-to-all-start.2 = ((bf16[8,16,640]{2,1,0:T(8,128)(2,1)}), bf16[8,16,640]{2,1,0:T(8,128)(2,1)S(1)}, u32[]{:S(2)}, u32[]{:S(2)}) async-start(bf16[8,16,640]{2,1,0:T(8,128)(2,1)} %get-tuple-element.75), calls=%async_computation.2 | async-start | bytes 327680 | tf_op jit(solution)/shard_map/cond/branch_0_fun/all_to_all | solution.py:318
  15.7 0.0 copy-start.9
  15.7 0.0 copy-start.3
  15.7 3.3 %fusion.2 = f32[2,16,256]{2,1,0:T(8,128)S(1)} fusion(bf16[5120,2,256]{2,1,0:T(2,128)(2,1)} %get-tuple-element.227, bf16[16,5120]{1,0:T(8,128)(2,1)S(1)} %get-tuple-element.77), kind=kOutput, calls=%fused_computation.2 | convolution fusion | flops 83886080 | bytes 5439488 | tf_op jit(solution)/shard_map/cond/branch_0_fun/rd,dcw->crw/dot_general | solution.py:323
  19.1 0.1 multiply_reduce_fusion
  19.2 0.0 copy-done.8
  19.2 0.1 convert_element_type.55
  19.3 0.0 copy-done.9
  19.3 0.1 multiply_multiply_fusion
  19.4 0.1 fusion.7
  19.5 0.1 subtract_convert_fusion
  19.6 0.1 pad_maximum_fusion
  19.7 0.1 pad_maximum_fusion.2
  19.8 0.2 copy.39
  20.0 0.0 copy-done.3
  20.0 0.1 copy.42
  20.1 3.9 %all-to-all-done.2 = bf16[8,16,640]{2,1,0:T(8,128)(2,1)S(1)} async-done(((bf16[8,16,640]{2,1,0:T(8,128)(2,1)}), bf16[8,16,640]{2,1,0:T(8,128)(2,1)S(1)}, u32[]{:S(2)}, u32[]{:S(2)}) %all-to-all-start.2) | async-done | bytes 163872 | tf_op jit(solution)/shard_map/cond/branch_0_fun/all_to_all | solution.py:318
  24.0 0.0 copy-start.1
  24.0 0.0 copy-start.4
  24.0 0.0 copy-start.6
  24.0 0.0 copy-start.7
  24.0 0.0 copy-start.11
  24.0 0.0 collective-permute-done.6.first_ref
  24.0 0.0 collective-permute-done.7.second_ref
  24.0 0.0 copy-done
  24.1 0.4 shard_map.138
  24.5 0.0 collective-permute-done.8
  24.5 0.2 copy-done.4
  24.7 0.1 copy-done.6
  24.8 0.0 copy-done.7
  24.8 0.0 copy-done.11
  24.8 0.0 copy-done.1
  24.8 20.6 %conditional.5 = (bf16[704,2048]{1,0:T(8,128)(2,1)}, bf16[8,16,2048]{2,1,0:T(8,128)(2,1)S(1)}) conditional(s32[]{:T(128)} %convert_element_type.72, (bf16[128,640]{1,0:T(8,128)(2,1)S(1)}, f32[128,2048]{1,0:T(8,128)S(1)}, bf16[160,2048]{1,0:T(8,128)(2,1)}, f32[128]{0:T(128)S(1)}, s32[4]{0:T(128)S(1)}, /*index=5*/f32[16,128]{1,0:T(8,128)S(1)}, ...), branch_computations={%region_6.7_spmd, %region_7.10_spmd} | conditional | flops 135761232 | bytes 19967384 | solution.py:380
  24.8 1.9 %branch_0_fun.5 = bf16[128,2048]{1,0:T(8,128)(2,1)S(1)} custom-call(bf16[128,640]{1,0:T(8,128)(2,1)S(1)} %get-tuple-element.90.rows_ref, f32[128,2048]{1,0:T(8,128)S(1)} %get-tuple-element.91.total_ref, bf16[160,2048]{1,0:T(8,128)(2,1)} %get-tuple-element.92.third_ref), custom_call_target="tpu_custom_call" | custom-call | tf_op jit(solution)/shard_map/cond/branch_0_fun/pallas_call | solution.py:344
  26.7 16.8 %all_to_all.20.returned_ref = bf16[8,16,2048]{2,1,0:T(8,128)(2,1)S(1)} all-to-all(bf16[8,16,2048]{2,1,0:T(8,128)(2,1)S(1)} %bitcast.56), channel_id=1, replica_groups=mesh['role'=2,'z'=8,'y'=4,'tp'=4] {'z'}, dimensions={0} | all-to-all | bytes 1048576 | tf_op jit(solution)/shard_map/cond/branch_0_fun/all_to_all | solution.py:355
  43.5 1.7 %branch_0_fun.6 = (bf16[8,16,2048]{2,1,0:T(8,128)(2,1)S(1)}, bf16[704,2048]{1,0:T(8,128)(2,1)}) custom-call(s32[4]{0:T(128)S(1)} %get-tuple-element.89.length_ref, bf16[8,16,2048]{2,1,0:T(8,128)(2,1)S(1)} %all_to_all.20.returned_ref, f32[1,128]{1,0:T(1,128)S(1)} %bitcast.70, f32[16,128]{1,0:T(8,128)S(1)} %get-tuple-element.94.cosine_ref, ...), custom_call_target="tpu_custom_call" | custom-call | tf_op jit(solution)/shard_map/cond/branch_0_fun/pallas_call | solution.py:358
  45.4 1.3 %collective-permute-start.9 = (bf16[704,2048]{1,0:T(8,128)(2,1)}, bf16[704,2048]{1,0:T(8,128)(2,1)S(1)}, u32[]{:S(2)}, u32[]{:S(2)}) collective-permute-start(bf16[704,2048]{1,0:T(8,128)(2,1)} %get-tuple-element.134), channel_id=1, source_target_pairs={{0,128},{1,129},{2,130},{3,131},{4,132},{5,133},{6,134},{7,135},{8... | collective-permute-start | bytes 8650760 | tf_op jit(solution)/shard_map/ppermute | solution.py:384
  46.7 15.3 %conditional.6 = (bf16[8,16,2048]{2,1,0:T(8,128)(2,1)S(1)}) conditional(s32[]{:T(128)} %convert_element_type.72, bf16[8,16,2048]{2,1,0:T(8,128)(2,1)S(1)} %get-tuple-element.135, bf16[8,16,2048]{2,1,0:T(8,128)(2,1)S(1)} %get-tuple-element.135), branch_computations={%region_10.11_spmd, %region_11.12_spmd} | conditional | bytes 2097160 | solution.py:389
  46.8 15.3 %all_to_all.21 = bf16[8,16,2048]{2,1,0:T(8,128)(2,1)S(1)} all-to-all(bf16[8,16,2048]{2,1,0:T(8,128)(2,1)S(1)} %copy.89), channel_id=1, replica_groups=mesh['role'=2,'z'=8,'y'=4,'tp'=4] {'z'}, dimensions={0} | all-to-all | bytes 1048576 | tf_op jit(solution)/shard_map/cond/branch_0_fun/all_to_all | solution.py:387
  62.0 0.0 collective-permute-done.9
  62.0 20.9 %conditional.7 = (bf16[1,256,2,256]{3,2,1,0:T(2,128)(2,1)}, bf16[1,4,4,5120]{3,2,1,0:T(4,128)(2,1)}) conditional(s32[]{:T(128)} %convert_element_type.72, (bf16[704,2048]{1,0:T(8,128)(2,1)S(1)}, bf16[4,4,5120]{2,1,0:T(4,128)(2,1)}, bf16[8,16,2048]{2,1,0:T(8,128)(2,1)S(1)}) %tuple.41, bf16[256,2,256]{0,2,1:T(8,128)(2,1)} %copy-done.1), branch_computations={%region_12.13_spmd, %region_13.14_spmd} | conditional | flops 369836032 | bytes 9978020 | solution.py:432
  62.0 0.0 copy-start.2
  62.0 1.0 %fusion.34 = bf16[128,704]{1,0:T(8,128)(2,1)S(1)} fusion(bf16[128,2048]{1,0:T(8,128)(2,1)S(1)} %bitcast.59, bf16[704,2048]{1,0:T(8,128)(2,1)S(1)} %get-tuple-element.108.handed_ref), kind=kOutput, calls=%fused_computation.81 | convolution fusion | flops 369098752 | bytes 3588096 | tf_op jit(solution)/shard_map/cond/branch_0_fun/dot_general | solution.py:395
  63.1 10.7 %all_to_all.22 = bf16[8,16,640]{2,1,0:T(8,128)(2,1)S(1)} all-to-all(bf16[8,16,640]{2,1,0:T(8,128)(2,1)S(1)} %bitcast.63), channel_id=1, replica_groups=mesh['role'=2,'z'=8,'y'=4,'tp'=4] {'z'}, dimensions={0} | all-to-all | bytes 327680 | tf_op jit(solution)/shard_map/cond/branch_0_fun/all_to_all | solution.py:401
  73.7 2.8 %collective-permute-start.3 = (bf16[8,16,640]{2,1,0:T(8,128)(2,1)S(1)}, bf16[8,16,640]{2,1,0:T(8,128)(2,1)S(1)}, u32[]{:S(2)}, u32[]{:S(2)}) collective-permute-start(bf16[8,16,640]{2,1,0:T(8,128)(2,1)S(1)} %all_to_all.22), channel_id=1, source_target_pairs={{0,2},{1,3},{2,0},{3,1},{4,6},{5,7},{6,4},{7,5},{8,10},{9,11},{10,... | collective-permute-start | bytes 491528 | tf_op jit(solution)/shard_map/cond/branch_0_fun/ppermute | solution.py:408
  76.5 0.3 collective-permute-start.4
  76.8 2.4 %collective-permute-start.5 = (bf16[8,16,640]{2,1,0:T(8,128)(2,1)S(1)}, bf16[8,16,640]{2,1,0:T(8,128)(2,1)S(1)}, u32[]{:S(2)}, u32[]{:S(2)}) collective-permute-start(bf16[8,16,640]{2,1,0:T(8,128)(2,1)S(1)} %all_to_all.22), channel_id=1, source_target_pairs={{0,3},{1,0},{2,1},{3,2},{4,7},{5,4},{6,5},{7,6},{8,11},{9,8},{10,9... | collective-permute-start | bytes 491528 | tf_op jit(solution)/shard_map/cond/branch_0_fun/ppermute | solution.py:408
  79.2 0.0 copy-done.2
  79.2 1.1 %branch_0_fun.7 = (bf16[1,256,2,256]{3,2,1,0:T(2,128)(2,1)}, f32[4,4,5120]{2,1,0:T(4,128)S(1)}) custom-call(bf16[704,2048]{1,0:T(8,128)(2,1)S(1)} %get-tuple-element.108.handed_ref, bf16[4,4,5120]{2,1,0:T(4,128)(2,1)S(1)} %copy-done.2), custom_call_target="tpu_custom_call" | custom-call | tf_op jit(solution)/shard_map/cond/branch_0_fun/pallas_call | solution.py:410
  80.3 0.0 collective-permute-done.3
  80.3 1.6 %collective-permute-done.4 = bf16[8,16,640]{2,1,0:T(8,128)(2,1)S(1)} collective-permute-done((bf16[8,16,640]{2,1,0:T(8,128)(2,1)S(1)}, bf16[8,16,640]{2,1,0:T(8,128)(2,1)S(1)}, u32[]{:S(2)}, u32[]{:S(2)}) %collective-permute-start.4) | collective-permute-done | bytes 163872 | tf_op jit(solution)/shard_map/cond/branch_0_fun/ppermute | solution.py:408
  81.9 0.0 collective-permute-done.5
  81.9 0.1 add_bitcast_fusion
  82.0 0.1 copy.40
  82.1 0.1 reshape.307
  82.2 0.8 fusion.31
  (10 shorter events, 0.1 us)
Async XLA Ops:
  0.6 23.4 %collective-permute-start.6 = (bf16[160,2048]{1,0:T(8,128)(2,1)}, bf16[160,2048]{1,0:T(8,128)(2,1)S(1)}, u32[]{:S(2)}, u32[]{:S(2)}) collective-permute-start(bf16[160,2048]{1,0:T(8,128)(2,1)} %own_ref.1), channel_id=1, source_target_pairs={{0,140},{4,128},{8,132},{12,136},{128,0},{132,4},{136,8},{140,12},... | collective-permute-start | bytes 1966088 | tf_op jit(solution)/shard_map/ppermute | solution.py:299
  3.9 20.2 %collective-permute-start.7 = (bf16[160,2048]{1,0:T(8,128)(2,1)}, bf16[160,2048]{1,0:T(8,128)(2,1)S(1)}, u32[]{:S(2)}, u32[]{:S(2)}) collective-permute-start(bf16[160,2048]{1,0:T(8,128)(2,1)} %own_ref.1), channel_id=1, source_target_pairs={{0,136},{4,140},{8,128},{12,132},{128,0},{132,4},{136,8},{140,12},... | collective-permute-start | bytes 1966088 | tf_op jit(solution)/shard_map/ppermute | solution.py:299
  4.6 19.9 %collective-permute-start.8 = (bf16[160,2048]{1,0:T(8,128)(2,1)}, bf16[160,2048]{1,0:T(8,128)(2,1)}, u32[]{:S(2)}, u32[]{:S(2)}) collective-permute-start(bf16[160,2048]{1,0:T(8,128)(2,1)} %own_ref.1), channel_id=1, source_target_pairs={{0,132},{4,136},{8,140},{12,128},{128,0},{132,4},{136,8},{140,12},... | collective-permute-start | bytes 1966088 | tf_op jit(solution)/shard_map/ppermute | solution.py:299
  5.5 18.6 %copy-start = (bf16[160,2048]{1,0:T(8,128)(2,1)S(1)}, bf16[160,2048]{1,0:T(8,128)(2,1)}, u32[]{:S(2)}) copy-start(bf16[160,2048]{1,0:T(8,128)(2,1)} %own_ref.1) | copy-start | bytes 1966084
  7.4 11.8 %copy-start.8 = (s32[4]{0:T(128)S(1)}, s32[4]{0:T(128)}, u32[]{:S(2)}) copy-start(s32[4]{0:T(128)} %get-tuple-element.76) | copy-start | bytes 52 | tf_op jit(solution)/shard_map/cond
  7.4 16.6 %all-to-all-start.2 = ((bf16[8,16,640]{2,1,0:T(8,128)(2,1)}), bf16[8,16,640]{2,1,0:T(8,128)(2,1)S(1)}, u32[]{:S(2)}, u32[]{:S(2)}) async-start(bf16[8,16,640]{2,1,0:T(8,128)(2,1)} %get-tuple-element.75), calls=%async_computation.2 | async-start | bytes 327680 | tf_op jit(solution)/shard_map/cond/branch_0_fun/all_to_all | solution.py:318
  15.7 3.6 %copy-start.9 = (f32[128]{0:T(128)S(1)}, f32[128]{0:T(128)}, u32[]{:S(2)}) copy-start(f32[128]{0:T(128)} %get-tuple-element.79) | copy-start | bytes 1540 | tf_op jit(solution)/shard_map/cond
  15.7 4.3 %copy-start.3 = (bf16[4,128,2,256]{3,2,1,0:T(2,128)(2,1)S(1)}, bf16[4,128,2,256]{3,2,1,0:T(2,128)(2,1)}, u32[]{:S(2)}) copy-start(bf16[4,128,2,256]{3,2,1,0:T(2,128)(2,1)} %get-tuple-element.229) | copy-start | bytes 1572868 | tf_op jit(solution)/shard_map/cond
  24.0 0.8 copy-start.1
  24.0 0.7 copy-start.4
  24.0 0.8 copy-start.6
  24.0 0.8 copy-start.7
  24.0 0.8 copy-start.11
  45.4 16.6 %collective-permute-start.9 = (bf16[704,2048]{1,0:T(8,128)(2,1)}, bf16[704,2048]{1,0:T(8,128)(2,1)S(1)}, u32[]{:S(2)}, u32[]{:S(2)}) collective-permute-start(bf16[704,2048]{1,0:T(8,128)(2,1)} %get-tuple-element.134), channel_id=1, source_target_pairs={{0,128},{1,129},{2,130},{3,131},{4,132},{5,133},{6,134},{7,135},{8... | collective-permute-start | bytes 8650760 | tf_op jit(solution)/shard_map/ppermute | solution.py:384
  62.0 17.1 %copy-start.2 = (bf16[4,4,5120]{2,1,0:T(4,128)(2,1)S(1)}, bf16[4,4,5120]{2,1,0:T(4,128)(2,1)}, u32[]{:S(2)}) copy-start(bf16[4,4,5120]{2,1,0:T(4,128)(2,1)} %get-tuple-element.109.hidden_ref) | copy-start | bytes 491524 | tf_op jit(solution)/shard_map/cond
  73.7 6.6 %collective-permute-start.3 = (bf16[8,16,640]{2,1,0:T(8,128)(2,1)S(1)}, bf16[8,16,640]{2,1,0:T(8,128)(2,1)S(1)}, u32[]{:S(2)}, u32[]{:S(2)}) collective-permute-start(bf16[8,16,640]{2,1,0:T(8,128)(2,1)S(1)} %all_to_all.22), channel_id=1, source_target_pairs={{0,2},{1,3},{2,0},{3,1},{4,6},{5,7},{6,4},{7,5},{8,10},{9,11},{10,... | collective-permute-start | bytes 491528 | tf_op jit(solution)/shard_map/cond/branch_0_fun/ppermute | solution.py:408
  76.5 5.4 %collective-permute-start.4 = (bf16[8,16,640]{2,1,0:T(8,128)(2,1)S(1)}, bf16[8,16,640]{2,1,0:T(8,128)(2,1)S(1)}, u32[]{:S(2)}, u32[]{:S(2)}) collective-permute-start(bf16[8,16,640]{2,1,0:T(8,128)(2,1)S(1)} %all_to_all.22), channel_id=1, source_target_pairs={{0,1},{1,2},{2,3},{3,0},{4,5},{5,6},{6,7},{7,4},{8,9},{9,10},{10,1... | collective-permute-start | bytes 491528 | tf_op jit(solution)/shard_map/cond/branch_0_fun/ppermute | solution.py:408
  76.8 5.1 %collective-permute-start.5 = (bf16[8,16,640]{2,1,0:T(8,128)(2,1)S(1)}, bf16[8,16,640]{2,1,0:T(8,128)(2,1)S(1)}, u32[]{:S(2)}, u32[]{:S(2)}) collective-permute-start(bf16[8,16,640]{2,1,0:T(8,128)(2,1)S(1)} %all_to_all.22), channel_id=1, source_target_pairs={{0,3},{1,0},{2,1},{3,2},{4,7},{5,4},{6,5},{7,6},{8,11},{9,8},{10,9... | collective-permute-start | bytes 491528 | tf_op jit(solution)/shard_map/cond/branch_0_fun/ppermute | solution.py:408
